TPU v7x, 32 devices: a whole 2x2x4 slice. The times are simulated.
32 devices in a mesh: expert: 8 (over z, core), context: 2 (over x), dp: 2 (over y).
Axes of the slice: x: 2, y: 2, z: 4, core: 2. Of those that a mesh axis runs over, the one named last changes fastest.
Arguments:
- tokens_in: bfloat16 [8, 512, 2048], P('expert', ('context', 'dp')), may hold values from -6 to 6
- doc_ids: int32 [8, 512], P('expert'), may hold values from 0 to 2, as said below
- routes: int32 [8, 512, 6], P('expert', ('context', 'dp')), may hold values from 0 to 15, all different within a row; in each aligned block of 128 rows (0 to 127, 128 to 255, ..., all dimensions but the last counted through in order) at most 64 rows name the same one
- gain_attn: bfloat16 [2048], P(('expert', 'context', 'dp')), may hold values from 0.5 to 1.5
- w_query: bfloat16 [2048, 2048], P(('expert', 'context', 'dp')), may hold values from -0.125 to 0.125
- w_key: bfloat16 [2048, 2048], P(('expert', 'context', 'dp')), may hold values from -0.125 to 0.125
- w_value: bfloat16 [2048, 2048], P(('expert', 'context', 'dp')), may hold values from -0.125 to 0.125
- w_out: bfloat16 [2048, 2048], P(('expert', 'context', 'dp')), may hold values from -0.5 to 0.5
- gain_moe: bfloat16 [2048], P(('expert', 'context', 'dp')), may hold values from 0.5 to 1.5
- w_router: bfloat16 [2048, 16], P(('expert', 'context', 'dp')), may hold values from -0.0625 to 0.0625
- shared_gate: bfloat16 [2048, 2816], P(('expert', 'context', 'dp')), may hold values from -0.125 to 0.125
- shared_up: bfloat16 [2048, 2816], P(('expert', 'context', 'dp')), may hold values from -0.125 to 0.125
- shared_down: bfloat16 [2816, 2048], P(('expert', 'context', 'dp')), may hold values from -0.109375 to 0.109375
- expert_gate: bfloat16 [16, 2048, 1408], P('expert', ('context', 'dp')), may hold values from -0.125 to 0.125
- expert_up: bfloat16 [16, 2048, 1408], P('expert', ('context', 'dp')), may hold values from -0.125 to 0.125
- expert_down: bfloat16 [16, 1408, 2048], P('expert', ('context', 'dp')), may hold values from -0.875 to 0.875
- cotangent: bfloat16 [8, 512, 2048], P('expert', ('context', 'dp')), may hold values from -6 to 6
Outputs:
- layer_out: float32 [8, 512, 2048], P('expert', ('context', 'dp'))
- grad_tokens: float32 [8, 512, 2048], P('expert', ('context', 'dp'))
- grad_gain_attn: float32 [2048], P(('expert', 'context', 'dp'))
- grad_query: float32 [2048, 2048], P(('expert', 'context', 'dp'))
- grad_key: float32 [2048, 2048], P(('expert', 'context', 'dp'))
- grad_value: float32 [2048, 2048], P(('expert', 'context', 'dp'))
- grad_out: float32 [2048, 2048], P(('expert', 'context', 'dp'))
- grad_gain_moe: float32 [2048], P(('expert', 'context', 'dp'))
- grad_router: float32 [2048, 16], P(('expert', 'context', 'dp'))
- grad_shared_gate: float32 [2048, 2816], P(('expert', 'context', 'dp'))
- grad_shared_up: float32 [2048, 2816], P(('expert', 'context', 'dp'))
- grad_shared_down: float32 [2816, 2048], P(('expert', 'context', 'dp'))
- grad_expert_gate: float32 [16, 2048, 1408], P('expert', ('context', 'dp'))
- grad_expert_up: float32 [16, 2048, 1408], P('expert', ('context', 'dp'))
- grad_expert_down: float32 [16, 1408, 2048], P('expert', ('context', 'dp'))
Inputs may be any that keep to these rules, and one draw needn't show every extreme that they name: `doc_ids`: Non-decreasing along each sequence, starting at 0 and rising by at most one from one position to the next. `routes`: A token names 6 different experts. Among the 128 tokens of one device no expert is named more than 64 times, a bound that some block reaches.
All inputs are finite; a program needn't handle non-finite values.
Results may differ from a plain program's by a relative error of at most 0.018.
Values may be sent and summed in bfloat16 or wider, within the bound.
No kernel may reach another device: no remote copies, remote signals or barrier semaphores. Data moves between devices by JAX's collectives and lax.ppermute only.
A program may use at most 448 MiB of HBM per device.

v0:
```python
import math

import jax
import jax.numpy as jnp
from jax import lax
from jax.sharding import Mesh
from jax.sharding import PartitionSpec as P

HD = 128
TOP = 6
EPS = 1e-06
MASKED = -1e30
Z, K, C, D = "z", "core", "context", "dp"
F32 = jnp.float32
LOW = jnp.bfloat16


class Line:
    def __init__(self, mesh, *names):
        self.names = names
        self.size = math.prod(mesh.shape[name] for name in names)

    def at(self):
        return lax.axis_index(self.names)

    def swap(self, value, delta):
        return lax.ppermute(value, self.names, [(i, i ^ delta) for i in range(self.size)])

    def share(self, value):
        return [value] + [self.swap(value, delta) for delta in range(1, self.size)]

    def give(self, pieces):
        return [pieces[0]] + [self.swap(pieces[delta], delta) for delta in range(1, self.size)]

    def give_from(self, stack, dim=0):
        here = self.at()
        return self.give([pick(stack, here ^ delta, dim) for delta in range(self.size)])


def pick(stack, index, dim=0):
    return lax.dynamic_index_in_dim(stack, index, dim, keepdims=False)


def settle(pieces, index, dim=0):
    shape = list(pieces[0].shape)
    shape.insert(dim, len(pieces))
    out = jnp.zeros(shape, pieces[0].dtype)
    for delta, piece in enumerate(pieces):
        out = lax.dynamic_update_index_in_dim(out, piece, index ^ delta, dim)
    return out


def dot(left, right):
    return jnp.dot(left, right, preferred_element_type=F32)


def total(pieces):
    out = pieces[0].astype(F32)
    for piece in pieces[1:]:
        out = out + piece.astype(F32)
    return out


def turn(values, cosine, sine, sign):
    half = HD // 2
    first, second = values[..., :half], values[..., half:]
    return jnp.concatenate(
        [first * cosine - sign * second * sine, second * cosine + sign * first * sine], axis=-1
    )


def norm_back(grad_normed, normed, scale, gain):
    scaled = grad_normed * gain
    return scale * (scaled - normed * jnp.mean(scaled * normed, axis=1, keepdims=True))


def swish_slope(values, sigma):
    return sigma * (1.0 + values * (1.0 - sigma))


def make_body(mesh):
    line_z, line_k, line_t = Line(mesh, Z), Line(mesh, K), Line(mesh, C, D)
    line_e = Line(mesh, Z, K)
    columns, cores, blocks, owners = line_z.size, line_k.size, line_t.size, line_e.size

    def body(
        tokens_in,
        doc_ids,
        routes,
        gain_attn,
        w_query,
        w_key,
        w_value,
        w_out,
        gain_moe,
        w_router,
        shared_gate,
        shared_up,
        shared_down,
        expert_gate,
        expert_up,
        expert_down,
        cotangent,
    ):
        col, core, blk = line_z.at(), line_k.at(), line_t.at()
        x_low, dy_low = tokens_in[0], cotangent[0]
        rows, width = x_low.shape
        length = doc_ids.shape[1]
        part = w_query.shape[0]
        span = width // blocks
        heads = span // HD
        experts = w_router.shape[1]
        group = experts // columns
        line_s = line_t if blocks == group else Line(mesh, C)
        rest = () if blocks == group else (D,)
        spot = line_s.at()

        small = jnp.concatenate([w_router.T, gain_attn[None], gain_moe[None]], axis=0)
        small = settle(line_t.share(small), blk)
        small = settle(line_e.share(small), line_e.at())
        small = small.transpose(2, 0, 1, 3).reshape(experts + 2, width)
        router_t = small[:experts]
        gain_first = small[experts].astype(F32)[None]
        gain_second = small[experts + 1].astype(F32)[None]

        mixed_in = jnp.concatenate(
            [w.reshape(part, blocks, span) for w in (w_query, w_key, w_value)], axis=2
        ).transpose(1, 0, 2)
        qkv = settle(line_t.give_from(mixed_in), blk).reshape(blocks * part, 3 * span)
        qkv = lax.all_gather(qkv, (Z, K), axis=0, tiled=True)
        move = [(i, (i % owners) * blocks + i // owners) for i in range(owners * blocks)]
        out_mat = lax.ppermute(w_out, (Z, K, C, D), move)
        out_mat = lax.all_gather(out_mat, (Z, K), axis=0, tiled=True)

        x_all = jnp.concatenate(line_t.share(x_low), axis=0).astype(F32)
        inputs = x_low.astype(F32)

        def fetch(weight):
            local, count, wide = weight.shape
            halves = weight.reshape(local, cores, count // cores, wide)
            other = line_k.swap(pick(halves, 1 - core, 1), 1)
            both = settle([pick(halves, core, 1), other], core)
            got = line_s.give_from(both.reshape(group, count // cores, wide))
            pieces = []
            for piece in got:
                pieces += [piece, line_k.swap(piece, 1)]
            whole = settle(pieces, spot * cores + core).reshape(line_s.size, count, wide)
            if rest:
                whole = lax.all_gather(whole, rest, axis=1, tiled=True)
            return whole.reshape(-1, wide)

        def fetch_shared(piece, dim):
            got = line_t.share(piece)
            pieces = got + [line_k.swap(one, 1) for one in got]
            return settle(pieces, core * blocks + blk, dim)

        hidden = shared_gate.shape[1] // columns
        both_in = jnp.concatenate(
            [w.reshape(part, columns, hidden) for w in (shared_gate, shared_up)], axis=2
        ).transpose(1, 0, 2)
        both_in = settle(line_z.give_from(both_in), col)

        dy_col = lax.all_gather(dy_low, Z, axis=0, tiled=True)
        routes_col = settle(line_z.share(routes[0]), col)

        mat_down = fetch(expert_down)
        mat_sdown = fetch_shared(shared_down, 0).reshape(hidden, width)
        mat_gate = fetch(expert_gate)
        mat_up = fetch(expert_up)
        mat_sin = fetch_shared(both_in, 1).reshape(width, 2 * hidden)

        doc_row = doc_ids[0]
        order = blk ^ jnp.arange(blocks, dtype=jnp.int32)
        doc_starts = jnp.sum((doc_row[None, :] < doc_row[:, None]).astype(jnp.int32), axis=1)
        offsets = jnp.arange(length, dtype=jnp.int32) - doc_starts

        def reorder(row):
            grid = row.reshape(blocks, rows)
            return jnp.concatenate([pick(grid, order[i]) for i in range(blocks)])

        doc_here, off_here = reorder(doc_row), reorder(offsets)
        place = reorder(jnp.arange(length, dtype=jnp.int32))
        frequency = jnp.exp(
            jnp.arange(HD // 2, dtype=F32) * (-math.log(10000.0) / (HD // 2))
        )
        angles = off_here.astype(F32)[:, None] * frequency[None, :]
        cosine, sine = jnp.cos(angles)[:, None, :], jnp.sin(angles)[:, None, :]
        allowed = (place[:, None] >= place[None, :]) & (doc_here[:, None] == doc_here[None, :])

        first_scale = lax.rsqrt(jnp.mean(x_all * x_all, axis=1, keepdims=True) + EPS)
        first_normed = x_all * first_scale
        normed_low = (first_normed * gain_first).astype(LOW)
        made = dot(normed_low, qkv)

        def per_head(values):
            return values.reshape(length, heads, HD)

        query_low = turn(per_head(made[:, :span]), cosine, sine, 1.0).astype(LOW)
        key_low = turn(per_head(made[:, span : 2 * span]), cosine, sine, 1.0).astype(LOW)
        value_low = per_head(made[:, 2 * span :].astype(LOW))
        score_scale = HD ** (-0.5)
        scores = jnp.einsum("qhd,khd->hqk", query_low, key_low, preferred_element_type=F32)
        scores = jnp.where(allowed[None], scores * score_scale, MASKED)
        exponent = jnp.exp(scores - jnp.max(scores, axis=2, keepdims=True))
        attn_probs = exponent / jnp.sum(exponent, axis=2, keepdims=True)
        probs_low = attn_probs.astype(LOW)
        mixed_low = (
            jnp.einsum("hqk,khd->qhd", probs_low, value_low, preferred_element_type=F32)
            .astype(LOW)
            .reshape(length, span)
        )
        attn_out = dot(mixed_low, out_mat).astype(LOW).reshape(blocks, rows, width)
        after_attn = inputs + total(line_t.give([attn_out[i] for i in range(blocks)]))

        second_scale = lax.rsqrt(jnp.mean(after_attn * after_attn, axis=1, keepdims=True) + EPS)
        second_normed = after_attn * second_scale
        second_low = (second_normed * gain_second).astype(LOW)
        second_col = lax.all_gather(second_low, Z, axis=0, tiled=True)

        def router(values):
            return jax.nn.softmax(dot(values, router_t.T), axis=1)

        router_probs = router(second_low)
        probs_col = router(second_col)

        capacity = min(rows, rows * TOP * 4 // (3 * experts))
        slots = columns * capacity
        wanted = col * group + (spot ^ jnp.arange(group, dtype=jnp.int32))
        hits = jnp.any(routes_col[None] == wanted[:, None, None, None], axis=3)
        ranks = jnp.cumsum(hits.astype(jnp.int32), axis=2) - 1
        ranks = jnp.where(hits, ranks, -1)
        chosen = ranks[:, :, None, :] == jnp.arange(capacity, dtype=jnp.int32)[:, None]
        same = jnp.eye(columns, dtype=jnp.bool_)[None, :, None, :, None]
        spread = (
            (chosen[:, :, :, None, :] & same).reshape(group * slots, columns * rows).astype(LOW)
        )

        def dispatch(values):
            sent = dot(spread, values).astype(LOW).reshape(group, slots, width)
            return jnp.concatenate(line_s.give([sent[i] for i in range(group)]), axis=0)

        def collect(values):
            parts = values.reshape(group, slots, width)
            back = line_s.give([parts[i] for i in range(group)])
            return dot(spread.T, jnp.concatenate(back, axis=0))

        dy_slots = dispatch(dy_col)
        du_raw = dot(dy_slots, mat_down.T)
        gate_col = jnp.sum(
            jnp.where(
                jnp.arange(experts, dtype=jnp.int32) == wanted[:, None, None], probs_col[None], 0.0
            ),
            axis=2,
        ).reshape(group, columns, 1, rows)
        gate_sent = jnp.sum(jnp.where(chosen, gate_col, 0.0), axis=3).reshape(group, 1, slots)
        gate = jnp.concatenate(line_s.give([gate_sent[i] for i in range(group)]), axis=1)
        gate = gate.reshape(group * slots, 1)

        second_slots = dispatch(second_col)
        pre_gate = dot(second_slots, mat_gate)
        pre_up = dot(second_slots, mat_up)
        sigma = jax.nn.sigmoid(pre_gate)
        hidden_low = (pre_gate * sigma * pre_up).astype(LOW)
        dgate = jnp.sum(hidden_low.astype(F32) * du_raw, axis=1)
        du = du_raw * gate
        grad_a = (du * pre_up * swish_slope(pre_gate, sigma)).astype(LOW)
        grad_b = (du * pre_gate * sigma).astype(LOW)
        grad_slots = (dot(grad_a, mat_gate.T) + dot(grad_b, mat_up.T)).astype(LOW)

        shared_pre = dot(second_col, mat_sin)
        shared_a, shared_b = shared_pre[:, :hidden], shared_pre[:, hidden:]
        shared_sigma = jax.nn.sigmoid(shared_a)
        shared_low = (shared_a * shared_sigma * shared_b).astype(LOW)
        dsu = dot(dy_col, mat_sdown.T)
        dsa = (dsu * shared_b * swish_slope(shared_a, shared_sigma)).astype(LOW)
        dsb = (dsu * shared_a * shared_sigma).astype(LOW)
        dsab = jnp.concatenate([dsa, dsb], axis=1)

        grad_second = (dot(dsab, mat_sin.T) + collect(grad_slots)).astype(LOW)
        grad_second = lax.psum_scatter(grad_second, Z, scatter_dimension=0, tiled=True)

        dgate_parts = dgate.reshape(group, 1, slots)
        dgate_back = line_s.give([dgate_parts[i] for i in range(group)])
        dgate_back = jnp.stack(dgate_back).reshape(group, columns, capacity, 1)
        dgate_col = jnp.sum(jnp.where(chosen, dgate_back, 0.0), axis=2)
        dgate_col = settle([dgate_col[i] for i in range(group)], spot)
        dprobs = settle(line_z.give_from(dgate_col.transpose(1, 0, 2)), col)
        dprobs = dprobs.reshape(experts, rows).T
        dlogits = (
            router_probs * (dprobs - jnp.sum(dprobs * router_probs, axis=1, keepdims=True))
        ).astype(LOW)
        grad_router_t = dot(dlogits.T, second_low)
        grad_second = grad_second.astype(F32) + dot(dlogits, router_t)

        grad_gain_second = jnp.sum(grad_second * second_normed, axis=0, keepdims=True)
        dy = dy_low.astype(F32)
        grad_after = dy + norm_back(grad_second, second_normed, second_scale, gain_second)
        grad_after_low = jnp.concatenate(line_t.share(grad_after.astype(LOW)), axis=0)

        grad_mixed = per_head(dot(grad_after_low, out_mat.T).astype(LOW))
        grad_outmat = dot(mixed_low.T, grad_after_low).astype(LOW)
        grad_probs = jnp.einsum("qhd,khd->hqk", grad_mixed, value_low, preferred_element_type=F32)
        grad_value = jnp.einsum("hqk,qhd->khd", probs_low, grad_mixed, preferred_element_type=F32)
        grad_scores = (
            attn_probs * (grad_probs - jnp.sum(grad_probs * attn_probs, axis=2, keepdims=True))
        ).astype(LOW)
        grad_query = jnp.einsum("hqk,khd->qhd", grad_scores, key_low, preferred_element_type=F32)
        grad_key = jnp.einsum("hqk,qhd->khd", grad_scores, query_low, preferred_element_type=F32)
        grad_query = turn(grad_query * score_scale, cosine, sine, -1.0)
        grad_key = turn(grad_key * score_scale, cosine, sine, -1.0)
        grad_made = jnp.concatenate(
            [g.astype(LOW).reshape(length, span) for g in (grad_query, grad_key, grad_value)], axis=1
        )
        grad_qkv = dot(normed_low.T, grad_made).astype(LOW)
        grad_first = dot(grad_made, qkv.T).astype(LOW).reshape(blocks, rows, width)
        grad_first = total(line_t.give([grad_first[i] for i in range(blocks)]))
        local_normed = first_normed[:rows]
        grad_gain_first = jnp.sum(grad_first * local_normed, axis=0, keepdims=True)
        grad_inputs = grad_after + norm_back(
            grad_first, local_normed, first_scale[:rows], gain_first
        )

        routed = (dot(hidden_low, mat_down) * gate).astype(LOW)
        layer_out = (dot(shared_low, mat_sdown) + collect(routed)).astype(LOW)
        layer_out = lax.psum_scatter(layer_out, Z, scatter_dimension=0, tiled=True)
        layer_out = after_attn + layer_out.astype(F32)

        def deliver(grad, local, count):
            wide = grad.shape[1]
            grad = grad.astype(LOW).reshape(line_s.size, -1, wide)
            if rest:
                grad = lax.psum_scatter(grad, rest, scatter_dimension=1, tiled=True)
            grad = grad.reshape(line_s.size, cores, count // cores, wide)
            mine = total([pick(grad, core, 1), line_k.swap(pick(grad, 1 - core, 1), 1)])
            got = settle(line_s.give_from(mine.astype(LOW)), spot)
            got = got.reshape(cores, local, count // cores, wide)
            other = line_k.swap(pick(got, 1 - core), 1)
            return settle([pick(got, core), other], core, 1).reshape(local, count, wide).astype(F32)

        weighted = (hidden_low.astype(F32) * gate).astype(LOW)
        grad_edown = deliver(dot(weighted.T, dy_slots), *expert_down.shape[:2])
        grad_egate = deliver(dot(second_slots.T, grad_a), *expert_gate.shape[:2])
        grad_eup = deliver(dot(second_slots.T, grad_b), *expert_up.shape[:2])

        def deliver_shared(grad):
            lead, _, count, wide = grad.shape
            grad = grad.reshape(lead, cores, blocks, count, wide)
            mine = total([pick(grad, core, 1), line_k.swap(pick(grad, 1 - core, 1), 1)])
            return total(line_t.give_from(mine.astype(LOW), 1))

        grad_sdown = dot(shared_low.T, dy_col).astype(LOW)
        grad_sdown = deliver_shared(grad_sdown.reshape(1, cores * blocks, -1, width))[0]
        grad_sin = dot(second_col.T, dsab).astype(LOW)
        grad_sin = deliver_shared(grad_sin.reshape(columns, cores * blocks, part, 2 * hidden))
        grad_sin = settle(line_z.give_from(grad_sin.astype(LOW)), col).transpose(1, 0, 2)
        grad_sgate = grad_sin[:, :, :hidden].reshape(part, -1).astype(F32)
        grad_sup = grad_sin[:, :, hidden:].reshape(part, -1).astype(F32)

        grad_outmat = lax.psum_scatter(grad_outmat, (Z, K), scatter_dimension=0, tiled=True)
        back = [(there, here) for here, there in move]
        grad_outmat = lax.ppermute(grad_outmat, (Z, K, C, D), back).astype(F32)
        grad_qkv = lax.psum_scatter(grad_qkv, (Z, K), scatter_dimension=0, tiled=True)
        grad_qkv = settle(line_t.give_from(grad_qkv.reshape(blocks, part, 3 * span)), blk)
        grad_qkv = grad_qkv.reshape(blocks, part, 3, span).transpose(2, 1, 0, 3)
        grad_qkv = grad_qkv.reshape(3, part, width).astype(F32)

        sums = jnp.concatenate([grad_router_t, grad_gain_first, grad_gain_second], axis=0)
        sums = sums.reshape(experts + 2, owners, blocks, part).transpose(2, 1, 0, 3)
        sums = total(line_t.give_from(sums))
        sums = total(line_e.give_from(sums))

        return (
            layer_out[None],
            grad_inputs[None],
            sums[experts],
            grad_qkv[0],
            grad_qkv[1],
            grad_qkv[2],
            grad_outmat,
            sums[experts + 1],
            sums[:experts].T,
            grad_sgate,
            grad_sup,
            grad_sdown,
            grad_egate,
            grad_eup,
            grad_edown,
        )

    return body


def solution(mesh):
    owners, blocks, halves = mesh.devices.shape
    mesh = Mesh(mesh.devices.reshape(owners // 2, 2, blocks, halves), (Z, K, C, D))
    every = P((Z, K, C, D))
    tokens = P((Z, K), (C, D))
    return jax.shard_map(
        make_body(mesh),
        mesh=mesh,
        in_specs=(tokens, P((Z, K)), tokens) + (every,) * 10 + (tokens,) * 4,
        out_specs=(tokens, tokens) + (every,) * 10 + (tokens,) * 3,
        check_vma=False,
    )
```

profile of v0, /device:TPU:0, one launch (start us, length us, event | category | flops | bytes accessed | tf_op | source)
XLA Modules:
  0.0 1089.6 jit_solution(10017302401200164382)
XLA Ops:
  27.2 3.7 collective-permute-start.16
  31.0 15.0 %collective-permute-start.2 = (bf16[128,2048]{1,0:T(8,128)(2,1)S(1)}, bf16[128,2048]{1,0:T(8,128)(2,1)}, u32[]{:S(2)}, u32[]{:S(2)}) collective-permute-start(bf16[128,2048]{1,0:T(8,128)(2,1)S(1)} %bitcast.613), channel_id=1, source_target_pairs={{0,3},{1,2},{2,1},{3,0},{4,7},{5,6},{6,5},{7,4},{8,11},{9,10},{10,... | collective-permute-start | bytes 1572872 | tf_op jit(solution)/shard_map/ppermute | solution.py:27
  46.0 6.0 collective-permute-start.1
  84.4 6.1 fusion.67
  102.6 6.2 collective-permute-start.38
  136.9 5.1 collective-permute-done.8
  153.0 6.2 collective-permute-start.11
  171.2 5.8 collective-permute-done.20
  180.7 7.1 collective-permute-done.21
  190.0 6.2 collective-permute-done.22
  203.2 4.6 collective-permute-done.31
  208.6 5.2 collective-permute-done.32
  227.8 6.9 collective-permute-done.23
  236.1 9.3 collective-permute-done.24
  245.6 14.9 %collective-permute-done.25 = bf16[4,64,1408]{2,1,0:T(8,128)(2,1)S(1)} collective-permute-done((bf16[4,64,1408]{2,1,0:T(8,128)(2,1)}, bf16[4,64,1408]{2,1,0:T(8,128)(2,1)S(1)}, u32[]{:S(2)}, u32[]{:S(2)}) %collective-permute-start.25) | collective-permute-done | bytes 720928 | tf_op jit(solution)/shard_map/ppermute | solution.py:27
  287.6 28.7 %collective-permute-done.45 = bf16[256,1408]{1,0:T(8,128)(2,1)S(1)} collective-permute-done((bf16[256,1408]{1,0:T(8,128)(2,1)S(1)}, bf16[256,1408]{1,0:T(8,128)(2,1)S(1)}, u32[]{:S(2)}, u32[]{:S(2)}) %collective-permute-start.45) | collective-permute-done | bytes 720928 | tf_op jit(solution)/shard_map/ppermute | solution.py:27
  319.4 14.6 %collective-permute-done.61 = bf16[176,2048]{1,0:T(8,128)(2,1)S(1)} collective-permute-done((bf16[176,2048]{1,0:T(8,128)(2,1)S(1)}, bf16[176,2048]{1,0:T(8,128)(2,1)S(1)}, u32[]{:S(2)}, u32[]{:S(2)}) %collective-permute-start.61) | collective-permute-done | bytes 720928 | tf_op jit(solution)/shard_map/ppermute | solution.py:27
  344.5 25.2 %collective-permute-done.63 = bf16[176,2048]{1,0:T(8,128)(2,1)} collective-permute-done((bf16[176,2048]{1,0:T(8,128)(2,1)S(1)}, bf16[176,2048]{1,0:T(8,128)(2,1)}, u32[]{:S(2)}, u32[]{:S(2)}) %collective-permute-start.63) | collective-permute-done | bytes 720928 | tf_op jit(solution)/shard_map/ppermute | solution.py:27
  375.8 6.9 fusion.50
  388.9 4.0 fusion.122
  407.4 7.7 collective-permute-done.19
  415.1 9.5 collective-permute-done.18
  432.7 4.1 convolution_convert_fusion.5
  442.5 29.9 %all-gather.10.cloned.1.call-done = bf16[512,2048]{1,0:T(8,128)(2,1)} async-done(((bf16[128,2048]{1,0:T(8,128)(2,1)}), bf16[512,2048]{1,0:T(8,128)(2,1)}) %all-gather.10.cloned.1.call-update) | async-done | bytes 2097168 | tf_op jit(solution)/shard_map/all_gather | solution.py:218
  472.3 3.9 convolution_convert_fusion.6
  482.7 6.4 fusion.125
  489.1 5.1 fusion.40
  494.2 5.5 convolution_convert_fusion.3
  499.8 4.7 constant_dynamic-slice_fusion.1
  511.8 20.0 %collective-permute-done.41 = bf16[256,2048]{1,0:T(8,128)(2,1)} collective-permute-done((bf16[256,2048]{1,0:T(8,128)(2,1)}, bf16[256,2048]{1,0:T(8,128)(2,1)}, u32[]{:S(2)}, u32[]{:S(2)}) %collective-permute-start.41) | collective-permute-done | bytes 1048608 | tf_op jit(solution)/shard_map/ppermute | solution.py:27
  531.9 12.5 %fusion.107 = f32[1024,1408]{1,0:T(8,128)} fusion(bf16[2048,1408]{1,0:T(8,128)(2,1)} %bitcast.113, bf16[256,2048]{1,0:T(8,128)(2,1)} %collective-permute-done.42, bf16[256,2048]{1,0:T(8,128)(2,1)} %collective-permute-done.41, bf16[256,2048]{1,0:T(8,128)(2,1)} %collective-permute-done.40, bf16[256,2048]{1,0:T(8,128)(2,1)S(1)} %copy-done.40), kind=kOutput, calls=%fused_computation.429 | convolution fusion | flops 5922357248 | bytes 15728640 | tf_op jit(solution)/shard_map/dot_general | solution.py:54
  544.4 12.7 %fusion.108 = f32[1024,1408]{1,0:T(8,128)} fusion(bf16[2048,1408]{1,0:T(8,128)(2,1)} %bitcast.96, bf16[256,2048]{1,0:T(8,128)(2,1)} %collective-permute-done.42, bf16[256,2048]{1,0:T(8,128)(2,1)} %collective-permute-done.41, bf16[256,2048]{1,0:T(8,128)(2,1)} %collective-permute-done.40, bf16[256,2048]{1,0:T(8,128)(2,1)S(1)} %copy-done.40), kind=kOutput, calls=%fused_computation.430 | convolution fusion | flops 5922357248 | bytes 15728640 | tf_op jit(solution)/shard_map/dot_general | solution.py:54
  558.2 15.5 %fusion.1 = (f32[1024]{0:T(1024)S(1)}, bf16[1024,1408]{1,0:T(8,128)(2,1)}, f32[1024,1408]{1,0:T(8,128)}) fusion(f32[1024,1408]{1,0:T(8,128)} %fusion.107, f32[1024,1408]{1,0:T(8,128)} %fusion.108, bf16[1408,2048]{1,0:T(8,128)(2,1)} %bitcast.130, bf16[256,2048]{1,0:T(8,128)(2,1)} %collective-permute-done.75, bf16[256,2048]{1,0:T(8,128)(2,1)} %collective-permute-done.74, ...), kind=kOutput, calls=%fused_computation.10 | convolution fusion | flops 5935332352 | bytes 30150656 | tf_op jit(solution)/shard_map/dot_general | solution.py:54
  590.8 7.5 multiply_convert_fusion.2
  598.3 10.8 fusion.126
  609.1 10.9 %add_convert_fusion = bf16[1024,2048]{1,0:T(8,128)(2,1)S(1)} fusion(f32[1024,2048]{1,0:T(8,128)} %fusion.126, bf16[1024,1408]{1,0:T(8,128)(2,1)S(1)} %get-tuple-element.25, bf16[2048,1408]{1,0:T(8,128)(2,1)} %bitcast.96), kind=kOutput, calls=%fused_computation.1 | convolution fusion | flops 5909774336 | bytes 21233664 | tf_op jit(solution)/shard_map/dot_general | solution.py:54
  621.8 8.7 multiply_convert_fusion
  632.8 8.4 convolution_convert_fusion.2
  644.7 8.5 convolution_convert_fusion.1
  653.2 10.9 convolution_convert_fusion
  677.8 17.8 %collective-permute-done.78 = bf16[256,2048]{1,0:T(8,128)(2,1)S(1)} collective-permute-done((bf16[256,2048]{1,0:T(8,128)(2,1)S(1)}, bf16[256,2048]{1,0:T(8,128)(2,1)S(1)}, u32[]{:S(2)}, u32[]{:S(2)}) %collective-permute-start.78) | collective-permute-done | bytes 1048608 | tf_op jit(solution)/shard_map/ppermute | solution.py:27
  697.0 20.9 %collective-permute-done.77 = bf16[256,2048]{1,0:T(8,128)(2,1)S(1)} collective-permute-done((bf16[256,2048]{1,0:T(8,128)(2,1)S(1)}, bf16[256,2048]{1,0:T(8,128)(2,1)S(1)}, u32[]{:S(2)}, u32[]{:S(2)}) %collective-permute-start.77) | collective-permute-done | bytes 1048608 | tf_op jit(solution)/shard_map/ppermute | solution.py:27
  722.6 4.7 add_convert_fusion.1
  727.8 20.6 %collective-permute-done.115 = bf16[1,88,2048]{2,1,0:T(8,128)(2,1)} collective-permute-done((bf16[1,88,2048]{2,1,0:T(8,128)(2,1)}, bf16[1,88,2048]{2,1,0:T(8,128)(2,1)}, u32[]{:S(2)}, u32[]{:S(2)}) %collective-permute-start.115) | collective-permute-done | bytes 360480 | tf_op jit(solution)/shard_map/ppermute | solution.py:27
  749.9 6.2 collective-permute-done.114
  763.9 14.5 %collective-permute-done.71 = bf16[256,2048]{1,0:T(8,128)(2,1)S(1)} collective-permute-done((bf16[256,2048]{1,0:T(8,128)(2,1)}, bf16[256,2048]{1,0:T(8,128)(2,1)S(1)}, u32[]{:S(2)}, u32[]{:S(2)}) %collective-permute-start.71) | collective-permute-done | bytes 1048608 | tf_op jit(solution)/shard_map/ppermute | solution.py:27
  779.0 13.6 %collective-permute-done.70 = bf16[256,2048]{1,0:T(8,128)(2,1)S(1)} collective-permute-done((bf16[256,2048]{1,0:T(8,128)(2,1)}, bf16[256,2048]{1,0:T(8,128)(2,1)S(1)}, u32[]{:S(2)}, u32[]{:S(2)}) %collective-permute-start.70) | collective-permute-done | bytes 1048608 | tf_op jit(solution)/shard_map/ppermute | solution.py:27
  792.7 3.9 fusion.8
  796.7 10.2 collective-permute-done.107
  808.3 5.0 add_convert_fusion.2
  817.4 21.4 %collective-permute-done.110 = bf16[64,1408]{1,0:T(8,128)(2,1)S(1)} collective-permute-done((bf16[64,1408]{1,0:T(8,128)(2,1)S(1)}, bf16[64,1408]{1,0:T(8,128)(2,1)S(1)}, u32[]{:S(2)}, u32[]{:S(2)}) %collective-permute-start.110) | collective-permute-done | bytes 180256 | tf_op jit(solution)/shard_map/ppermute | solution.py:27
  858.2 4.7 fusion.3
  875.7 5.2 collective-permute-done.87
  881.0 9.7 collective-permute-done.86
  892.5 5.7 collective-permute-done.85
  920.6 8.1 convolution_convert_fusion.4
  946.1 4.7 collective-permute-done.127
  953.4 9.1 collective-permute-done.129
  992.0 7.9 collective-permute-done.90
  1000.0 9.7 collective-permute-done.89
  1017.1 5.1 bitcast_convert_fusion
  1025.0 11.5 %collective-permute-start.98 = (f32[18,64]{1,0:T(8,128)S(1)}, f32[18,64]{1,0:T(8,128)S(1)}, u32[]{:S(2)}, u32[]{:S(2)}) collective-permute-start(f32[18,64]{1,0:T(8,128)S(1)} %bitcast.664), channel_id=1, source_target_pairs={{0,20},{4,16},{8,28},{12,24},{16,4},{20,0},{24,12},{28,8},{1,21},{... | collective-permute-start | bytes 13832 | tf_op jit(solution)/shard_map/ppermute | solution.py:27
  1040.0 4.0 add_bitcast_fusion
  1052.6 16.4 %collective-permute-start.102 = (bf16[64,1536]{1,0:T(8,128)(2,1)S(1)}, bf16[64,1536]{1,0:T(8,128)(2,1)S(1)}, u32[]{:S(2)}, u32[]{:S(2)}) collective-permute-start(bf16[64,1536]{1,0:T(8,128)(2,1)S(1)} %get-tuple-element.107), channel_id=1, source_target_pairs={{0,2},{1,3},{2,0},{3,1},{4,6},{5,7},{6,4},{7,5},{8,10},{9,11},{10,... | collective-permute-start | bytes 589832 | tf_op jit(solution)/shard_map/ppermute | solution.py:27
  (766 shorter events, 433.7 us)
Async XLA Ops:
  7.2 368.6 %all-gather.6.cloned.1.call-start = ((), (), s32[]{:S(2)}) async-start(), calls=%async_computation.4 | async-start | bytes 7077888 | tf_op jit(solution)/shard_map/all_gather | solution.py:130
  27.1 368.9 %all-gather.8.cloned.1.call-start = ((), (), s32[]{:S(2)}) async-start(), calls=%async_computation.5 | async-start | bytes 2359296 | tf_op jit(solution)/shard_map/all_gather | solution.py:133
  30.9 401.7 %all-gather.12.cloned.1.call-start = ((), (), s32[]{:S(2)}) async-start(), calls=%async_computation.11 | async-start | bytes 2621440 | tf_op jit(solution)/shard_map/all_gather | solution.py:163
  31.0 184.8 %collective-permute-start.2 = (bf16[128,2048]{1,0:T(8,128)(2,1)S(1)}, bf16[128,2048]{1,0:T(8,128)(2,1)}, u32[]{:S(2)}, u32[]{:S(2)}) collective-permute-start(bf16[128,2048]{1,0:T(8,128)(2,1)S(1)} %bitcast.613), channel_id=1, source_target_pairs={{0,3},{1,2},{2,1},{3,0},{4,7},{5,6},{6,5},{7,4},{8,11},{9,10},{10,... | collective-permute-start | bytes 1572872 | tf_op jit(solution)/shard_map/ppermute | solution.py:27
  46.0 169.9 %collective-permute-start.1 = (bf16[128,2048]{1,0:T(8,128)(2,1)S(1)}, bf16[128,2048]{1,0:T(8,128)(2,1)}, u32[]{:S(2)}, u32[]{:S(2)}) collective-permute-start(bf16[128,2048]{1,0:T(8,128)(2,1)S(1)} %bitcast.614), channel_id=1, source_target_pairs={{0,2},{1,3},{2,0},{3,1},{4,6},{5,7},{6,4},{7,5},{8,10},{9,11},{10,... | collective-permute-start | bytes 1572872 | tf_op jit(solution)/shard_map/ppermute | solution.py:27
  52.0 50.6 %collective-permute-start.3 = (bf16[18,64]{1,0:T(8,128)(2,1)S(1)}, bf16[18,64]{1,0:T(8,128)(2,1)S(1)}, u32[]{:S(2)}, u32[]{:S(2)}) collective-permute-start(bf16[18,64]{1,0:T(8,128)(2,1)S(1)} %get-tuple-element.152), channel_id=1, source_target_pairs={{0,1},{1,0},{2,3},{3,2},{4,5},{5,4},{6,7},{7,6},{8,9},{9,8},{10,11... | collective-permute-start | bytes 6920 | tf_op jit(solution)/shard_map/ppermute | solution.py:27
  52.1 50.5 %collective-permute-start.4 = (bf16[18,64]{1,0:T(8,128)(2,1)S(1)}, bf16[18,64]{1,0:T(8,128)(2,1)S(1)}, u32[]{:S(2)}, u32[]{:S(2)}) collective-permute-start(bf16[18,64]{1,0:T(8,128)(2,1)S(1)} %get-tuple-element.152), channel_id=1, source_target_pairs={{0,2},{1,3},{2,0},{3,1},{4,6},{5,7},{6,4},{7,5},{8,10},{9,11},{10,... | collective-permute-start | bytes 6920 | tf_op jit(solution)/shard_map/ppermute | solution.py:27
  52.7 56.1 %collective-permute-start.5 = (bf16[18,64]{1,0:T(8,128)(2,1)S(1)}, bf16[18,64]{1,0:T(8,128)(2,1)S(1)}, u32[]{:S(2)}, u32[]{:S(2)}) collective-permute-start(bf16[18,64]{1,0:T(8,128)(2,1)S(1)} %get-tuple-element.152), channel_id=1, source_target_pairs={{0,3},{1,2},{2,1},{3,0},{4,7},{5,6},{6,5},{7,4},{8,11},{9,10},{10,... | collective-permute-start | bytes 6920 | tf_op jit(solution)/shard_map/ppermute | solution.py:27
  55.6 416.8 %all-gather.10.cloned.1.call-start = ((), (), s32[]{:S(2)}) async-start(), calls=%async_computation.6 | async-start | bytes 2621440 | tf_op jit(solution)/shard_map/all_gather | solution.py:218
  113.8 103.4 %collective-permute-start = (bf16[128,2048]{1,0:T(8,128)(2,1)S(1)}, bf16[128,2048]{1,0:T(8,128)(2,1)}, u32[]{:S(2)}, u32[]{:S(2)}) collective-permute-start(bf16[128,2048]{1,0:T(8,128)(2,1)S(1)} %bitcast.615), channel_id=1, source_target_pairs={{0,1},{1,0},{2,3},{3,2},{4,5},{5,4},{6,7},{7,6},{8,9},{9,8},{10,11... | collective-permute-start | bytes 1572872 | tf_op jit(solution)/shard_map/ppermute | solution.py:27
  115.2 84.7 %collective-permute-start.30 = (bf16[88,2048]{1,0:T(8,128)(2,1)}, bf16[88,2048]{1,0:T(8,128)(2,1)}, u32[]{:S(2)}, u32[]{:S(2)}) collective-permute-start(bf16[88,2048]{1,0:T(8,128)(2,1)} %param.29), channel_id=1, source_target_pairs={{0,1},{1,0},{2,3},{3,2},{4,5},{5,4},{6,7},{7,6},{8,9},{9,8},{10,11... | collective-permute-start | bytes 1081352 | tf_op jit(solution)/shard_map/ppermute | solution.py:27
  213.8 47.5 %collective-permute-start.51 = (bf16[2,256,1408]{2,1,0:T(8,128)(2,1)S(1)}, bf16[2,256,1408]{2,1,0:T(8,128)(2,1)S(1)}, u32[]{:S(2)}, u32[]{:S(2)}) collective-permute-start(bf16[2,256,1408]{2,1,0:T(8,128)(2,1)S(1)} %copy-done.35), channel_id=1, source_target_pairs={{0,4},{4,0},{1,5},{5,1},{2,6},{6,2},{3,7},{7,3},{8,12},{12,8},{9,1... | collective-permute-start | bytes 4325384 | tf_op jit(solution)/shard_map/ppermute | solution.py:27
  214.6 46.8 %collective-permute-start.43 = (bf16[2,256,1408]{2,1,0:T(8,128)(2,1)S(1)}, bf16[2,256,1408]{2,1,0:T(8,128)(2,1)S(1)}, u32[]{:S(2)}, u32[]{:S(2)}) collective-permute-start(bf16[2,256,1408]{2,1,0:T(8,128)(2,1)S(1)} %copy-done.34), channel_id=1, source_target_pairs={{0,4},{4,0},{1,5},{5,1},{2,6},{6,2},{3,7},{7,3},{8,12},{12,8},{9,1... | collective-permute-start | bytes 4325384 | tf_op jit(solution)/shard_map/ppermute | solution.py:27
  215.9 50.5 %collective-permute-start.59 = (bf16[2,176,2048]{2,1,0:T(8,128)(2,1)S(1)}, bf16[2,176,2048]{2,1,0:T(8,128)(2,1)S(1)}, u32[]{:S(2)}, u32[]{:S(2)}) collective-permute-start(bf16[2,176,2048]{2,1,0:T(8,128)(2,1)S(1)} %copy-done.33), channel_id=1, source_target_pairs={{0,4},{4,0},{1,5},{5,1},{2,6},{6,2},{3,7},{7,3},{8,12},{12,8},{9,1... | collective-permute-start | bytes 4325384 | tf_op jit(solution)/shard_map/ppermute | solution.py:27
  234.6 25.9 %collective-permute-start.25 = (bf16[4,64,1408]{2,1,0:T(8,128)(2,1)}, bf16[4,64,1408]{2,1,0:T(8,128)(2,1)S(1)}, u32[]{:S(2)}, u32[]{:S(2)}) collective-permute-start(bf16[4,64,1408]{2,1,0:T(8,128)(2,1)} %bitcast_dynamic-update-slice_fusion.69), channel_id=1, source_target_pairs={{0,3},{1,2},{2,1},{3,0},{4,7},{5,6},{6,5},{7,4},{8,11},{9,10},{10,... | collective-permute-start | bytes 2162696 | tf_op jit(solution)/shard_map/ppermute | solution.py:27
  279.6 57.7 %collective-permute-start.55 = (bf16[256,1408]{1,0:T(8,128)(2,1)S(1)}, bf16[256,1408]{1,0:T(8,128)(2,1)S(1)}, u32[]{:S(2)}, u32[]{:S(2)}) collective-permute-start(bf16[256,1408]{1,0:T(8,128)(2,1)S(1)} %get-tuple-element.72), channel_id=1, source_target_pairs={{0,2},{1,3},{2,0},{3,1},{4,6},{5,7},{6,4},{7,5},{8,10},{9,11},{10,... | collective-permute-start | bytes 2162696 | tf_op jit(solution)/shard_map/ppermute | solution.py:27
  280.4 93.7 %collective-permute-start.57 = (bf16[256,1408]{1,0:T(8,128)(2,1)S(1)}, bf16[256,1408]{1,0:T(8,128)(2,1)S(1)}, u32[]{:S(2)}, u32[]{:S(2)}) collective-permute-start(bf16[256,1408]{1,0:T(8,128)(2,1)S(1)} %get-tuple-element.70), channel_id=1, source_target_pairs={{0,3},{1,2},{2,1},{3,0},{4,7},{5,6},{6,5},{7,4},{8,11},{9,10},{10,... | collective-permute-start | bytes 2162696 | tf_op jit(solution)/shard_map/ppermute | solution.py:27
  282.2 34.0 %collective-permute-start.45 = (bf16[256,1408]{1,0:T(8,128)(2,1)S(1)}, bf16[256,1408]{1,0:T(8,128)(2,1)S(1)}, u32[]{:S(2)}, u32[]{:S(2)}) collective-permute-start(bf16[256,1408]{1,0:T(8,128)(2,1)S(1)} %get-tuple-element.68), channel_id=1, source_target_pairs={{0,1},{1,0},{2,3},{3,2},{4,5},{5,4},{6,7},{7,6},{8,9},{9,8},{10,11... | collective-permute-start | bytes 2162696 | tf_op jit(solution)/shard_map/ppermute | solution.py:27
  285.0 55.7 %collective-permute-start.47 = (bf16[256,1408]{1,0:T(8,128)(2,1)S(1)}, bf16[256,1408]{1,0:T(8,128)(2,1)S(1)}, u32[]{:S(2)}, u32[]{:S(2)}) collective-permute-start(bf16[256,1408]{1,0:T(8,128)(2,1)S(1)} %get-tuple-element.67), channel_id=1, source_target_pairs={{0,2},{1,3},{2,0},{3,1},{4,6},{5,7},{6,4},{7,5},{8,10},{9,11},{10,... | collective-permute-start | bytes 2162696 | tf_op jit(solution)/shard_map/ppermute | solution.py:27
  286.7 31.8 %collective-permute-start.60 = (bf16[176,2048]{1,0:T(8,128)(2,1)S(1)}, bf16[176,2048]{1,0:T(8,128)(2,1)S(1)}, u32[]{:S(2)}, u32[]{:S(2)}) collective-permute-start(bf16[176,2048]{1,0:T(8,128)(2,1)S(1)} %get-tuple-element.76), channel_id=1, source_target_pairs={{0,4},{4,0},{1,5},{5,1},{2,6},{6,2},{3,7},{7,3},{8,12},{12,8},{9,1... | collective-permute-start | bytes 2162696 | tf_op jit(solution)/shard_map/ppermute | solution.py:27
  334.0 70.9 %collective-permute-start.49 = (bf16[256,1408]{1,0:T(8,128)(2,1)}, bf16[256,1408]{1,0:T(8,128)(2,1)}, u32[]{:S(2)}, u32[]{:S(2)}) collective-permute-start(bf16[256,1408]{1,0:T(8,128)(2,1)} %get-tuple-element.65), channel_id=1, source_target_pairs={{0,3},{1,2},{2,1},{3,0},{4,7},{5,6},{6,5},{7,4},{8,11},{9,10},{10,... | collective-permute-start | bytes 2162696 | tf_op jit(solution)/shard_map/ppermute | solution.py:27
  337.3 32.3 %collective-permute-start.63 = (bf16[176,2048]{1,0:T(8,128)(2,1)S(1)}, bf16[176,2048]{1,0:T(8,128)(2,1)}, u32[]{:S(2)}, u32[]{:S(2)}) collective-permute-start(bf16[176,2048]{1,0:T(8,128)(2,1)S(1)} %get-tuple-element.77), channel_id=1, source_target_pairs={{0,2},{1,3},{2,0},{3,1},{4,6},{5,7},{6,4},{7,5},{8,10},{9,11},{10,... | collective-permute-start | bytes 2162696 | tf_op jit(solution)/shard_map/ppermute | solution.py:27
  340.7 28.9 %collective-permute-start.62 = (bf16[176,2048]{1,0:T(8,128)(2,1)S(1)}, bf16[176,2048]{1,0:T(8,128)(2,1)S(1)}, u32[]{:S(2)}, u32[]{:S(2)}) collective-permute-start(bf16[176,2048]{1,0:T(8,128)(2,1)S(1)} %collective-permute-done.61), channel_id=1, source_target_pairs={{0,4},{4,0},{1,5},{5,1},{2,6},{6,2},{3,7},{7,3},{8,12},{12,8},{9,1... | collective-permute-start | bytes 2162696 | tf_op jit(solution)/shard_map/ppermute | solution.py:27
  341.9 65.0 %collective-permute-start.65 = (bf16[176,2048]{1,0:T(8,128)(2,1)}, bf16[176,2048]{1,0:T(8,128)(2,1)}, u32[]{:S(2)}, u32[]{:S(2)}) collective-permute-start(bf16[176,2048]{1,0:T(8,128)(2,1)} %get-tuple-element.75), channel_id=1, source_target_pairs={{0,3},{1,2},{2,1},{3,0},{4,7},{5,6},{6,5},{7,4},{8,11},{9,10},{10,... | collective-permute-start | bytes 2162696 | tf_op jit(solution)/shard_map/ppermute | solution.py:27
  369.6 31.9 %collective-permute-start.64 = (bf16[176,2048]{1,0:T(8,128)(2,1)}, bf16[176,2048]{1,0:T(8,128)(2,1)}, u32[]{:S(2)}, u32[]{:S(2)}) collective-permute-start(bf16[176,2048]{1,0:T(8,128)(2,1)} %collective-permute-done.63), channel_id=1, source_target_pairs={{0,4},{4,0},{1,5},{5,1},{2,6},{6,2},{3,7},{7,3},{8,12},{12,8},{9,1... | collective-permute-start | bytes 2162696 | tf_op jit(solution)/shard_map/ppermute | solution.py:27
  404.9 25.9 %collective-permute-start.58 = (bf16[256,1408]{1,0:T(8,128)(2,1)S(1)}, bf16[256,1408]{1,0:T(8,128)(2,1)S(1)}, u32[]{:S(2)}, u32[]{:S(2)}) collective-permute-start(bf16[256,1408]{1,0:T(8,128)(2,1)S(1)} %copy-done.47), channel_id=1, source_target_pairs={{0,4},{4,0},{1,5},{5,1},{2,6},{6,2},{3,7},{7,3},{8,12},{12,8},{9,1... | collective-permute-start | bytes 2162696 | tf_op jit(solution)/shard_map/ppermute | solution.py:27
  427.8 435.0 %reduce-scatter.7.cloned.1.call-start = ((), (), s32[]{:S(2)}) async-start(), calls=%async_computation.8 | async-start | bytes 2621440 | tf_op jit(solution)/shard_map/reduce_scatter | solution.py:280
  438.9 118.2 %collective-permute-start.75 = (bf16[256,2048]{1,0:T(8,128)(2,1)}, bf16[256,2048]{1,0:T(8,128)(2,1)}, u32[]{:S(2)}, u32[]{:S(2)}) collective-permute-start(bf16[256,2048]{1,0:T(8,128)(2,1)} %get-tuple-element.44), channel_id=1, source_target_pairs={{0,3},{1,2},{2,1},{3,0},{4,7},{5,6},{6,5},{7,4},{8,11},{9,10},{10,... | collective-permute-start | bytes 3145736 | tf_op jit(solution)/shard_map/ppermute | solution.py:27
  440.5 116.6 %collective-permute-start.74 = (bf16[256,2048]{1,0:T(8,128)(2,1)}, bf16[256,2048]{1,0:T(8,128)(2,1)}, u32[]{:S(2)}, u32[]{:S(2)}) collective-permute-start(bf16[256,2048]{1,0:T(8,128)(2,1)} %get-tuple-element.45), channel_id=1, source_target_pairs={{0,2},{1,3},{2,0},{3,1},{4,6},{5,7},{6,4},{7,5},{8,10},{9,11},{10,... | collective-permute-start | bytes 3145736 | tf_op jit(solution)/shard_map/ppermute | solution.py:27
  478.5 32.7 %collective-permute-start.42 = (bf16[256,2048]{1,0:T(8,128)(2,1)}, bf16[256,2048]{1,0:T(8,128)(2,1)}, u32[]{:S(2)}, u32[]{:S(2)}) collective-permute-start(bf16[256,2048]{1,0:T(8,128)(2,1)} %get-tuple-element.40), channel_id=1, source_target_pairs={{0,3},{1,2},{2,1},{3,0},{4,7},{5,6},{6,5},{7,4},{8,11},{9,10},{10,... | collective-permute-start | bytes 3145736 | tf_op jit(solution)/shard_map/ppermute | solution.py:27
  480.8 51.0 %collective-permute-start.41 = (bf16[256,2048]{1,0:T(8,128)(2,1)}, bf16[256,2048]{1,0:T(8,128)(2,1)}, u32[]{:S(2)}, u32[]{:S(2)}) collective-permute-start(bf16[256,2048]{1,0:T(8,128)(2,1)} %get-tuple-element.41), channel_id=1, source_target_pairs={{0,2},{1,3},{2,0},{3,1},{4,6},{5,7},{6,4},{7,5},{8,10},{9,11},{10,... | collective-permute-start | bytes 3145736 | tf_op jit(solution)/shard_map/ppermute | solution.py:27
  481.4 50.4 %collective-permute-start.40 = (bf16[256,2048]{1,0:T(8,128)(2,1)}, bf16[256,2048]{1,0:T(8,128)(2,1)}, u32[]{:S(2)}, u32[]{:S(2)}) collective-permute-start(bf16[256,2048]{1,0:T(8,128)(2,1)} %get-tuple-element.42), channel_id=1, source_target_pairs={{0,1},{1,0},{2,3},{3,2},{4,5},{5,4},{6,7},{7,6},{8,9},{9,8},{10,11... | collective-permute-start | bytes 3145736 | tf_op jit(solution)/shard_map/ppermute | solution.py:27
  511.2 46.0 %collective-permute-start.73 = (bf16[256,2048]{1,0:T(8,128)(2,1)S(1)}, bf16[256,2048]{1,0:T(8,128)(2,1)S(1)}, u32[]{:S(2)}, u32[]{:S(2)}) collective-permute-start(bf16[256,2048]{1,0:T(8,128)(2,1)S(1)} %copy-done.43), channel_id=1, source_target_pairs={{0,1},{1,0},{2,3},{3,2},{4,5},{5,4},{6,7},{7,6},{8,9},{9,8},{10,11... | collective-permute-start | bytes 3145736 | tf_op jit(solution)/shard_map/ppermute | solution.py:27
  531.8 227.2 %collective-permute-start.105 = (bf16[4,4,64,1408]{3,2,0,1:T(8,128)(2,1)}, bf16[4,4,64,1408]{3,2,0,1:T(8,128)(2,1)}, u32[]{:S(2)}, u32[]{:S(2)}) collective-permute-start(bf16[4,4,64,1408]{3,2,0,1:T(8,128)(2,1)} %bitcast.580), channel_id=1, source_target_pairs={{0,4},{4,0},{1,5},{5,1},{2,6},{6,2},{3,7},{7,3},{8,12},{12,8},{9,1... | collective-permute-start | bytes 8650760 | tf_op jit(solution)/shard_map/ppermute | solution.py:27
  578.4 93.7 %collective-permute-start.112 = (bf16[1,4,88,2048]{3,2,1,0:T(8,128)(2,1)}, bf16[1,4,88,2048]{3,2,1,0:T(8,128)(2,1)}, u32[]{:S(2)}, u32[]{:S(2)}) collective-permute-start(bf16[1,4,88,2048]{3,2,1,0:T(8,128)(2,1)} %dynamic-slice_bitcast_fusion.6), channel_id=1, source_target_pairs={{0,4},{4,0},{1,5},{5,1},{2,6},{6,2},{3,7},{7,3},{8,12},{12,8},{9,1... | collective-permute-start | bytes 4325384 | tf_op jit(solution)/shard_map/ppermute | solution.py:27
  586.4 82.1 %collective-permute-start.82 = (f32[4,128]{1,0:T(4,128)S(1)}, f32[4,128]{1,0:T(4,128)S(1)}, u32[]{:S(2)}, u32[]{:S(2)}) collective-permute-start(f32[4,128]{1,0:T(4,128)S(1)} %bitcast.678), channel_id=1, source_target_pairs={{0,8},{8,0},{16,24},{24,16},{1,9},{9,1},{17,25},{25,17},{2,10},{10... | collective-permute-start | bytes 6152 | tf_op jit(solution)/shard_map/ppermute | solution.py:27
  587.0 83.0 %collective-permute-start.83 = (f32[4,128]{1,0:T(4,128)S(1)}, f32[4,128]{1,0:T(4,128)S(1)}, u32[]{:S(2)}, u32[]{:S(2)}) collective-permute-start(f32[4,128]{1,0:T(4,128)S(1)} %bitcast.677), channel_id=1, source_target_pairs={{0,16},{8,24},{16,0},{24,8},{1,17},{9,25},{17,1},{25,9},{2,18},{10... | collective-permute-start | bytes 6152 | tf_op jit(solution)/shard_map/ppermute | solution.py:27
  588.5 82.9 %collective-permute-start.84 = (f32[4,128]{1,0:T(4,128)S(1)}, f32[4,128]{1,0:T(4,128)S(1)}, u32[]{:S(2)}, u32[]{:S(2)}) collective-permute-start(f32[4,128]{1,0:T(4,128)S(1)} %bitcast.676), channel_id=1, source_target_pairs={{0,24},{8,16},{16,8},{24,0},{1,25},{9,17},{17,9},{25,1},{2,26},{10... | collective-permute-start | bytes 6152 | tf_op jit(solution)/shard_map/ppermute | solution.py:27
  668.5 27.1 %collective-permute-start.78 = (bf16[256,2048]{1,0:T(8,128)(2,1)S(1)}, bf16[256,2048]{1,0:T(8,128)(2,1)S(1)}, u32[]{:S(2)}, u32[]{:S(2)}) collective-permute-start(bf16[256,2048]{1,0:T(8,128)(2,1)S(1)} %get-tuple-element.32), channel_id=1, source_target_pairs={{0,3},{1,2},{2,1},{3,0},{4,7},{5,6},{6,5},{7,4},{8,11},{9,10},{10,... | collective-permute-start | bytes 3145736 | tf_op jit(solution)/shard_map/ppermute | solution.py:27
  670.0 47.9 %collective-permute-start.77 = (bf16[256,2048]{1,0:T(8,128)(2,1)S(1)}, bf16[256,2048]{1,0:T(8,128)(2,1)S(1)}, u32[]{:S(2)}, u32[]{:S(2)}) collective-permute-start(bf16[256,2048]{1,0:T(8,128)(2,1)S(1)} %get-tuple-element.33), channel_id=1, source_target_pairs={{0,2},{1,3},{2,0},{3,1},{4,6},{5,7},{6,4},{7,5},{8,10},{9,11},{10,... | collective-permute-start | bytes 3145736 | tf_op jit(solution)/shard_map/ppermute | solution.py:27
  671.4 47.2 %collective-permute-start.76 = (bf16[256,2048]{1,0:T(8,128)(2,1)S(1)}, bf16[256,2048]{1,0:T(8,128)(2,1)S(1)}, u32[]{:S(2)}, u32[]{:S(2)}) collective-permute-start(bf16[256,2048]{1,0:T(8,128)(2,1)S(1)} %get-tuple-element.34), channel_id=1, source_target_pairs={{0,1},{1,0},{2,3},{3,2},{4,5},{5,4},{6,7},{7,6},{8,9},{9,8},{10,11... | collective-permute-start | bytes 3145736 | tf_op jit(solution)/shard_map/ppermute | solution.py:27
  672.1 90.3 %collective-permute-start.72 = (bf16[256,2048]{1,0:T(8,128)(2,1)}, bf16[256,2048]{1,0:T(8,128)(2,1)}, u32[]{:S(2)}, u32[]{:S(2)}) collective-permute-start(bf16[256,2048]{1,0:T(8,128)(2,1)} %get-tuple-element.36), channel_id=1, source_target_pairs={{0,3},{1,2},{2,1},{3,0},{4,7},{5,6},{6,5},{7,4},{8,11},{9,10},{10,... | collective-permute-start | bytes 3145736 | tf_op jit(solution)/shard_map/ppermute | solution.py:27
  695.6 52.8 %collective-permute-start.115 = (bf16[1,88,2048]{2,1,0:T(8,128)(2,1)}, bf16[1,88,2048]{2,1,0:T(8,128)(2,1)}, u32[]{:S(2)}, u32[]{:S(2)}) collective-permute-start(bf16[1,88,2048]{2,1,0:T(8,128)(2,1)} %get-tuple-element.98), channel_id=1, source_target_pairs={{0,3},{1,2},{2,1},{3,0},{4,7},{5,6},{6,5},{7,4},{8,11},{9,10},{10,... | collective-permute-start | bytes 1081352 | tf_op jit(solution)/shard_map/ppermute | solution.py:27
  718.0 38.1 %collective-permute-start.114 = (bf16[1,88,2048]{2,1,0:T(8,128)(2,1)}, bf16[1,88,2048]{2,1,0:T(8,128)(2,1)}, u32[]{:S(2)}, u32[]{:S(2)}) collective-permute-start(bf16[1,88,2048]{2,1,0:T(8,128)(2,1)} %get-tuple-element.99), channel_id=1, source_target_pairs={{0,2},{1,3},{2,0},{3,1},{4,6},{5,7},{6,4},{7,5},{8,10},{9,11},{10,... | collective-permute-start | bytes 1081352 | tf_op jit(solution)/shard_map/ppermute | solution.py:27
  718.6 38.1 %collective-permute-start.113 = (bf16[1,88,2048]{2,1,0:T(8,128)(2,1)}, bf16[1,88,2048]{2,1,0:T(8,128)(2,1)}, u32[]{:S(2)}, u32[]{:S(2)}) collective-permute-start(bf16[1,88,2048]{2,1,0:T(8,128)(2,1)} %get-tuple-element.97), channel_id=1, source_target_pairs={{0,1},{1,0},{2,3},{3,2},{4,5},{5,4},{6,7},{7,6},{8,9},{9,8},{10,11... | collective-permute-start | bytes 1081352 | tf_op jit(solution)/shard_map/ppermute | solution.py:27
  727.4 312.6 %reduce-scatter.5.cloned.1.call-start = ((), (), s32[]{:S(2)}) async-start(), calls=%async_computation.7 | async-start | bytes 2621440 | tf_op jit(solution)/shard_map/reduce_scatter | solution.py:325
  748.4 30.0 %collective-permute-start.71 = (bf16[256,2048]{1,0:T(8,128)(2,1)}, bf16[256,2048]{1,0:T(8,128)(2,1)S(1)}, u32[]{:S(2)}, u32[]{:S(2)}) collective-permute-start(bf16[256,2048]{1,0:T(8,128)(2,1)} %get-tuple-element.37), channel_id=1, source_target_pairs={{0,2},{1,3},{2,0},{3,1},{4,6},{5,7},{6,4},{7,5},{8,10},{9,11},{10,... | collective-permute-start | bytes 3145736 | tf_op jit(solution)/shard_map/ppermute | solution.py:27
  756.0 36.6 %collective-permute-start.70 = (bf16[256,2048]{1,0:T(8,128)(2,1)}, bf16[256,2048]{1,0:T(8,128)(2,1)S(1)}, u32[]{:S(2)}, u32[]{:S(2)}) collective-permute-start(bf16[256,2048]{1,0:T(8,128)(2,1)} %get-tuple-element.38), channel_id=1, source_target_pairs={{0,1},{1,0},{2,3},{3,2},{4,5},{5,4},{6,7},{7,6},{8,9},{9,8},{10,11... | collective-permute-start | bytes 3145736 | tf_op jit(solution)/shard_map/ppermute | solution.py:27
  756.7 86.2 %collective-permute-start.116 = (bf16[4,256,1408]{2,1,0:T(8,128)(2,1)}, bf16[4,256,1408]{2,1,0:T(8,128)(2,1)}, u32[]{:S(2)}, u32[]{:S(2)}) collective-permute-start(bf16[4,256,1408]{2,1,0:T(8,128)(2,1)} %dynamic-slice_bitcast_fusion.2), channel_id=1, source_target_pairs={{0,4},{4,0},{1,5},{5,1},{2,6},{6,2},{3,7},{7,3},{8,12},{12,8},{9,1... | collective-permute-start | bytes 8650760 | tf_op jit(solution)/shard_map/ppermute | solution.py:27
  759.0 92.9 %collective-permute-start.121 = (bf16[4,256,1408]{2,1,0:T(8,128)(2,1)}, bf16[4,256,1408]{2,1,0:T(8,128)(2,1)}, u32[]{:S(2)}, u32[]{:S(2)}) collective-permute-start(bf16[4,256,1408]{2,1,0:T(8,128)(2,1)} %dynamic-slice_bitcast_fusion.1), channel_id=1, source_target_pairs={{0,4},{4,0},{1,5},{5,1},{2,6},{6,2},{3,7},{7,3},{8,12},{12,8},{9,1... | collective-permute-start | bytes 8650760 | tf_op jit(solution)/shard_map/ppermute | solution.py:27
  762.5 34.1 %collective-permute-start.108 = (bf16[4,64,1408]{2,1,0:T(8,128)(2,1)S(1)}, bf16[4,64,1408]{2,1,0:T(8,128)(2,1)S(1)}, u32[]{:S(2)}, u32[]{:S(2)}) collective-permute-start(bf16[4,64,1408]{2,1,0:T(8,128)(2,1)S(1)} %get-tuple-element.62), channel_id=1, source_target_pairs={{0,3},{1,2},{2,1},{3,0},{4,7},{5,6},{6,5},{7,4},{8,11},{9,10},{10,... | collective-permute-start | bytes 2162696 | tf_op jit(solution)/shard_map/ppermute | solution.py:27
  778.4 28.5 %collective-permute-start.107 = (bf16[4,64,1408]{2,1,0:T(8,128)(2,1)S(1)}, bf16[4,64,1408]{2,1,0:T(8,128)(2,1)S(1)}, u32[]{:S(2)}, u32[]{:S(2)}) collective-permute-start(bf16[4,64,1408]{2,1,0:T(8,128)(2,1)S(1)} %get-tuple-element.63), channel_id=1, source_target_pairs={{0,2},{1,3},{2,0},{3,1},{4,6},{5,7},{6,4},{7,5},{8,10},{9,11},{10,... | collective-permute-start | bytes 2162696 | tf_op jit(solution)/shard_map/ppermute | solution.py:27
  796.6 61.5 %collective-permute-start.126 = (bf16[4,176,2048]{2,1,0:T(8,128)(2,1)}, bf16[4,176,2048]{2,1,0:T(8,128)(2,1)}, u32[]{:S(2)}, u32[]{:S(2)}) collective-permute-start(bf16[4,176,2048]{2,1,0:T(8,128)(2,1)} %dynamic-slice_bitcast_fusion), channel_id=1, source_target_pairs={{0,4},{4,0},{1,5},{5,1},{2,6},{6,2},{3,7},{7,3},{8,12},{12,8},{9,1... | collective-permute-start | bytes 8650760 | tf_op jit(solution)/shard_map/ppermute | solution.py:27
  813.3 231.3 %reduce-scatter.11.cloned.1.call-start = ((), (), s32[]{:S(2)}) async-start(), calls=%async_computation.10 | async-start | bytes 2359296 | tf_op jit(solution)/shard_map/reduce_scatter | solution.py:359
  849.8 79.0 %collective-permute-start.118 = (bf16[256,1408]{1,0:T(8,128)(2,1)}, bf16[256,1408]{1,0:T(8,128)(2,1)}, u32[]{:S(2)}, u32[]{:S(2)}) collective-permute-start(bf16[256,1408]{1,0:T(8,128)(2,1)} %get-tuple-element.58), channel_id=1, source_target_pairs={{0,2},{1,3},{2,0},{3,1},{4,6},{5,7},{6,4},{7,5},{8,10},{9,11},{10,... | collective-permute-start | bytes 2162696 | tf_op jit(solution)/shard_map/ppermute | solution.py:27
  866.6 31.7 %collective-permute-start.85 = (bf16[128,2048]{1,0:T(8,128)(2,1)S(1)}, bf16[128,2048]{1,0:T(8,128)(2,1)S(1)}, u32[]{:S(2)}, u32[]{:S(2)}) collective-permute-start(bf16[128,2048]{1,0:T(8,128)(2,1)S(1)} %fusion.106), channel_id=1, source_target_pairs={{0,1},{1,0},{2,3},{3,2},{4,5},{5,4},{6,7},{7,6},{8,9},{9,8},{10,11... | collective-permute-start | bytes 1572872 | tf_op jit(solution)/shard_map/ppermute | solution.py:27
  872.1 58.8 %collective-permute-start.119 = (bf16[256,1408]{1,0:T(8,128)(2,1)}, bf16[256,1408]{1,0:T(8,128)(2,1)}, u32[]{:S(2)}, u32[]{:S(2)}) collective-permute-start(bf16[256,1408]{1,0:T(8,128)(2,1)} %get-tuple-element.57), channel_id=1, source_target_pairs={{0,3},{1,2},{2,1},{3,0},{4,7},{5,6},{6,5},{7,4},{8,11},{9,10},{10,... | collective-permute-start | bytes 2162696 | tf_op jit(solution)/shard_map/ppermute | solution.py:27
  880.9 53.6 %collective-permute-start.122 = (bf16[256,1408]{1,0:T(8,128)(2,1)}, bf16[256,1408]{1,0:T(8,128)(2,1)}, u32[]{:S(2)}, u32[]{:S(2)}) collective-permute-start(bf16[256,1408]{1,0:T(8,128)(2,1)} %get-tuple-element.55), channel_id=1, source_target_pairs={{0,1},{1,0},{2,3},{3,2},{4,5},{5,4},{6,7},{7,6},{8,9},{9,8},{10,11... | collective-permute-start | bytes 2162696 | tf_op jit(solution)/shard_map/ppermute | solution.py:27
  890.7 49.3 %collective-permute-start.123 = (bf16[256,1408]{1,0:T(8,128)(2,1)}, bf16[256,1408]{1,0:T(8,128)(2,1)}, u32[]{:S(2)}, u32[]{:S(2)}) collective-permute-start(bf16[256,1408]{1,0:T(8,128)(2,1)} %get-tuple-element.54), channel_id=1, source_target_pairs={{0,2},{1,3},{2,0},{3,1},{4,6},{5,7},{6,4},{7,5},{8,10},{9,11},{10,... | collective-permute-start | bytes 2162696 | tf_op jit(solution)/shard_map/ppermute | solution.py:27
  898.2 43.8 %collective-permute-start.124 = (bf16[256,1408]{1,0:T(8,128)(2,1)}, bf16[256,1408]{1,0:T(8,128)(2,1)}, u32[]{:S(2)}, u32[]{:S(2)}) collective-permute-start(bf16[256,1408]{1,0:T(8,128)(2,1)} %get-tuple-element.53), channel_id=1, source_target_pairs={{0,3},{1,2},{2,1},{3,0},{4,7},{5,6},{6,5},{7,4},{8,11},{9,10},{10,... | collective-permute-start | bytes 2162696 | tf_op jit(solution)/shard_map/ppermute | solution.py:27
  902.9 143.5 %reduce-scatter.9.cloned.1.call-start = ((), (), s32[]{:S(2)}) async-start(), calls=%async_computation.9 | async-start | bytes 7077888 | tf_op jit(solution)/shard_map/reduce_scatter | solution.py:362
  934.5 28.1 %collective-permute-start.129 = (bf16[176,2048]{1,0:T(8,128)(2,1)}, bf16[176,2048]{1,0:T(8,128)(2,1)S(1)}, u32[]{:S(2)}, u32[]{:S(2)}) collective-permute-start(bf16[176,2048]{1,0:T(8,128)(2,1)} %get-tuple-element.49), channel_id=1, source_target_pairs={{0,3},{1,2},{2,1},{3,0},{4,7},{5,6},{6,5},{7,4},{8,11},{9,10},{10,... | collective-permute-start | bytes 2162696 | tf_op jit(solution)/shard_map/ppermute | solution.py:27
  940.0 33.7 %collective-permute-start.120 = (bf16[2,256,1408]{2,1,0:T(8,128)(2,1)S(1)}, bf16[2,256,1408]{2,1,0:T(8,128)(2,1)S(1)}, u32[]{:S(2)}, u32[]{:S(2)}) collective-permute-start(bf16[2,256,1408]{2,1,0:T(8,128)(2,1)S(1)} %dynamic-slice_bitcast_fusion.5), channel_id=1, source_target_pairs={{0,4},{4,0},{1,5},{5,1},{2,6},{6,2},{3,7},{7,3},{8,12},{12,8},{9,1... | collective-permute-start | bytes 4325384 | tf_op jit(solution)/shard_map/ppermute | solution.py:27
  945.6 28.3 %collective-permute-start.125 = (bf16[2,256,1408]{2,1,0:T(8,128)(2,1)S(1)}, bf16[2,256,1408]{2,1,0:T(8,128)(2,1)S(1)}, u32[]{:S(2)}, u32[]{:S(2)}) collective-permute-start(bf16[2,256,1408]{2,1,0:T(8,128)(2,1)S(1)} %dynamic-slice_bitcast_fusion.4), channel_id=1, source_target_pairs={{0,4},{4,0},{1,5},{5,1},{2,6},{6,2},{3,7},{7,3},{8,12},{12,8},{9,1... | collective-permute-start | bytes 4325384 | tf_op jit(solution)/shard_map/ppermute | solution.py:27
  (183 other events, 2949.0 us)
Sparse Core Ops, SparseCore 0:
  27.2 67.6 all-gather.5
  96.6 28.1 all-gather.7
  126.3 48.3 all-gather.11
  427.9 44.3 all-gather.9
  727.5 41.5 reduce-scatter.6
  813.4 48.1 reduce-scatter.4
  903.0 43.5 reduce-scatter.10
  948.9 68.2 reduce-scatter.8
where the time goes:
time: 1100 us; the launch traced here: 1090 us
  waiting for transfers between devices  416 us (38%)
  local copies, waits for them, and re-layouts  205 us (19%)
  matrix products  185 us (17%)
  starting transfers between devices  181 us (16%)
  other arithmetic  78.9 us (7%)
  between operations  24.4 us (2%)
    ppermute x129, waiting for transfers between devices, swap(): lax.ppermute(value, self.names, [(i, i ^ delta) for i in range(self.size)])  386 us
    ppermute x129, starting transfers between devices, swap(): lax.ppermute(value, self.names, [(i, i ^ delta) for i in range(self.size)])  175 us
    dot_general x29, matrix products, dot(): return jnp.dot(left, right, preferred_element_type=F32)  172 us
    dynamic_update_slice x95, local copies, waits for them, and re-layouts, settle(): out = lax.dynamic_update_index_in_dim(out, piece, index ^ delta, dim)  75.7 us
    squeeze x22, local copies, waits for them, and re-layouts, pick(): return lax.dynamic_index_in_dim(stack, index, dim, keepdims=False)  30.9 us
    all_gather x1, waiting for transfers between devices, body(): second_col = lax.all_gather(second_low, Z, axis=0, tiled=True)  29.9 us
    unnamed x235, local copies, waits for them, and re-layouts  23.1 us
  transfers between devices with their start and end apart: 139, of which 50 were waited for; matrix products, arithmetic and copies ran while one was open for 41% of the time, Pallas kernels for 0%

commit v1 on v0

--- a/solution.py
+++ b/solution.py
@@ -36,6 +36,9 @@
         here = self.at()
         return self.give([pick(stack, here ^ delta, dim) for delta in range(self.size)])
 
+    def trade(self, blocks):
+        return lax.all_to_all(blocks, self.names, split_axis=0, concat_axis=0, tiled=True)
+
 
 def pick(stack, index, dim=0):
     return lax.dynamic_index_in_dim(stack, index, dim, keepdims=False)
@@ -50,6 +53,14 @@
     return out
 
 
+def in_order(first, mine, other):
+    return jnp.where(first, mine, other), jnp.where(first, other, mine)
+
+
+def after(value, *events):
+    return lax.optimization_barrier((value, *events))[0]
+
+
 def dot(left, right):
     return jnp.dot(left, right, preferred_element_type=F32)
 
@@ -80,8 +91,8 @@
 
 def make_body(mesh):
     line_z, line_k, line_t = Line(mesh, Z), Line(mesh, K), Line(mesh, C, D)
-    line_e = Line(mesh, Z, K)
-    columns, cores, blocks, owners = line_z.size, line_k.size, line_t.size, line_e.size
+    columns, cores, blocks = line_z.size, line_k.size, line_t.size
+    owners = columns * cores
 
     def body(
         tokens_in,
@@ -115,59 +126,53 @@
         rest = () if blocks == group else (D,)
         spot = line_s.at()
 
-        small = jnp.concatenate([w_router.T, gain_attn[None], gain_moe[None]], axis=0)
-        small = settle(line_t.share(small), blk)
-        small = settle(line_e.share(small), line_e.at())
-        small = small.transpose(2, 0, 1, 3).reshape(experts + 2, width)
+        first = core == 0
+        half = width // 2
+
+        def column_halves(value):
+            return in_order(first, value[..., :half], value[..., half:])
+
+        def side_by_side(mine, other):
+            return jnp.concatenate(in_order(first, mine, other), axis=-1)
+
+        def both_cores(mine, other):
+            return jnp.concatenate(in_order(first, mine, line_k.swap(other, 1)), axis=0)
+
+        def all_rows(whole):
+            if rest:
+                whole = lax.all_gather(whole, rest, axis=1, tiled=True)
+            return whole.reshape(-1, whole.shape[-1])
+
+        down_part = both_cores(*column_halves(expert_down))
+        in_part = both_cores(*in_order(first, expert_gate, expert_up))
+
+        small = jnp.concatenate([w_router, gain_attn[:, None], gain_moe[:, None]], axis=1)
+        small = jnp.pad(small, ((0, 0), (0, -small.shape[1] % 128)))
+        extra = small.shape[1]
+        mixed_in = jnp.concatenate(
+            [w.reshape(part, blocks, span) for w in (w_query, w_key, w_value)]
+            + [jnp.broadcast_to(small[:, None], (part, blocks, extra))],
+            axis=2,
+        ).transpose(1, 0, 2)
+        move = [(i, (i % owners) * blocks + i // owners) for i in range(owners * blocks)]
+        out_part = lax.ppermute(w_out, (Z, K, C, D), move)
+        out_part = out_part.reshape(part, blocks, span).transpose(1, 0, 2)
+        attn_part = settle(line_t.give_from(mixed_in), blk)
+        attn_part = jnp.concatenate([attn_part, out_part], axis=2).reshape(blocks * part, -1)
+        attn_mat = lax.all_gather(attn_part, (Z, K), axis=0, tiled=True)
+        dy_col = lax.all_gather(after(dy_low, attn_mat), Z, axis=0, tiled=True)
+
+        x_all = jnp.concatenate(line_t.share(x_low), axis=0).astype(F32)
+        down_got = line_s.trade(down_part)
+        in_got = line_s.trade(after(in_part, down_got))
+        attn_mat = after(attn_mat, down_got)
+        qkv = attn_mat[:, : 3 * span]
+        small = attn_mat[:, 3 * span : 3 * span + extra].T
         router_t = small[:experts]
         gain_first = small[experts].astype(F32)[None]
         gain_second = small[experts + 1].astype(F32)[None]
-
-        mixed_in = jnp.concatenate(
-            [w.reshape(part, blocks, span) for w in (w_query, w_key, w_value)], axis=2
-        ).transpose(1, 0, 2)
-        qkv = settle(line_t.give_from(mixed_in), blk).reshape(blocks * part, 3 * span)
-        qkv = lax.all_gather(qkv, (Z, K), axis=0, tiled=True)
-        move = [(i, (i % owners) * blocks + i // owners) for i in range(owners * blocks)]
-        out_mat = lax.ppermute(w_out, (Z, K, C, D), move)
-        out_mat = lax.all_gather(out_mat, (Z, K), axis=0, tiled=True)
-
-        x_all = jnp.concatenate(line_t.share(x_low), axis=0).astype(F32)
-        inputs = x_low.astype(F32)
-
-        def fetch(weight):
-            local, count, wide = weight.shape
-            halves = weight.reshape(local, cores, count // cores, wide)
-            other = line_k.swap(pick(halves, 1 - core, 1), 1)
-            both = settle([pick(halves, core, 1), other], core)
-            got = line_s.give_from(both.reshape(group, count // cores, wide))
-            pieces = []
-            for piece in got:
-                pieces += [piece, line_k.swap(piece, 1)]
-            whole = settle(pieces, spot * cores + core).reshape(line_s.size, count, wide)
-            if rest:
-                whole = lax.all_gather(whole, rest, axis=1, tiled=True)
-            return whole.reshape(-1, wide)
-
-        def fetch_shared(piece, dim):
-            got = line_t.share(piece)
-            pieces = got + [line_k.swap(one, 1) for one in got]
-            return settle(pieces, core * blocks + blk, dim)
-
-        hidden = shared_gate.shape[1] // columns
-        both_in = jnp.concatenate(
-            [w.reshape(part, columns, hidden) for w in (shared_gate, shared_up)], axis=2
-        ).transpose(1, 0, 2)
-        both_in = settle(line_z.give_from(both_in), col)
-
-        dy_col = lax.all_gather(dy_low, Z, axis=0, tiled=True)
-        routes_col = settle(line_z.share(routes[0]), col)
-
-        mat_down = fetch(expert_down)
-        mat_sdown = fetch_shared(shared_down, 0).reshape(hidden, width)
-        mat_gate = fetch(expert_gate)
-        mat_up = fetch(expert_up)
-        mat_sin = fetch_shared(both_in, 1).reshape(width, 2 * hidden)
+        out_mat = attn_mat[:, 3 * span + extra :].reshape(owners, blocks, part, span)
+        out_mat = out_mat.transpose(0, 2, 1, 3).reshape(owners * part, width)
 
         doc_row = doc_ids[0]
         order = blk ^ jnp.arange(blocks, dtype=jnp.int32)
@@ -191,6 +196,7 @@
         first_normed = x_all * first_scale
         normed_low = (first_normed * gain_first).astype(LOW)
         made = dot(normed_low, qkv)
+        routes_col = settle(line_z.share(after(routes[0], made)), col)
 
         def per_head(values):
             return values.reshape(length, heads, HD)
@@ -210,12 +216,24 @@
             .reshape(length, span)
         )
         attn_out = dot(mixed_low, out_mat).astype(LOW).reshape(blocks, rows, width)
+        in_got = after(in_got, attn_out)
+        inputs = after(x_low, in_got).astype(F32)
         after_attn = inputs + total(line_t.give([attn_out[i] for i in range(blocks)]))
 
         second_scale = lax.rsqrt(jnp.mean(after_attn * after_attn, axis=1, keepdims=True) + EPS)
         second_normed = after_attn * second_scale
         second_low = (second_normed * gain_second).astype(LOW)
         second_col = lax.all_gather(second_low, Z, axis=0, tiled=True)
+        hidden = shared_gate.shape[1] // columns
+        shared_in = jnp.concatenate(
+            [w.reshape(part, columns, hidden).transpose(1, 0, 2) for w in (shared_gate, shared_up)],
+            axis=2,
+        )
+        shared_in = line_z.trade(after(shared_in, second_low))
+        mat_down = all_rows(after(down_got, second_low))
+        mat_down = side_by_side(mat_down, line_k.swap(mat_down, 1))
+        mat_mine = all_rows(after(in_got, second_low))
+        mat_other = line_k.swap(mat_mine, 1)
 
         def router(values):
             return jax.nn.softmax(dot(values, router_t.T), axis=1)
@@ -242,7 +260,7 @@
         def collect(values):
             parts = values.reshape(group, slots, width)
             back = line_s.give([parts[i] for i in range(group)])
-            return dot(spread.T, jnp.concatenate(back, axis=0))
+            return jnp.concatenate(back, axis=0)
 
         dy_slots = dispatch(dy_col)
         du_raw = dot(dy_slots, mat_down.T)
@@ -256,28 +274,39 @@
         gate = jnp.concatenate(line_s.give([gate_sent[i] for i in range(group)]), axis=1)
         gate = gate.reshape(group * slots, 1)
 
-        second_slots = dispatch(second_col)
-        pre_gate = dot(second_slots, mat_gate)
-        pre_up = dot(second_slots, mat_up)
+        second_slots = after(dispatch(after(second_col, dy_slots)), du_raw)
+        made_mine, made_other = dot(second_slots, mat_mine), dot(second_slots, mat_other)
+        pre_gate = jnp.where(first, made_mine, made_other)
+        pre_up = jnp.where(first, made_other, made_mine)
         sigma = jax.nn.sigmoid(pre_gate)
         hidden_low = (pre_gate * sigma * pre_up).astype(LOW)
         dgate = jnp.sum(hidden_low.astype(F32) * du_raw, axis=1)
         du = du_raw * gate
         grad_a = (du * pre_up * swish_slope(pre_gate, sigma)).astype(LOW)
         grad_b = (du * pre_gate * sigma).astype(LOW)
-        grad_slots = (dot(grad_a, mat_gate.T) + dot(grad_b, mat_up.T)).astype(LOW)
-
-        shared_pre = dot(second_col, mat_sin)
+        grad_mine = jnp.where(first, grad_a, grad_b)
+        grad_other = jnp.where(first, grad_b, grad_a)
+        grad_slots = (dot(grad_mine, mat_mine.T) + dot(grad_other, mat_other.T)).astype(LOW)
+
+        mat_sin, mat_sdown = after((shared_in, shared_down), second_slots)
+        mat_sin = lax.all_gather(mat_sin, (K, C, D), axis=1, tiled=True)
+        mat_sin = mat_sin.reshape(width, 2 * hidden)
+        mat_sdown = lax.all_gather(mat_sdown, (K, C, D), axis=0, tiled=True)
+        second_late, dy_late = after((second_col, dy_col), grad_slots)
+        shared_pre = dot(second_late, mat_sin)
         shared_a, shared_b = shared_pre[:, :hidden], shared_pre[:, hidden:]
         shared_sigma = jax.nn.sigmoid(shared_a)
         shared_low = (shared_a * shared_sigma * shared_b).astype(LOW)
-        dsu = dot(dy_col, mat_sdown.T)
+        dsu = dot(dy_late, mat_sdown.T)
         dsa = (dsu * shared_b * swish_slope(shared_a, shared_sigma)).astype(LOW)
         dsb = (dsu * shared_a * shared_sigma).astype(LOW)
         dsab = jnp.concatenate([dsa, dsb], axis=1)
 
-        grad_second = (dot(dsab, mat_sin.T) + collect(grad_slots)).astype(LOW)
-        grad_second = lax.psum_scatter(grad_second, Z, scatter_dimension=0, tiled=True)
+        grad_routed = dot(spread.T, after(collect(grad_slots), dsab))
+        grad_second = dot(dsab, mat_sin.T) + grad_routed
+        grad_second = lax.psum_scatter(
+            grad_second.astype(LOW), Z, scatter_dimension=0, tiled=True
+        )
 
         dgate_parts = dgate.reshape(group, 1, slots)
         dgate_back = line_s.give([dgate_parts[i] for i in range(group)])
@@ -320,54 +349,70 @@
             grad_first, local_normed, first_scale[:rows], gain_first
         )
 
-        routed = (dot(hidden_low, mat_down) * gate).astype(LOW)
-        layer_out = (dot(shared_low, mat_sdown) + collect(routed)).astype(LOW)
-        layer_out = lax.psum_scatter(layer_out, Z, scatter_dimension=0, tiled=True)
+        routed = (dot(after(hidden_low, grad_slots), mat_down) * gate).astype(LOW)
+        layer_out = dot(shared_low, mat_sdown) + dot(spread.T, collect(after(routed, grad_routed)))
+        layer_out = lax.psum_scatter(layer_out.astype(LOW), Z, scatter_dimension=0, tiled=True)
         layer_out = after_attn + layer_out.astype(F32)
 
-        def deliver(grad, local, count):
-            wide = grad.shape[1]
-            grad = grad.astype(LOW).reshape(line_s.size, -1, wide)
+        def send_home(mine, other):
+            mine = total([mine, line_k.swap(other, 1)]).astype(LOW)
+            mine = mine.reshape(line_s.size, -1, mine.shape[-1])
             if rest:
-                grad = lax.psum_scatter(grad, rest, scatter_dimension=1, tiled=True)
-            grad = grad.reshape(line_s.size, cores, count // cores, wide)
-            mine = total([pick(grad, core, 1), line_k.swap(pick(grad, 1 - core, 1), 1)])
-            got = settle(line_s.give_from(mine.astype(LOW)), spot)
-            got = got.reshape(cores, local, count // cores, wide)
-            other = line_k.swap(pick(got, 1 - core), 1)
-            return settle([pick(got, core), other], core, 1).reshape(local, count, wide).astype(F32)
+                mine = lax.psum_scatter(mine, rest, scatter_dimension=1, tiled=True)
+            return line_s.trade(mine)
+
+        def home(got):
+            got = got.reshape(cores, -1, *got.shape[1:])
+            kept, other = in_order(first, got[0], got[1])
+            return kept, line_k.swap(other, 1)
 
         weighted = (hidden_low.astype(F32) * gate).astype(LOW)
-        grad_edown = deliver(dot(weighted.T, dy_slots), *expert_down.shape[:2])
-        grad_egate = deliver(dot(second_slots.T, grad_a), *expert_gate.shape[:2])
-        grad_eup = deliver(dot(second_slots.T, grad_b), *expert_up.shape[:2])
-
-        def deliver_shared(grad):
-            lead, _, count, wide = grad.shape
-            grad = grad.reshape(lead, cores, blocks, count, wide)
-            mine = total([pick(grad, core, 1), line_k.swap(pick(grad, 1 - core, 1), 1)])
-            return total(line_t.give_from(mine.astype(LOW), 1))
-
-        grad_sdown = dot(shared_low.T, dy_col).astype(LOW)
-        grad_sdown = deliver_shared(grad_sdown.reshape(1, cores * blocks, -1, width))[0]
-        grad_sin = dot(second_col.T, dsab).astype(LOW)
-        grad_sin = deliver_shared(grad_sin.reshape(columns, cores * blocks, part, 2 * hidden))
-        grad_sin = settle(line_z.give_from(grad_sin.astype(LOW)), col).transpose(1, 0, 2)
-        grad_sgate = grad_sin[:, :, :hidden].reshape(part, -1).astype(F32)
-        grad_sup = grad_sin[:, :, hidden:].reshape(part, -1).astype(F32)
+        grad_down = dot(after(weighted, grad_slots).T, dy_slots).astype(LOW)
+        down_back = send_home(*column_halves(grad_down))
+        slots_late = after(second_slots, grad_slots)
+        in_back = send_home(
+            dot(slots_late.T, grad_mine).astype(LOW), dot(slots_late.T, grad_other).astype(LOW)
+        )
+
+        def shared_home(grad):
+            lead, count, wide = grad.shape
+            count = count // (cores * blocks)
+            grad = grad.astype(LOW).reshape(lead, cores, blocks * count, wide)
+            mine, other = in_order(first, grad[:, 0], grad[:, 1])
+            mine = total([mine, line_k.swap(other, 1)]).astype(LOW)
+            return line_t.trade(mine.reshape(lead, blocks, count, wide).transpose(1, 0, 2, 3))
+
+        sdown_back = shared_home(dot(shared_low.T, dy_late)[None])
+        sin_back = shared_home(
+            dot(second_late.T, dsab).reshape(columns, cores * blocks * part, 2 * hidden)
+        )
+
+        down_back, in_back, sdown_back, sin_back = after(
+            (down_back, in_back, sdown_back, sin_back), grad_made
+        )
+        grad_edown = side_by_side(*home(down_back)).astype(F32)
+        kept, came = home(in_back)
+        grad_egate = jnp.where(first, kept, came).astype(F32)
+        grad_eup = jnp.where(first, came, kept).astype(F32)
+        grad_sdown = total([sdown_back[i, 0] for i in range(blocks)])
+        grad_sin = total([sin_back[i] for i in range(blocks)]).astype(LOW)
+        grad_sin = line_z.trade(grad_sin).transpose(1, 0, 2).astype(F32)
+        grad_sgate = grad_sin[:, :, :hidden].reshape(part, -1)
+        grad_sup = grad_sin[:, :, hidden:].reshape(part, -1)
 
         grad_outmat = lax.psum_scatter(grad_outmat, (Z, K), scatter_dimension=0, tiled=True)
         back = [(there, here) for here, there in move]
         grad_outmat = lax.ppermute(grad_outmat, (Z, K, C, D), back).astype(F32)
         grad_qkv = lax.psum_scatter(grad_qkv, (Z, K), scatter_dimension=0, tiled=True)
-        grad_qkv = settle(line_t.give_from(grad_qkv.reshape(blocks, part, 3 * span)), blk)
+        grad_qkv = line_t.trade(grad_qkv.reshape(blocks, part, 3 * span))
         grad_qkv = grad_qkv.reshape(blocks, part, 3, span).transpose(2, 1, 0, 3)
         grad_qkv = grad_qkv.reshape(3, part, width).astype(F32)
 
         sums = jnp.concatenate([grad_router_t, grad_gain_first, grad_gain_second], axis=0)
-        sums = sums.reshape(experts + 2, owners, blocks, part).transpose(2, 1, 0, 3)
+        sums = sums.reshape(experts + 2, columns, cores, blocks, part).transpose(3, 2, 1, 0, 4)
         sums = total(line_t.give_from(sums))
-        sums = total(line_e.give_from(sums))
+        sums = total(line_k.give_from(sums))
+        sums = total(line_z.give_from(sums))
 
         return (
             layer_out[None],

time: 1100 us -> 836 us (0.76)
  local copies, waits for them, and re-layouts: 205 us -> 61 us
  waiting for transfers between devices: 416 us -> 326 us
  starting transfers between devices: 181 us -> 111 us
  other arithmetic: 78.9 us -> 111 us
    ppermute x129 -> x56, waiting for transfers between devices: 386 us -> 143 us  [swap(): lax.ppermute(value, self.names, [(i, i ^ delta) for i in range(self.size)])]
    all_to_all x0 -> x9, waiting for transfers between devices: none -> 129 us  [trade(): lax.all_to_all(blocks, self.names, split_axis=0, concat_axis=0, tiled=True)]
    ppermute x129 -> x56, starting transfers between devices: 175 us -> 60.1 us  [swap(): lax.ppermute(value, self.names, [(i, i ^ delta) for i in range(self.size)])]
    dynamic_update_slice x95 -> x17, local copies, waits for them, and re-layouts: 75.7 us -> 0.27 us  [settle(): out = lax.dynamic_update_index_in_dim(out, piece, index ^ delta, dim)]
    all_to_all x0 -> x9, starting transfers between devices: none -> 45.4 us  [trade(): lax.all_to_all(blocks, self.names, split_axis=0, concat_axis=0, tiled=True)]
    squeeze x22 -> x4, local copies, waits for them, and re-layouts: 30.9 us -> 1.01 us  [pick(): return lax.dynamic_index_in_dim(stack, index, dim, keepdims=False)]
    select_n x0 -> x11, other arithmetic: none -> 28.7 us  [in_order(): return (jnp.where(first, mine, other), jnp.where(first, other, mine))]
    all_gather x3 -> x4, waiting for transfers between devices: 0.02 us -> 20 us  [the longest x1 19.9 us: body(): attn_mat = lax.all_gather(attn_part, (Z, K), axis=0, tiled=True)]
  transfers between devices with their start and end apart: 139 -> 76, of which waited for: 50 -> 35; matrix products, arithmetic and copies ran while one was open for 41% -> 42% of each run, Pallas kernels for 0% -> 0%
where the time goes in v1:
time: 836 us; the launch traced here: 826 us
  waiting for transfers between devices  326 us (39%)
  matrix products  195 us (23%)
  starting transfers between devices  111 us (13%)
  other arithmetic  111 us (13%)
  local copies, waits for them, and re-layouts  61 us (7%)
  between operations  23.5 us (3%)
    dot_general x29, matrix products, dot(): return jnp.dot(left, right, preferred_element_type=F32)  179 us
    ppermute x56, waiting for transfers between devices, swap(): lax.ppermute(value, self.names, [(i, i ^ delta) for i in range(self.size)])  143 us
    all_to_all x9, waiting for transfers between devices, trade(): lax.all_to_all(blocks, self.names, split_axis=0, concat_axis=0, tiled=True)  129 us
    ppermute x56, starting transfers between devices, swap(): lax.ppermute(value, self.names, [(i, i ^ delta) for i in range(self.size)])  60.1 us
    all_to_all x9, starting transfers between devices, trade(): lax.all_to_all(blocks, self.names, split_axis=0, concat_axis=0, tiled=True)  45.4 us
    all_gather x1, waiting for transfers between devices, body(): second_col = lax.all_gather(second_low, Z, axis=0, tiled=True)  34.4 us
    select_n x11, other arithmetic, in_order(): return (jnp.where(first, mine, other), jnp.where(first, other, mine))  28.7 us
    all_gather x1, waiting for transfers between devices, body(): attn_mat = lax.all_gather(attn_part, (Z, K), axis=0, tiled=True)  19.9 us
  transfers between devices with their start and end apart: 76, of which 35 were waited for; matrix products, arithmetic and copies ran while one was open for 42% of the time, Pallas kernels for 0%

profile of v1, /device:TPU:0, one launch (start us, length us, event | category | flops | bytes accessed | tf_op | source)
XLA Modules:
  0.0 826.4 jit_solution(5328327154820124336)
XLA Ops:
  15.4 3.4 collective-permute-start.5
  26.2 5.1 collective-permute-done.7
  36.5 3.9 broadcast_select_fusion.11
  55.4 4.9 all-to-all-start
  69.6 24.8 %all-to-all-done = bf16[4,352,1024]{2,1,0:T(8,128)(2,1)} async-done(((bf16[4,352,1024]{2,1,0:T(8,128)(2,1)}), bf16[4,352,1024]{2,1,0:T(8,128)(2,1)}, u32[]{:S(2)}, u32[]{:S(2)}) %all-to-all-start) | async-done | bytes 2883616 | tf_op jit(solution)/shard_map/all_to_all | solution.py:40
  94.4 5.2 all-to-all-start.1
  100.1 19.9 %all-gather.6.cloned.1.call-done = bf16[2048,2176]{1,0:T(8,128)(2,1)} async-done(((bf16[256,2176]{1,0:T(8,128)(2,1)}), bf16[2048,2176]{1,0:T(8,128)(2,1)}) %all-gather.6.cloned.1.call-update) | async-done | bytes 8912912 | tf_op jit(solution)/shard_map/all_gather | solution.py:162
  121.9 6.7 fusion.6
  134.5 5.1 fusion.98
  153.4 21.3 %all-to-all-done.1 = bf16[4,512,1408]{2,1,0:T(8,128)(2,1)} async-done(((bf16[4,512,1408]{2,1,0:T(8,128)(2,1)}), bf16[4,512,1408]{2,1,0:T(8,128)(2,1)}, u32[]{:S(2)}, u32[]{:S(2)}) %all-to-all-start.1) | async-done | bytes 5767200 | tf_op jit(solution)/shard_map/all_to_all | solution.py:40
  177.4 8.9 %collective-permute-done.10 = bf16[128,2048]{1,0:T(8,128)(2,1)S(1)} collective-permute-done((bf16[128,2048]{1,0:T(8,128)(2,1)}, bf16[128,2048]{1,0:T(8,128)(2,1)S(1)}, u32[]{:S(2)}, u32[]{:S(2)}) %collective-permute-start.10) | collective-permute-done | bytes 524320 | tf_op jit(solution)/shard_map/ppermute | solution.py:27
  197.9 3.8 collective-permute-done.14
  204.8 3.5 all-to-all-start.2
  208.5 3.9 convolution_convert_fusion.6
  217.7 5.5 broadcast_select_fusion.2
  223.3 34.4 %all-gather.8.cloned.1.call-done = bf16[512,2048]{1,0:T(8,128)(2,1)} async-done(((bf16[128,2048]{1,0:T(8,128)(2,1)}), bf16[512,2048]{1,0:T(8,128)(2,1)}) %all-gather.8.cloned.1.call-update) | async-done | bytes 2097168 | tf_op jit(solution)/shard_map/all_gather | solution.py:226
  257.7 3.9 convolution_convert_fusion.5
  265.7 11.1 %fusion.17 = f32[1024,1408]{1,0:T(8,128)} fusion(bf16[1408,1024]{1,0:T(8,128)(2,1)S(1)} %copy-done.23, bf16[1408,1024]{1,0:T(8,128)(2,1)S(1)} %copy-done.22, bf16[256,2048]{1,0:T(8,128)(2,1)} %collective-permute-done.17, bf16[256,2048]{1,0:T(8,128)(2,1)} %collective-permute-done.16, bf16[256,2048]{1,0:T(8,128)(2,1)} %collective-permute-done.15, ...), kind=kOutput, calls=%fused_computation.49 | convolution fusion | flops 5933891584 | bytes 15728640 | tf_op jit(solution)/shard_map/dot_general | solution.py:65
  276.8 12.4 %collective-permute-done.24 = bf16[256,2048]{1,0:T(8,128)(2,1)S(1)} collective-permute-done((bf16[256,2048]{1,0:T(8,128)(2,1)S(1)}, bf16[256,2048]{1,0:T(8,128)(2,1)S(1)}, u32[]{:S(2)}, u32[]{:S(2)}) %collective-permute-start.24) | collective-permute-done | bytes 1048608 | tf_op jit(solution)/shard_map/ppermute | solution.py:27
  289.2 21.3 %collective-permute-done.23 = bf16[256,2048]{1,0:T(8,128)(2,1)S(1)} collective-permute-done((bf16[256,2048]{1,0:T(8,128)(2,1)S(1)}, bf16[256,2048]{1,0:T(8,128)(2,1)S(1)}, u32[]{:S(2)}, u32[]{:S(2)}) %collective-permute-start.23) | collective-permute-done | bytes 1048608 | tf_op jit(solution)/shard_map/ppermute | solution.py:27
  310.5 3.3 pad_maximum_fusion.3
  318.6 10.9 %fusion.101 = f32[1024,1408]{1,0:T(8,128)S(1)} fusion(bf16[1024,2048]{1,0:T(8,128)(2,1)} %pad_maximum_fusion.3, bf16[2048,1408]{1,0:T(8,128)(2,1)} %bitcast.39), kind=kOutput, calls=%fused_computation.301 | convolution fusion | flops 5905580032 | bytes 15728640 | tf_op jit(solution)/shard_map/dot_general | solution.py:65
  329.5 15.6 %fusion.1 = (f32[1024]{0:T(1024)S(1)}, bf16[1024,1408]{1,0:T(8,128)(2,1)}, f32[1024,1408]{1,0:T(8,128)}, f32[1024,1408]{1,0:T(8,128)}) fusion(f32[1024,1408]{1,0:T(8,128)S(1)} %bitcast.287, f32[1024,1408]{1,0:T(8,128)S(1)} %fusion.101, pred[]{:T(512)S(6)} %eq.85, bf16[1024,2048]{1,0:T(8,128)(2,1)S(1)} %copy-done.18, ...), kind=kOutput, calls=%fused_computation.11 | convolution fusion | flops 5921438720 | bytes 35917824 | tf_op jit(solution)/shard_map/dot_general | solution.py:65
  361.4 9.0 %multiply_convert_fusion.2 = (bf16[1024,1408]{1,0:T(8,128)(2,1)S(1)}, bf16[1024,1408]{1,0:T(8,128)(2,1)S(1)}, bf16[1024,1408]{1,0:T(8,128)(2,1)S(1)}) fusion(f32[1024,1408]{1,0:T(8,128)} %get-tuple-element.71, f32[1024,1408]{1,0:T(8,128)} %fusion.17, f32[1024]{0:T(1024)S(1)} %bitcast.331, f32[1024,1408]{1,0:T(8,128)} %get-tuple-element.183, ...), kind=kLoop, calls=%fused_computation.19 | loop fusion | flops 25952256 | bytes 34607104 | tf_op jit(solution)/shard_map/convert_element_type | solution.py:286
  370.4 12.9 %fusion.35 = f32[1024,2048]{1,0:T(8,128)} fusion(bf16[2048,1408]{1,0:T(8,128)(2,1)} %bitcast.39, bf16[1024,1408]{1,0:T(8,128)(2,1)S(1)} %get-tuple-element.75, bf16[1024,1408]{1,0:T(8,128)(2,1)S(1)} %get-tuple-element.74, pred[]{:T(512)S(6)} %eq.85), kind=kOutput, calls=%fused_computation.114 | convolution fusion | flops 5907021824 | bytes 19922944 | tf_op jit(solution)/shard_map/dot_general | solution.py:65
  383.3 10.8 %add_convert_fusion.1 = bf16[1024,2048]{1,0:T(8,128)(2,1)S(1)} fusion(f32[1024,2048]{1,0:T(8,128)} %fusion.35, bf16[2048,1408]{1,0:T(8,128)(2,1)} %collective-permute-done.25, bf16[1024,1408]{1,0:T(8,128)(2,1)S(1)} %get-tuple-element.74, bf16[1024,1408]{1,0:T(8,128)(2,1)S(1)} %get-tuple-element.75, pred[]{:T(512)S(6)} %eq.85), kind=kOutput, calls=%fused_computation.3 | convolution fusion | flops 5911216128 | bytes 24117248 | tf_op jit(solution)/shard_map/dot_general | solution.py:65
  399.4 8.0 convolution_convert_fusion.3
  407.4 8.9 %convolution_convert_fusion.1 = bf16[2048,1408]{1,0:T(8,128)(2,1)} fusion(bf16[1024,2048]{1,0:T(8,128)(2,1)S(1)} %copy-done.19, bf16[1024,1408]{1,0:T(8,128)(2,1)S(1)} %get-tuple-element.74, bf16[1024,1408]{1,0:T(8,128)(2,1)S(1)} %get-tuple-element.75, pred[]{:T(512)S(6)} %eq.85), kind=kOutput, calls=%fused_computation.5 | convolution fusion | flops 5909905408 | bytes 15728641 | tf_op jit(solution)/shard_map/dot_general | solution.py:65
  418.3 4.9 collective-permute-done.28
  425.6 15.2 %collective-permute-done.27 = bf16[256,2048]{1,0:T(8,128)(2,1)S(1)} collective-permute-done((bf16[256,2048]{1,0:T(8,128)(2,1)}, bf16[256,2048]{1,0:T(8,128)(2,1)S(1)}, u32[]{:S(2)}, u32[]{:S(2)}) %collective-permute-start.27) | collective-permute-done | bytes 1048608 | tf_op jit(solution)/shard_map/ppermute | solution.py:27
  443.5 3.5 copy.300
  449.6 5.1 fusion.102
  454.6 6.6 multiply_convert_fusion.7
  464.4 5.1 add_convert_fusion.3
  469.5 10.2 %multiply_convert_fusion = bf16[1024,2048]{1,0:T(8,128)(2,1)S(1)} fusion(bf16[1024,1408]{1,0:T(8,128)(2,1)} %get-tuple-element.51, f32[1024]{0:T(1024)S(1)} %bitcast.332, bf16[1408,1024]{1,0:T(8,128)(2,1)} %get-tuple-element.81, bf16[1408,1024]{1,0:T(8,128)(2,1)} %get-tuple-element.80), kind=kOutput, calls=%fused_computation.2 | convolution fusion | flops 5921308672 | bytes 12849152 | tf_op jit(solution)/shard_map/dot_general | solution.py:65
  485.1 5.6 add_convert_fusion.2
  490.7 4.7 all-to-all-start.4
  495.5 3.7 fusion.103
  499.2 9.6 %collective-permute-done.31 = bf16[256,2048]{1,0:T(8,128)(2,1)} collective-permute-done((bf16[256,2048]{1,0:T(8,128)(2,1)}, bf16[256,2048]{1,0:T(8,128)(2,1)}, u32[]{:S(2)}, u32[]{:S(2)}) %collective-permute-start.31) | collective-permute-done | bytes 1048608 | tf_op jit(solution)/shard_map/ppermute | solution.py:27
  508.8 22.1 %collective-permute-done.30 = bf16[256,2048]{1,0:T(8,128)(2,1)} collective-permute-done((bf16[256,2048]{1,0:T(8,128)(2,1)}, bf16[256,2048]{1,0:T(8,128)(2,1)}, u32[]{:S(2)}, u32[]{:S(2)}) %collective-permute-start.30) | collective-permute-done | bytes 1048608 | tf_op jit(solution)/shard_map/ppermute | solution.py:27
  531.3 6.0 add_convert_fusion.4
  537.4 12.2 %add_convert_fusion = bf16[2048,1408]{1,0:T(8,128)(2,1)} fusion(bf16[2048,1408]{1,0:T(8,128)(2,1)} %collective-permute-done.53, bf16[1024,2048]{1,0:T(8,128)(2,1)} %pad_maximum_fusion.3, bf16[1024,1408]{1,0:T(8,128)(2,1)} %copy-done.26, bf16[1024,1408]{1,0:T(8,128)(2,1)S(1)} %copy-done.25, pred[]{:T(512)S(6)} %eq.85), kind=kOutput, calls=%fused_computation.1 | convolution fusion | flops 5921439744 | bytes 21495808 | tf_op jit(solution)/shard_map/dot_general | solution.py:65
  549.7 5.3 convolution_convert_fusion
  562.6 10.8 %collective-permute-done.40 = bf16[128,2048]{1,0:T(8,128)(2,1)S(1)} collective-permute-done((bf16[128,2048]{1,0:T(8,128)(2,1)S(1)}, bf16[128,2048]{1,0:T(8,128)(2,1)S(1)}, u32[]{:S(2)}, u32[]{:S(2)}) %collective-permute-start.40) | collective-permute-done | bytes 524320 | tf_op jit(solution)/shard_map/ppermute | solution.py:27
  573.4 10.3 %collective-permute-done.39 = bf16[128,2048]{1,0:T(8,128)(2,1)S(1)} collective-permute-done((bf16[128,2048]{1,0:T(8,128)(2,1)S(1)}, bf16[128,2048]{1,0:T(8,128)(2,1)S(1)}, u32[]{:S(2)}, u32[]{:S(2)}) %collective-permute-start.39) | collective-permute-done | bytes 524320 | tf_op jit(solution)/shard_map/ppermute | solution.py:27
  587.9 3.3 convolution_convert_fusion.10
  599.8 5.2 all-to-all-start.5
  611.8 7.7 convolution_convert_fusion.4
  619.5 3.5 convolution_convert_fusion.7
  628.4 40.8 %all-to-all-done.5 = bf16[4,512,1408]{2,1,0:T(8,128)(2,1)} async-done(((bf16[4,512,1408]{2,1,0:T(8,128)(2,1)}), bf16[4,512,1408]{2,1,0:T(8,128)(2,1)}, u32[]{:S(2)}, u32[]{:S(2)}) %all-to-all-start.5) | async-done | bytes 5767200 | tf_op jit(solution)/shard_map/all_to_all | solution.py:40
  669.2 4.3 all-to-all-start.6
  673.5 4.7 fusion.3
  680.1 11.5 %all-to-all-done.6 = bf16[4,1,88,2048]{3,2,1,0:T(8,128)(2,1)} async-done(((bf16[4,1,88,2048]{3,2,1,0:T(8,128)(2,1)}), bf16[4,1,88,2048]{3,2,1,0:T(8,128)(2,1)}, u32[]{:S(2)}, u32[]{:S(2)}) %all-to-all-start.6) | async-done | bytes 1441824 | tf_op jit(solution)/shard_map/all_to_all | solution.py:40
  691.6 5.0 all-to-all-start.7
  696.6 3.8 convert_multiply_fusion.2
  701.6 6.8 fusion.21
  714.4 24.9 %all-to-all-done.7 = bf16[4,4,64,1408]{3,2,1,0:T(8,128)(2,1)} async-done(((bf16[4,4,64,1408]{3,2,1,0:T(8,128)(2,1)}), bf16[4,4,64,1408]{3,2,1,0:T(8,128)(2,1)}, u32[]{:S(2)}, u32[]{:S(2)}) %all-to-all-start.7) | async-done | bytes 2883616 | tf_op jit(solution)/shard_map/all_to_all | solution.py:40
  742.3 4.6 all-to-all-start.8
  747.0 4.6 broadcast_select_fusion.7
  769.1 3.9 collective-permute-start.50
  773.7 4.2 add_bitcast_fusion
  790.6 7.9 all-to-all-start.3
  798.5 8.7 %select_convert_fusion = (f32[2,512,1408]{2,1,0:T(8,128)}, f32[2,512,1408]{2,1,0:T(8,128)}) fusion(bf16[2,512,1408]{2,1,0:T(8,128)(2,1)} %collective-permute-done.56, pred[]{:T(512)S(6)} %eq.85, bf16[4,512,1408]{2,1,0:T(8,128)(2,1)} %all-to-all-done.5), kind=kLoop, calls=%fused_computation.61 | loop fusion | flops 7208960 | bytes 20185088 | tf_op jit(solution)/shard_map/convert_element_type | solution.py:396
  808.0 5.2 all-to-all-done.3
  (473 shorter events, 213.0 us)
Async XLA Ops:
  7.2 112.9 %all-gather.6.cloned.1.call-start = ((), (), s32[]{:S(2)}) async-start(), calls=%async_computation.13 | async-start | bytes 10027008 | tf_op jit(solution)/shard_map/all_gather | solution.py:162
  7.2 24.1 %collective-permute-start.8 = (bf16[64,2048]{1,0:T(8,128)(2,1)}, bf16[64,2048]{1,0:T(8,128)(2,1)S(1)}, u32[]{:S(2)}, u32[]{:S(2)}) collective-permute-start(bf16[64,2048]{1,0:T(8,128)(2,1)} %param.24), channel_id=1, source_target_pairs={{0,0},{1,4},{2,8},{3,12},{4,16},{5,20},{6,24},{7,28},{8,1},{9,5},{... | collective-permute-start | bytes 786440 | tf_op jit(solution)/shard_map/ppermute | solution.py:158
  15.4 10.0 %collective-permute-start.5 = (bf16[64,1664]{1,0:T(8,128)(2,1)S(1)}, bf16[64,1664]{1,0:T(8,128)(2,1)S(1)}, u32[]{:S(2)}, u32[]{:S(2)}) collective-permute-start(bf16[64,1664]{1,0:T(8,128)(2,1)S(1)} %bitcast.326), channel_id=1, source_target_pairs={{0,1},{1,0},{2,3},{3,2},{4,5},{5,4},{6,7},{7,6},{8,9},{9,8},{10,11... | collective-permute-start | bytes 638984 | tf_op jit(solution)/shard_map/ppermute | solution.py:27
  18.8 7.4 collective-permute-start.6
  21.3 10.0 %collective-permute-start.7 = (bf16[64,1664]{1,0:T(8,128)(2,1)S(1)}, bf16[64,1664]{1,0:T(8,128)(2,1)S(1)}, u32[]{:S(2)}, u32[]{:S(2)}) collective-permute-start(bf16[64,1664]{1,0:T(8,128)(2,1)S(1)} %bitcast.324), channel_id=1, source_target_pairs={{0,3},{1,2},{2,1},{3,0},{4,7},{5,6},{6,5},{7,4},{8,11},{9,10},{10,... | collective-permute-start | bytes 638984 | tf_op jit(solution)/shard_map/ppermute | solution.py:27
  32.7 29.5 %collective-permute-start.4 = (bf16[128,2048]{1,0:T(8,128)(2,1)S(1)}, bf16[128,2048]{1,0:T(8,128)(2,1)}, u32[]{:S(2)}, u32[]{:S(2)}) collective-permute-start(bf16[128,2048]{1,0:T(8,128)(2,1)S(1)} %bitcast.294), channel_id=1, source_target_pairs={{0,3},{1,2},{2,1},{3,0},{4,7},{5,6},{6,5},{7,4},{8,11},{9,10},{10,... | collective-permute-start | bytes 1572872 | tf_op jit(solution)/shard_map/ppermute | solution.py:27
  35.4 26.7 %collective-permute-start.3 = (bf16[128,2048]{1,0:T(8,128)(2,1)S(1)}, bf16[128,2048]{1,0:T(8,128)(2,1)}, u32[]{:S(2)}, u32[]{:S(2)}) collective-permute-start(bf16[128,2048]{1,0:T(8,128)(2,1)S(1)} %bitcast.295), channel_id=1, source_target_pairs={{0,2},{1,3},{2,0},{3,1},{4,6},{5,7},{6,4},{7,5},{8,10},{9,11},{10,... | collective-permute-start | bytes 1572872 | tf_op jit(solution)/shard_map/ppermute | solution.py:27
  35.4 26.7 %collective-permute-start.2 = (bf16[128,2048]{1,0:T(8,128)(2,1)S(1)}, bf16[128,2048]{1,0:T(8,128)(2,1)}, u32[]{:S(2)}, u32[]{:S(2)}) collective-permute-start(bf16[128,2048]{1,0:T(8,128)(2,1)S(1)} %bitcast.296), channel_id=1, source_target_pairs={{0,1},{1,0},{2,3},{3,2},{4,5},{5,4},{6,7},{7,6},{8,9},{9,8},{10,11... | collective-permute-start | bytes 1572872 | tf_op jit(solution)/shard_map/ppermute | solution.py:27
  40.4 23.6 %collective-permute-start = (bf16[2,512,1408]{2,1,0:T(8,128)(2,1)}, bf16[2,512,1408]{2,1,0:T(8,128)(2,1)}, u32[]{:S(2)}, u32[]{:S(2)}) collective-permute-start(bf16[2,512,1408]{2,1,0:T(8,128)(2,1)} %broadcast_select_fusion.11), channel_id=1, source_target_pairs={{0,4},{4,0},{1,5},{5,1},{2,6},{6,2},{3,7},{7,3},{8,12},{12,8},{9,1... | collective-permute-start | bytes 8650760 | tf_op jit(solution)/shard_map/ppermute | solution.py:27
  41.8 10.1 %collective-permute-start.1 = (bf16[2,352,1024]{2,1,0:T(8,128)(2,1)}, bf16[2,352,1024]{2,1,0:T(8,128)(2,1)}, u32[]{:S(2)}, u32[]{:S(2)}) collective-permute-start(bf16[2,352,1024]{2,1,0:T(8,128)(2,1)} %broadcast_select_fusion.19), channel_id=1, source_target_pairs={{0,4},{4,0},{1,5},{5,1},{2,6},{6,2},{3,7},{7,3},{8,12},{12,8},{9,1... | collective-permute-start | bytes 4325384 | tf_op jit(solution)/shard_map/ppermute | solution.py:27
  55.4 39.0 %all-to-all-start = ((bf16[4,352,1024]{2,1,0:T(8,128)(2,1)}), bf16[4,352,1024]{2,1,0:T(8,128)(2,1)}, u32[]{:S(2)}, u32[]{:S(2)}) async-start(bf16[4,352,1024]{2,1,0:T(8,128)(2,1)} %pad_maximum_fusion.7), calls=%async_computation | async-start | bytes 5767168 | tf_op jit(solution)/shard_map/all_to_all | solution.py:40
  94.4 80.3 %all-to-all-start.1 = ((bf16[4,512,1408]{2,1,0:T(8,128)(2,1)}), bf16[4,512,1408]{2,1,0:T(8,128)(2,1)}, u32[]{:S(2)}, u32[]{:S(2)}) async-start(bf16[4,512,1408]{2,1,0:T(8,128)(2,1)} %pad_maximum_fusion), calls=%async_computation.1 | async-start | bytes 11534336 | tf_op jit(solution)/shard_map/all_to_all | solution.py:40
  99.6 108.9 %all-gather.10.cloned.1.call-start = ((), (), s32[]{:S(2)}) async-start(), calls=%async_computation.15 | async-start | bytes 2621440 | tf_op jit(solution)/shard_map/all_gather | solution.py:163
  132.6 125.0 %all-gather.8.cloned.1.call-start = ((), (), s32[]{:S(2)}) async-start(), calls=%async_computation.14 | async-start | bytes 2621440 | tf_op jit(solution)/shard_map/all_gather | solution.py:226
  149.9 27.5 %collective-permute-start.11 = (bf16[128,2048]{1,0:T(8,128)(2,1)}, bf16[128,2048]{1,0:T(8,128)(2,1)S(1)}, u32[]{:S(2)}, u32[]{:S(2)}) collective-permute-start(bf16[128,2048]{1,0:T(8,128)(2,1)} %get-tuple-element.118), channel_id=1, source_target_pairs={{0,3},{1,2},{2,1},{3,0},{4,7},{5,6},{6,5},{7,4},{8,11},{9,10},{10,... | collective-permute-start | bytes 1572872 | tf_op jit(solution)/shard_map/ppermute | solution.py:27
  152.4 33.9 %collective-permute-start.10 = (bf16[128,2048]{1,0:T(8,128)(2,1)}, bf16[128,2048]{1,0:T(8,128)(2,1)S(1)}, u32[]{:S(2)}, u32[]{:S(2)}) collective-permute-start(bf16[128,2048]{1,0:T(8,128)(2,1)} %get-tuple-element.119), channel_id=1, source_target_pairs={{0,2},{1,3},{2,0},{3,1},{4,6},{5,7},{6,4},{7,5},{8,10},{9,11},{10,... | collective-permute-start | bytes 1572872 | tf_op jit(solution)/shard_map/ppermute | solution.py:27
  152.9 33.3 %collective-permute-start.9 = (bf16[128,2048]{1,0:T(8,128)(2,1)}, bf16[128,2048]{1,0:T(8,128)(2,1)S(1)}, u32[]{:S(2)}, u32[]{:S(2)}) collective-permute-start(bf16[128,2048]{1,0:T(8,128)(2,1)} %get-tuple-element.117), channel_id=1, source_target_pairs={{0,1},{1,0},{2,3},{3,2},{4,5},{5,4},{6,7},{7,6},{8,9},{9,8},{10,11... | collective-permute-start | bytes 1572872 | tf_op jit(solution)/shard_map/ppermute | solution.py:27
  189.7 28.0 %collective-permute-start.18 = (bf16[1408,1024]{1,0:T(8,128)(2,1)}, bf16[1408,1024]{1,0:T(8,128)(2,1)}, u32[]{:S(2)}, u32[]{:S(2)}) collective-permute-start(bf16[1408,1024]{1,0:T(8,128)(2,1)} %bitcast.37), channel_id=1, source_target_pairs={{0,4},{4,0},{1,5},{5,1},{2,6},{6,2},{3,7},{7,3},{8,12},{12,8},{9,1... | collective-permute-start | bytes 8650760 | tf_op jit(solution)/shard_map/ppermute | solution.py:27
  191.2 5.1 collective-permute-start.12
  196.3 5.4 collective-permute-start.14
  204.8 109.1 %all-to-all-start.2 = ((bf16[4,64,1408]{2,1,0:T(8,128)(2,1)}), bf16[4,64,1408]{2,1,0:T(8,128)(2,1)S(1)}, u32[]{:S(2)}, u32[]{:S(2)}) async-start(bf16[4,64,1408]{2,1,0:T(8,128)(2,1)} %copy.298), calls=%async_computation.2 | async-start | bytes 1441792 | tf_op jit(solution)/shard_map/all_to_all | solution.py:40
  208.3 235.3 %all-gather.12.cloned.1.call-start = ((), (), s32[]{:S(2)}) async-start(), calls=%async_computation.16 | async-start | bytes 6488064 | tf_op jit(solution)/shard_map/all_gather | solution.py:292
  214.2 50.9 %collective-permute-start.17 = (bf16[256,2048]{1,0:T(8,128)(2,1)}, bf16[256,2048]{1,0:T(8,128)(2,1)}, u32[]{:S(2)}, u32[]{:S(2)}) collective-permute-start(bf16[256,2048]{1,0:T(8,128)(2,1)} %get-tuple-element.101), channel_id=1, source_target_pairs={{0,3},{1,2},{2,1},{3,0},{4,7},{5,6},{6,5},{7,4},{8,11},{9,10},{10,... | collective-permute-start | bytes 3145736 | tf_op jit(solution)/shard_map/ppermute | solution.py:27
  215.2 50.5 %collective-permute-start.16 = (bf16[256,2048]{1,0:T(8,128)(2,1)}, bf16[256,2048]{1,0:T(8,128)(2,1)}, u32[]{:S(2)}, u32[]{:S(2)}) collective-permute-start(bf16[256,2048]{1,0:T(8,128)(2,1)} %get-tuple-element.102), channel_id=1, source_target_pairs={{0,2},{1,3},{2,0},{3,1},{4,6},{5,7},{6,4},{7,5},{8,10},{9,11},{10,... | collective-permute-start | bytes 3145736 | tf_op jit(solution)/shard_map/ppermute | solution.py:27
  216.6 49.1 %collective-permute-start.15 = (bf16[256,2048]{1,0:T(8,128)(2,1)}, bf16[256,2048]{1,0:T(8,128)(2,1)}, u32[]{:S(2)}, u32[]{:S(2)}) collective-permute-start(bf16[256,2048]{1,0:T(8,128)(2,1)} %get-tuple-element.103), channel_id=1, source_target_pairs={{0,1},{1,0},{2,3},{3,2},{4,5},{5,4},{6,7},{7,6},{8,9},{9,8},{10,11... | collective-permute-start | bytes 3145736 | tf_op jit(solution)/shard_map/ppermute | solution.py:27
  262.1 27.1 %collective-permute-start.24 = (bf16[256,2048]{1,0:T(8,128)(2,1)S(1)}, bf16[256,2048]{1,0:T(8,128)(2,1)S(1)}, u32[]{:S(2)}, u32[]{:S(2)}) collective-permute-start(bf16[256,2048]{1,0:T(8,128)(2,1)S(1)} %get-tuple-element.97), channel_id=1, source_target_pairs={{0,3},{1,2},{2,1},{3,0},{4,7},{5,6},{6,5},{7,4},{8,11},{9,10},{10,... | collective-permute-start | bytes 3145736 | tf_op jit(solution)/shard_map/ppermute | solution.py:27
  264.6 45.8 %collective-permute-start.23 = (bf16[256,2048]{1,0:T(8,128)(2,1)S(1)}, bf16[256,2048]{1,0:T(8,128)(2,1)S(1)}, u32[]{:S(2)}, u32[]{:S(2)}) collective-permute-start(bf16[256,2048]{1,0:T(8,128)(2,1)S(1)} %get-tuple-element.98), channel_id=1, source_target_pairs={{0,2},{1,3},{2,0},{3,1},{4,6},{5,7},{6,4},{7,5},{8,10},{9,11},{10,... | collective-permute-start | bytes 3145736 | tf_op jit(solution)/shard_map/ppermute | solution.py:27
  265.1 45.4 %collective-permute-start.22 = (bf16[256,2048]{1,0:T(8,128)(2,1)S(1)}, bf16[256,2048]{1,0:T(8,128)(2,1)}, u32[]{:S(2)}, u32[]{:S(2)}) collective-permute-start(bf16[256,2048]{1,0:T(8,128)(2,1)S(1)} %get-tuple-element.99), channel_id=1, source_target_pairs={{0,1},{1,0},{2,3},{3,2},{4,5},{5,4},{6,7},{7,6},{8,9},{9,8},{10,11... | collective-permute-start | bytes 3145736 | tf_op jit(solution)/shard_map/ppermute | solution.py:27
  315.3 139.3 %all-gather.14.cloned.1.call-start = ((), (), s32[]{:S(2)}) async-start(), calls=%async_computation.17 | async-start | bytes 3244032 | tf_op jit(solution)/shard_map/all_gather | solution.py:294
  315.6 13.9 %collective-permute-start.25 = (bf16[2048,1408]{1,0:T(8,128)(2,1)}, bf16[2048,1408]{1,0:T(8,128)(2,1)}, u32[]{:S(2)}, u32[]{:S(2)}) collective-permute-start(bf16[2048,1408]{1,0:T(8,128)(2,1)} %bitcast.39), channel_id=1, source_target_pairs={{0,4},{4,0},{1,5},{5,1},{2,6},{6,2},{3,7},{7,3},{8,12},{12,8},{9,1... | collective-permute-start | bytes 17301512 | tf_op jit(solution)/shard_map/ppermute | solution.py:27
  348.8 206.2 %reduce-scatter.7.cloned.1.call-start = ((), (), s32[]{:S(2)}) async-start(), calls=%async_computation.19 | async-start | bytes 2621440 | tf_op jit(solution)/shard_map/reduce_scatter | solution.py:307
  353.1 126.6 %collective-permute-start.35 = (f32[4,128]{1,0:T(4,128)S(1)}, f32[4,128]{1,0:T(4,128)S(1)}, u32[]{:S(2)}, u32[]{:S(2)}) collective-permute-start(f32[4,128]{1,0:T(4,128)S(1)} %bitcast.344), channel_id=1, source_target_pairs={{0,8},{8,0},{16,24},{24,16},{1,9},{9,1},{17,25},{25,17},{2,10},{10... | collective-permute-start | bytes 6152 | tf_op jit(solution)/shard_map/ppermute | solution.py:27
  353.2 126.5 %collective-permute-start.36 = (f32[4,128]{1,0:T(4,128)S(1)}, f32[4,128]{1,0:T(4,128)S(1)}, u32[]{:S(2)}, u32[]{:S(2)}) collective-permute-start(f32[4,128]{1,0:T(4,128)S(1)} %bitcast.343), channel_id=1, source_target_pairs={{0,16},{8,24},{16,0},{24,8},{1,17},{9,25},{17,1},{25,9},{2,18},{10... | collective-permute-start | bytes 6152 | tf_op jit(solution)/shard_map/ppermute | solution.py:27
  395.9 27.2 %collective-permute-start.28 = (bf16[256,2048]{1,0:T(8,128)(2,1)}, bf16[256,2048]{1,0:T(8,128)(2,1)S(1)}, u32[]{:S(2)}, u32[]{:S(2)}) collective-permute-start(bf16[256,2048]{1,0:T(8,128)(2,1)} %get-tuple-element.93), channel_id=1, source_target_pairs={{0,3},{1,2},{2,1},{3,0},{4,7},{5,6},{6,5},{7,4},{8,11},{9,10},{10,... | collective-permute-start | bytes 3145736 | tf_op jit(solution)/shard_map/ppermute | solution.py:27
  397.1 43.7 %collective-permute-start.27 = (bf16[256,2048]{1,0:T(8,128)(2,1)}, bf16[256,2048]{1,0:T(8,128)(2,1)S(1)}, u32[]{:S(2)}, u32[]{:S(2)}) collective-permute-start(bf16[256,2048]{1,0:T(8,128)(2,1)} %get-tuple-element.94), channel_id=1, source_target_pairs={{0,2},{1,3},{2,0},{3,1},{4,6},{5,7},{6,4},{7,5},{8,10},{9,11},{10,... | collective-permute-start | bytes 3145736 | tf_op jit(solution)/shard_map/ppermute | solution.py:27
  398.0 43.3 %collective-permute-start.26 = (bf16[256,2048]{1,0:T(8,128)(2,1)S(1)}, bf16[256,2048]{1,0:T(8,128)(2,1)S(1)}, u32[]{:S(2)}, u32[]{:S(2)}) collective-permute-start(bf16[256,2048]{1,0:T(8,128)(2,1)S(1)} %get-tuple-element.95), channel_id=1, source_target_pairs={{0,1},{1,0},{2,3},{3,2},{4,5},{5,4},{6,7},{7,6},{8,9},{9,8},{10,11... | collective-permute-start | bytes 3145736 | tf_op jit(solution)/shard_map/ppermute | solution.py:27
  423.1 56.6 %collective-permute-start.37 = (f32[4,128]{1,0:T(4,128)S(1)}, f32[4,128]{1,0:T(4,128)S(1)}, u32[]{:S(2)}, u32[]{:S(2)}) collective-permute-start(f32[4,128]{1,0:T(4,128)S(1)} %bitcast.342), channel_id=1, source_target_pairs={{0,24},{8,16},{16,8},{24,0},{1,25},{9,17},{17,9},{25,1},{2,26},{10... | collective-permute-start | bytes 6152 | tf_op jit(solution)/shard_map/ppermute | solution.py:27
  440.8 44.3 %collective-permute-start.52 = (bf16[1408,1024]{1,0:T(8,128)(2,1)}, bf16[1408,1024]{1,0:T(8,128)(2,1)}, u32[]{:S(2)}, u32[]{:S(2)}) collective-permute-start(bf16[1408,1024]{1,0:T(8,128)(2,1)} %broadcast_select_fusion), channel_id=1, source_target_pairs={{0,4},{4,0},{1,5},{5,1},{2,6},{6,2},{3,7},{7,3},{8,12},{12,8},{9,1... | collective-permute-start | bytes 8650760 | tf_op jit(solution)/shard_map/ppermute | solution.py:27
  441.3 96.1 %collective-permute-start.53 = (bf16[2048,1408]{1,0:T(8,128)(2,1)}, bf16[2048,1408]{1,0:T(8,128)(2,1)}, u32[]{:S(2)}, u32[]{:S(2)}) collective-permute-start(bf16[2048,1408]{1,0:T(8,128)(2,1)} %convolution_convert_fusion.1), channel_id=1, source_target_pairs={{0,4},{4,0},{1,5},{5,1},{2,6},{6,2},{3,7},{7,3},{8,12},{12,8},{9,1... | collective-permute-start | bytes 17301512 | tf_op jit(solution)/shard_map/ppermute | solution.py:27
  481.6 27.2 %collective-permute-start.31 = (bf16[256,2048]{1,0:T(8,128)(2,1)}, bf16[256,2048]{1,0:T(8,128)(2,1)}, u32[]{:S(2)}, u32[]{:S(2)}) collective-permute-start(bf16[256,2048]{1,0:T(8,128)(2,1)} %get-tuple-element.89), channel_id=1, source_target_pairs={{0,3},{1,2},{2,1},{3,0},{4,7},{5,6},{6,5},{7,4},{8,11},{9,10},{10,... | collective-permute-start | bytes 3145736 | tf_op jit(solution)/shard_map/ppermute | solution.py:27
  483.6 47.3 %collective-permute-start.30 = (bf16[256,2048]{1,0:T(8,128)(2,1)}, bf16[256,2048]{1,0:T(8,128)(2,1)}, u32[]{:S(2)}, u32[]{:S(2)}) collective-permute-start(bf16[256,2048]{1,0:T(8,128)(2,1)} %get-tuple-element.90), channel_id=1, source_target_pairs={{0,2},{1,3},{2,0},{3,1},{4,6},{5,7},{6,4},{7,5},{8,10},{9,11},{10,... | collective-permute-start | bytes 3145736 | tf_op jit(solution)/shard_map/ppermute | solution.py:27
  484.1 47.2 %collective-permute-start.29 = (bf16[256,2048]{1,0:T(8,128)(2,1)S(1)}, bf16[256,2048]{1,0:T(8,128)(2,1)}, u32[]{:S(2)}, u32[]{:S(2)}) collective-permute-start(bf16[256,2048]{1,0:T(8,128)(2,1)S(1)} %get-tuple-element.91), channel_id=1, source_target_pairs={{0,1},{1,0},{2,3},{3,2},{4,5},{5,4},{6,7},{7,6},{8,9},{9,8},{10,11... | collective-permute-start | bytes 3145736 | tf_op jit(solution)/shard_map/ppermute | solution.py:27
  490.7 109.1 %all-to-all-start.4 = ((bf16[4,352,1024]{2,1,0:T(8,128)(2,1)}), bf16[4,352,1024]{2,1,0:T(8,128)(2,1)}, u32[]{:S(2)}, u32[]{:S(2)}) async-start(bf16[4,352,1024]{2,1,0:T(8,128)(2,1)} %bitcast.281), calls=%async_computation.8 | async-start | bytes 5767168 | tf_op jit(solution)/shard_map/all_to_all | solution.py:40
  495.4 278.3 %reduce-scatter.5.cloned.1.call-start = ((), (), s32[]{:S(2)}) async-start(), calls=%async_computation.18 | async-start | bytes 2621440 | tf_op jit(solution)/shard_map/reduce_scatter | solution.py:354
  537.3 251.6 %reduce-scatter.11.cloned.1.call-start = ((), (), s32[]{:S(2)}) async-start(), calls=%async_computation.21 | async-start | bytes 2359296 | tf_op jit(solution)/shard_map/reduce_scatter | solution.py:403
  557.1 16.3 %collective-permute-start.40 = (bf16[128,2048]{1,0:T(8,128)(2,1)S(1)}, bf16[128,2048]{1,0:T(8,128)(2,1)S(1)}, u32[]{:S(2)}, u32[]{:S(2)}) collective-permute-start(bf16[128,2048]{1,0:T(8,128)(2,1)S(1)} %fusion.83), channel_id=1, source_target_pairs={{0,3},{1,2},{2,1},{3,0},{4,7},{5,6},{6,5},{7,4},{8,11},{9,10},{10,... | collective-permute-start | bytes 1572872 | tf_op jit(solution)/shard_map/ppermute | solution.py:27
  559.2 24.5 %collective-permute-start.39 = (bf16[128,2048]{1,0:T(8,128)(2,1)S(1)}, bf16[128,2048]{1,0:T(8,128)(2,1)S(1)}, u32[]{:S(2)}, u32[]{:S(2)}) collective-permute-start(bf16[128,2048]{1,0:T(8,128)(2,1)S(1)} %fusion.83), channel_id=1, source_target_pairs={{0,2},{1,3},{2,0},{3,1},{4,6},{5,7},{6,4},{7,5},{8,10},{9,11},{10,... | collective-permute-start | bytes 1572872 | tf_op jit(solution)/shard_map/ppermute | solution.py:27
  559.7 24.3 %collective-permute-start.38 = (bf16[128,2048]{1,0:T(8,128)(2,1)S(1)}, bf16[128,2048]{1,0:T(8,128)(2,1)S(1)}, u32[]{:S(2)}, u32[]{:S(2)}) collective-permute-start(bf16[128,2048]{1,0:T(8,128)(2,1)S(1)} %fusion.83), channel_id=1, source_target_pairs={{0,1},{1,0},{2,3},{3,2},{4,5},{5,4},{6,7},{7,6},{8,9},{9,8},{10,11... | collective-permute-start | bytes 1572872 | tf_op jit(solution)/shard_map/ppermute | solution.py:27
  562.6 111.0 %collective-permute-start.55 = (bf16[4,256,1408]{2,1,0:T(8,128)(2,1)}, bf16[4,256,1408]{2,1,0:T(8,128)(2,1)}, u32[]{:S(2)}, u32[]{:S(2)}) collective-permute-start(bf16[4,256,1408]{2,1,0:T(8,128)(2,1)} %select_bitcast_fusion), channel_id=1, source_target_pairs={{0,4},{4,0},{1,5},{5,1},{2,6},{6,2},{3,7},{7,3},{8,12},{12,8},{9,1... | collective-permute-start | bytes 8650760 | tf_op jit(solution)/shard_map/ppermute | solution.py:27
  599.8 69.4 %all-to-all-start.5 = ((bf16[4,512,1408]{2,1,0:T(8,128)(2,1)}), bf16[4,512,1408]{2,1,0:T(8,128)(2,1)}, u32[]{:S(2)}, u32[]{:S(2)}) async-start(bf16[4,512,1408]{2,1,0:T(8,128)(2,1)} %bitcast.288), calls=%async_computation.9 | async-start | bytes 11534336 | tf_op jit(solution)/shard_map/all_to_all | solution.py:40
  605.0 185.6 %reduce-scatter.9.cloned.1.call-start = ((), (), s32[]{:S(2)}) async-start(), calls=%async_computation.20 | async-start | bytes 7077888 | tf_op jit(solution)/shard_map/reduce_scatter | solution.py:406
  669.2 22.4 %all-to-all-start.6 = ((bf16[4,1,88,2048]{3,2,1,0:T(8,128)(2,1)}), bf16[4,1,88,2048]{3,2,1,0:T(8,128)(2,1)}, u32[]{:S(2)}, u32[]{:S(2)}) async-start(bf16[4,1,88,2048]{3,2,1,0:T(8,128)(2,1)} %bitcast.293), calls=%async_computation.10 | async-start | bytes 2883584 | tf_op jit(solution)/shard_map/all_to_all | solution.py:40
  691.6 47.8 %all-to-all-start.7 = ((bf16[4,4,64,1408]{3,2,1,0:T(8,128)(2,1)}), bf16[4,4,64,1408]{3,2,1,0:T(8,128)(2,1)}, u32[]{:S(2)}, u32[]{:S(2)}) async-start(bf16[4,4,64,1408]{3,2,1,0:T(8,128)(2,1)} %copy.322), calls=%async_computation.11 | async-start | bytes 5767168 | tf_op jit(solution)/shard_map/all_to_all | solution.py:40
  710.9 43.0 %collective-permute-start.43 = (bf16[128,2048]{1,0:T(8,128)(2,1)}, bf16[128,2048]{1,0:T(8,128)(2,1)S(1)}, u32[]{:S(2)}, u32[]{:S(2)}) collective-permute-start(bf16[128,2048]{1,0:T(8,128)(2,1)} %get-tuple-element.115), channel_id=1, source_target_pairs={{0,3},{1,2},{2,1},{3,0},{4,7},{5,6},{6,5},{7,4},{8,11},{9,10},{10,... | collective-permute-start | bytes 1572872 | tf_op jit(solution)/shard_map/ppermute | solution.py:27
  713.8 40.1 %collective-permute-start.42 = (bf16[128,2048]{1,0:T(8,128)(2,1)}, bf16[128,2048]{1,0:T(8,128)(2,1)}, u32[]{:S(2)}, u32[]{:S(2)}) collective-permute-start(bf16[128,2048]{1,0:T(8,128)(2,1)} %get-tuple-element.116), channel_id=1, source_target_pairs={{0,2},{1,3},{2,0},{3,1},{4,6},{5,7},{6,4},{7,5},{8,10},{9,11},{10,... | collective-permute-start | bytes 1572872 | tf_op jit(solution)/shard_map/ppermute | solution.py:27
  714.4 39.5 %collective-permute-start.41 = (bf16[128,2048]{1,0:T(8,128)(2,1)}, bf16[128,2048]{1,0:T(8,128)(2,1)}, u32[]{:S(2)}, u32[]{:S(2)}) collective-permute-start(bf16[128,2048]{1,0:T(8,128)(2,1)} %get-tuple-element.114), channel_id=1, source_target_pairs={{0,1},{1,0},{2,3},{3,2},{4,5},{5,4},{6,7},{7,6},{8,9},{9,8},{10,11... | collective-permute-start | bytes 1572872 | tf_op jit(solution)/shard_map/ppermute | solution.py:27
  742.3 36.7 %all-to-all-start.8 = ((bf16[4,64,1408]{2,1,0:T(8,128)(2,1)}), bf16[4,64,1408]{2,1,0:T(8,128)(2,1)S(1)}, u32[]{:S(2)}, u32[]{:S(2)}) async-start(bf16[4,64,1408]{2,1,0:T(8,128)(2,1)} %fusion.38), calls=%async_computation.12 | async-start | bytes 1441792 | tf_op jit(solution)/shard_map/all_to_all | solution.py:40
  751.6 46.9 %collective-permute-start.56 = (bf16[2,512,1408]{2,1,0:T(8,128)(2,1)}, bf16[2,512,1408]{2,1,0:T(8,128)(2,1)}, u32[]{:S(2)}, u32[]{:S(2)}) collective-permute-start(bf16[2,512,1408]{2,1,0:T(8,128)(2,1)} %broadcast_select_fusion.7), channel_id=1, source_target_pairs={{0,4},{4,0},{1,5},{5,1},{2,6},{6,2},{3,7},{7,3},{8,12},{12,8},{9,1... | collective-permute-start | bytes 8650760 | tf_op jit(solution)/shard_map/ppermute | solution.py:27
  759.2 6.6 collective-permute-start.46
  759.2 6.7 collective-permute-start.45
  765.8 17.4 %collective-permute-start.57 = (bf16[2,352,1024]{2,1,0:T(8,128)(2,1)}, bf16[2,352,1024]{2,1,0:T(8,128)(2,1)}, u32[]{:S(2)}, u32[]{:S(2)}) collective-permute-start(bf16[2,352,1024]{2,1,0:T(8,128)(2,1)} %broadcast_select_fusion.15), channel_id=1, source_target_pairs={{0,4},{4,0},{1,5},{5,1},{2,6},{6,2},{3,7},{7,3},{8,12},{12,8},{9,1... | collective-permute-start | bytes 4325384 | tf_op jit(solution)/shard_map/ppermute | solution.py:27
  769.1 8.7 %collective-permute-start.50 = (f32[18,64]{1,0:T(8,128)S(1)}, f32[18,64]{1,0:T(8,128)S(1)}, u32[]{:S(2)}, u32[]{:S(2)}) collective-permute-start(f32[18,64]{1,0:T(8,128)S(1)} %bitcast.337), channel_id=1, source_target_pairs={{0,24},{8,16},{16,8},{24,0},{1,25},{9,17},{17,9},{25,1},{2,26},{10... | collective-permute-start | bytes 13832 | tf_op jit(solution)/shard_map/ppermute | solution.py:27
  789.0 18.2 %collective-permute-start.51 = (bf16[64,2048]{1,0:T(8,128)(2,1)}, bf16[64,2048]{1,0:T(8,128)(2,1)S(1)}, u32[]{:S(2)}, u32[]{:S(2)}) collective-permute-start(bf16[64,2048]{1,0:T(8,128)(2,1)} %reduce-scatter.11.cloned.1.call-done), channel_id=1, source_target_pairs={{0,0},{4,1},{8,2},{12,3},{16,4},{20,5},{24,6},{28,7},{1,8},{5,9},{... | collective-permute-start | bytes 786440 | tf_op jit(solution)/shard_map/ppermute | solution.py:405
  790.6 22.6 %all-to-all-start.3 = ((bf16[4,64,1536]{2,1,0:T(8,128)(2,1)}), bf16[4,64,1536]{2,1,0:T(8,128)(2,1)S(1)}, u32[]{:S(2)}, u32[]{:S(2)}) async-start(bf16[4,64,1536]{2,1,0:T(8,128)(2,1)} %bitcast.312), calls=%async_computation.6 | async-start | bytes 1572864 | tf_op jit(solution)/shard_map/all_to_all | solution.py:40
  (91 other events, 1000.6 us)
Sparse Core Ops, SparseCore 0:
  32.8 87.2 all-gather.5
  132.7 44.4 all-gather.9
  196.4 61.1 all-gather.7
  315.4 42.3 all-gather.11
  359.5 31.2 all-gather.13
  469.6 44.1 reduce-scatter.6
  537.4 44.1 reduce-scatter.4
  588.0 36.0 reduce-scatter.10
  626.4 68.2 reduce-scatter.8

commit v2 on v1

v2 whole, which is shorter than its diff:
```python
import math

import jax
import jax.numpy as jnp
from jax import lax
from jax.experimental import pallas as pl
from jax.experimental.pallas import tpu as pltpu
from jax.sharding import Mesh
from jax.sharding import PartitionSpec as P

HD = 128
TOP = 6
EPS = 1e-06
MASKED = -1e30
Z, K, C, D = "z", "core", "context", "dp"
F32 = jnp.float32
LOW = jnp.bfloat16


class Line:
    def __init__(self, mesh, *names):
        self.names = names
        self.size = math.prod(mesh.shape[name] for name in names)

    def at(self):
        return lax.axis_index(self.names)

    def swap(self, value, delta):
        return lax.ppermute(value, self.names, [(i, i ^ delta) for i in range(self.size)])

    def share(self, value):
        return [value] + [self.swap(value, delta) for delta in range(1, self.size)]

    def give(self, pieces):
        return [pieces[0]] + [self.swap(pieces[delta], delta) for delta in range(1, self.size)]

    def give_from(self, stack, dim=0):
        here = self.at()
        return self.give([pick(stack, here ^ delta, dim) for delta in range(self.size)])

    def trade(self, blocks):
        return lax.all_to_all(blocks, self.names, split_axis=0, concat_axis=0, tiled=True)


def pick(stack, index, dim=0):
    return lax.dynamic_index_in_dim(stack, index, dim, keepdims=False)


def settle(pieces, index, dim=0):
    shape = list(pieces[0].shape)
    shape.insert(dim, len(pieces))
    out = jnp.zeros(shape, pieces[0].dtype)
    for delta, piece in enumerate(pieces):
        out = lax.dynamic_update_index_in_dim(out, piece, index ^ delta, dim)
    return out


def in_order(first, mine, other):
    return jnp.where(first, mine, other), jnp.where(first, other, mine)


def after(value, *events):
    return lax.optimization_barrier((value, *events))[0]


def dot(left, right):
    return jnp.dot(left, right, preferred_element_type=F32)


def total(pieces):
    out = pieces[0].astype(F32)
    for piece in pieces[1:]:
        out = out + piece.astype(F32)
    return out


def norm_back(grad_normed, normed, scale, gain):
    scaled = grad_normed * gain
    return scale * (scaled - normed * jnp.mean(scaled * normed, axis=1, keepdims=True))


def swish_slope(values, sigma):
    return sigma * (1.0 + values * (1.0 - sigma))


def whole_spec(array):
    return pl.BlockSpec(array.shape, lambda j: (0,) * array.ndim)


def attention_probs(query, key, places, docs, places_row, docs_row):
    across = (((1,), (1,)), ((), ()))
    scores = lax.dot_general(query, key, across, preferred_element_type=F32) * HD ** (-0.5)
    allowed = (places >= places_row) & (docs == docs_row)
    scores = jnp.where(allowed, scores, MASKED)
    exponent = jnp.exp(scores - jnp.max(scores, axis=1, keepdims=True))
    return exponent / jnp.sum(exponent, axis=1, keepdims=True)


def attention_kernel(
    normed, w_q, w_k, w_v, w_o, cosine, sine, places, docs, places_row, docs_row,
    query, key, value, mixed, out, sums,
):
    step = pl.program_id(0)
    weights = jnp.concatenate([w_q[...], w_k[...], w_v[...]], axis=1)
    made = jnp.dot(normed[...], weights, preferred_element_type=F32)

    def rotated(values):
        swapped = pltpu.roll(values, HD // 2, axis=1)
        return (values * cosine[...] + swapped * sine[...]).astype(LOW)

    query[...] = rotated(made[:, :HD])
    key[...] = rotated(made[:, HD : 2 * HD])
    value[...] = made[:, 2 * HD :].astype(LOW)
    probs = attention_probs(
        query[...], key[...], places[...], docs[...], places_row[...], docs_row[...]
    )
    low = jnp.dot(probs.astype(LOW), value[...], preferred_element_type=F32).astype(LOW)
    mixed[...] = low
    part = jnp.dot(low, w_o[...], preferred_element_type=F32)

    @pl.when(step == 0)
    def _():
        sums[...] = part

    @pl.when(step > 0)
    def _():
        sums[...] += part

    @pl.when(step == pl.num_programs(0) - 1)
    def _():
        out[...] = sums[...].astype(LOW)


def attention_forward(normed, mats, out_mat, tables):
    length, width = normed.shape
    span = out_mat.shape[0]
    heads = span // HD
    head = lambda rows, first: pl.BlockSpec((rows, HD), lambda j: (0, first + j))
    shapes = [jax.ShapeDtypeStruct((length, span), LOW)] * 4
    shapes.append(jax.ShapeDtypeStruct((length, width), LOW))
    return pl.pallas_call(
        attention_kernel,
        grid=(heads,),
        in_specs=[
            whole_spec(normed),
            head(width, 0),
            head(width, heads),
            head(width, 2 * heads),
            pl.BlockSpec((HD, width), lambda j: (j, 0)),
        ]
        + [whole_spec(table) for table in tables],
        out_specs=[head(length, 0)] * 4 + [whole_spec(shapes[4])],
        out_shape=shapes,
        scratch_shapes=[pltpu.VMEM((length, width), F32)],
        compiler_params=pltpu.CompilerParams(vmem_limit_bytes=48 * 2**20),
        cost_estimate=pl.CostEstimate(
            flops=2 * length * span * (4 * width + 2 * length),
            bytes_accessed=2 * (2 * length * width + 4 * width * span + 4 * length * span),
            transcendentals=heads * length * length,
        ),
    )(normed, mats, mats, mats, out_mat, *tables)


def attention_back_kernel(
    grad_out, w_o, query, key, value, mixed, cosine, sine, places, docs, places_row, docs_row,
    grads, grad_w,
):
    step = pl.program_id(0)
    heads = (grads.shape[1] - 1) // (3 * HD)
    across = (((1,), (1,)), ((), ()))
    down = (((0,), (0,)), ((), ()))
    given = grad_out[...]
    grad_w[...] = lax.dot_general(mixed[...], given, down, preferred_element_type=F32).astype(LOW)
    low = lax.dot_general(given, w_o[...], across, preferred_element_type=F32).astype(LOW)
    probs = attention_probs(
        query[...], key[...], places[...], docs[...], places_row[...], docs_row[...]
    )
    grad_p = lax.dot_general(low, value[...], across, preferred_element_type=F32)
    grad_v = lax.dot_general(probs.astype(LOW), low, down, preferred_element_type=F32)
    grad_s = probs * (grad_p - jnp.sum(grad_p * probs, axis=1, keepdims=True))
    grad_s = grad_s.astype(LOW)
    scale = HD ** (-0.5)
    grad_q = jnp.dot(grad_s, key[...], preferred_element_type=F32) * scale
    grad_k = lax.dot_general(grad_s, query[...], down, preferred_element_type=F32) * scale

    def unrotated(values):
        swapped = pltpu.roll(values, HD // 2, axis=1)
        return (values * cosine[...] - swapped * sine[...]).astype(LOW)

    def column(first):
        return pl.ds(pl.multiple_of((first * heads + step) * HD, HD), HD)

    grads[:, column(0)] = unrotated(grad_q)
    grads[:, column(1)] = unrotated(grad_k)
    grads[:, column(2)] = grad_v.astype(LOW)

    @pl.when(step == 0)
    def _():
        rest = grads.shape[1] - 3 * HD * heads
        grads[:, 3 * HD * heads :] = jnp.zeros((grads.shape[0], rest), LOW)


def attention_back(grad_out, out_mat, kept, tables, extra):
    length, width = grad_out.shape
    span = out_mat.shape[0]
    heads = span // HD
    head = pl.BlockSpec((length, HD), lambda j: (0, j))
    row = pl.BlockSpec((HD, width), lambda j: (j, 0))
    shapes = [
        jax.ShapeDtypeStruct((length, 3 * span + extra), LOW),
        jax.ShapeDtypeStruct((span, width), LOW),
    ]

    return pl.pallas_call(
        attention_back_kernel,
        grid=(heads,),
        in_specs=[whole_spec(grad_out), row] + [head] * 4 + [whole_spec(t) for t in tables],
        out_specs=[whole_spec(shapes[0]), row],
        out_shape=shapes,
        compiler_params=pltpu.CompilerParams(vmem_limit_bytes=48 * 2**20),
        cost_estimate=pl.CostEstimate(
            flops=2 * length * span * (2 * width + 5 * length),
            bytes_accessed=2 * (length * width + 2 * width * span + 7 * length * span),
            transcendentals=heads * length * length,
        ),
    )(grad_out, out_mat, *kept, *tables)


def expert_kernel(flag, slots, mine, other, raw, gate, hidden, grads, dgate):
    step = pl.program_id(0)
    tile = mine.shape[1]
    wide = grads.shape[1] // 2
    is_first = flag[0] == 1
    weights = jnp.concatenate([mine[...], other[...]], axis=1)
    count = slots.shape[0]
    chunk = min(count, 256)
    left_at = pl.multiple_of(step * tile, tile)
    right_at = pl.multiple_of(wide + step * tile, tile)
    for at in range(0, count, chunk):
        here = slice(at, at + chunk)
        made = jnp.dot(slots[here, :], weights, preferred_element_type=F32)
        left, right = made[:, :tile], made[:, tile:]
        a = jnp.where(is_first, left, right)
        b = jnp.where(is_first, right, left)
        sigma = jax.nn.sigmoid(a)
        silu = a * sigma
        low = (silu * b).astype(LOW)
        hidden[here, :] = low
        du = raw[here, :]
        part = jnp.sum(low.astype(F32) * du, axis=1, keepdims=True)
        du = du * gate[here, :]
        da = du * b * (sigma * (1.0 + a * (1.0 - sigma)))
        db = du * silu
        grads[here, pl.ds(left_at, tile)] = jnp.where(is_first, da, db).astype(LOW)
        grads[here, pl.ds(right_at, tile)] = jnp.where(is_first, db, da).astype(LOW)
        dgate[here, :] = part + jnp.where(step == 0, 0.0, dgate[here, :])


def expert_forward(flag, slots, mine, other, raw, gate):
    count, width = slots.shape
    wide = mine.shape[1]
    tile = 128
    column = lambda rows: pl.BlockSpec((rows, tile), lambda j: (0, j))
    shapes = (
        jax.ShapeDtypeStruct((count, wide), LOW),
        jax.ShapeDtypeStruct((count, 2 * wide), LOW),
        jax.ShapeDtypeStruct((count, 1), F32),
    )
    return pl.pallas_call(
        expert_kernel,
        grid=(wide // tile,),
        in_specs=[
            pl.BlockSpec(memory_space=pltpu.SMEM),
            whole_spec(slots),
            column(width),
            column(width),
            column(count),
            whole_spec(gate),
        ],
        out_specs=(column(count), whole_spec(shapes[1]), whole_spec(shapes[2])),
        out_shape=shapes,
        compiler_params=pltpu.CompilerParams(vmem_limit_bytes=48 * 2**20),
        cost_estimate=pl.CostEstimate(
            flops=4 * count * width * wide,
            bytes_accessed=2 * (count * width + 2 * width * wide + 5 * count * wide),
            transcendentals=count * wide,
        ),
    )(flag, slots, mine, other, raw, gate)


def back_kernel(flag, grads, mine, other, dgate, out):
    step = pl.program_id(0)
    tile = mine.shape[0]
    wide = grads.shape[1] // 2
    width = out.shape[1] - 128
    across = (((1,), (1,)), ((), ()))
    made = lax.dot_general(grads[:, :wide], mine[...], across, preferred_element_type=F32)
    made += lax.dot_general(grads[:, wide:], other[...], across, preferred_element_type=F32)
    out[:, pl.ds(pl.multiple_of(step * tile, tile), tile)] = made.astype(LOW)

    @pl.when(step == 0)
    def _():
        lanes = lax.broadcasted_iota(jnp.int32, (out.shape[0], 128), 1)
        high = dgate[...].astype(LOW).astype(F32)
        rest = dgate[...] - high
        cols = jnp.where(lanes == flag[1], high, jnp.where(lanes == flag[1] + 64, rest, 0.0))
        out[:, width:] = cols.astype(LOW)


def expert_back(flag, grads, mine, other, dgate):
    count = grads.shape[0]
    width, wide = mine.shape
    tile = 256
    shape = jax.ShapeDtypeStruct((count, width + 128), LOW)
    row = pl.BlockSpec((tile, wide), lambda j: (j, 0))
    return pl.pallas_call(
        back_kernel,
        grid=(width // tile,),
        in_specs=[
            pl.BlockSpec(memory_space=pltpu.SMEM),
            whole_spec(grads),
            row,
            row,
            whole_spec(dgate),
        ],
        out_specs=whole_spec(shape),
        out_shape=shape,
        compiler_params=pltpu.CompilerParams(vmem_limit_bytes=48 * 2**20),
        cost_estimate=pl.CostEstimate(
            flops=4 * count * width * wide,
            bytes_accessed=2 * (2 * count * wide + 2 * width * wide + count * width),
            transcendentals=0,
        ),
    )(flag, grads, mine, other, dgate)


def make_body(mesh):
    line_z, line_k, line_t = Line(mesh, Z), Line(mesh, K), Line(mesh, C, D)
    columns, cores, blocks = line_z.size, line_k.size, line_t.size
    owners = columns * cores

    def body(
        tokens_in,
        doc_ids,
        routes,
        gain_attn,
        w_query,
        w_key,
        w_value,
        w_out,
        gain_moe,
        w_router,
        shared_gate,
        shared_up,
        shared_down,
        expert_gate,
        expert_up,
        expert_down,
        cotangent,
    ):
        col, core, blk = line_z.at(), line_k.at(), line_t.at()
        x_low, dy_low = tokens_in[0], cotangent[0]
        rows, width = x_low.shape
        length = doc_ids.shape[1]
        part = w_query.shape[0]
        span = width // blocks
        heads = span // HD
        experts = w_router.shape[1]
        group = experts // columns
        line_s = line_t if blocks == group else Line(mesh, C)
        rest = () if blocks == group else (D,)
        spot = line_s.at()

        first = core == 0
        half = width // 2

        def column_halves(value):
            return in_order(first, value[..., :half], value[..., half:])

        def side_by_side(mine, other):
            return jnp.concatenate(in_order(first, mine, other), axis=-1)

        def both_cores(mine, other):
            return jnp.concatenate(in_order(first, mine, line_k.swap(other, 1)), axis=0)

        def all_rows(whole):
            if rest:
                whole = lax.all_gather(whole, rest, axis=1, tiled=True)
            return whole.reshape(-1, whole.shape[-1])

        down_part = both_cores(*column_halves(expert_down))
        in_part = both_cores(*in_order(first, expert_gate, expert_up))

        small = jnp.concatenate([w_router, gain_attn[:, None], gain_moe[:, None]], axis=1)
        small = jnp.pad(small, ((0, 0), (0, -small.shape[1] % 128)))
        extra = small.shape[1]
        mixed_in = jnp.concatenate(
            [w.reshape(part, blocks, span) for w in (w_query, w_key, w_value)]
            + [jnp.broadcast_to(small[:, None], (part, blocks, extra))],
            axis=2,
        ).transpose(1, 0, 2)
        move = [(i, (i % owners) * blocks + i // owners) for i in range(owners * blocks)]
        out_part = lax.ppermute(w_out, (Z, K, C, D), move)
        out_part = out_part.reshape(part, blocks, span).transpose(1, 0, 2)
        attn_part = settle(line_t.give_from(mixed_in), blk)
        attn_part = jnp.concatenate([attn_part, out_part], axis=2).reshape(blocks * part, -1)
        attn_mat = lax.all_gather(attn_part, (Z, K), axis=0, tiled=True)
        dy_col = lax.all_gather(after(dy_low, attn_mat), Z, axis=0, tiled=True)

        x_got = line_t.share(x_low)
        down_got = line_s.trade(down_part)
        routes_got = line_z.share(routes[0])
        down_got, in_part, x_got, routes_got = lax.optimization_barrier(
            (down_got, in_part, x_got, routes_got)
        )
        in_got = line_s.trade(in_part)
        routes_col = settle(routes_got, col)
        x_all = jnp.concatenate(x_got, axis=0).astype(F32)
        small = attn_mat[:, 3 * span : 3 * span + extra].T
        router_t = small[:experts]
        gain_first = small[experts].astype(F32)[None]
        gain_second = small[experts + 1].astype(F32)[None]
        out_mat = attn_mat[:, 3 * span + extra :].reshape(owners, blocks, part, span)
        out_mat = out_mat.transpose(0, 2, 1, 3).reshape(owners * part, width)

        doc_row = doc_ids[0]
        order = blk ^ jnp.arange(blocks, dtype=jnp.int32)
        doc_starts = jnp.sum((doc_row[None, :] < doc_row[:, None]).astype(jnp.int32), axis=1)
        offsets = jnp.arange(length, dtype=jnp.int32) - doc_starts

        def reorder(row):
            grid = row.reshape(blocks, rows)
            return jnp.concatenate([pick(grid, order[i]) for i in range(blocks)])

        doc_here, off_here = reorder(doc_row), reorder(offsets)
        place = reorder(jnp.arange(length, dtype=jnp.int32))
        frequency = jnp.exp(
            jnp.arange(HD // 2, dtype=F32) * (-math.log(10000.0) / (HD // 2))
        )
        angles = off_here.astype(F32)[:, None] * frequency[None, :]
        cosine, sine = jnp.cos(angles), jnp.sin(angles)
        tables = (
            jnp.concatenate([cosine, cosine], axis=1),
            jnp.concatenate([-sine, sine], axis=1),
            place[:, None],
            doc_here[:, None],
            place[None, :],
            doc_here[None, :],
        )

        first_scale = lax.rsqrt(jnp.mean(x_all * x_all, axis=1, keepdims=True) + EPS)
        first_normed = x_all * first_scale
        normed_low = (first_normed * gain_first).astype(LOW)
        *kept, attn_out = attention_forward(normed_low, attn_mat, out_mat, tables)
        attn_out = attn_out.reshape(blocks, rows, width)

        hidden = shared_gate.shape[1] // columns
        shared_in = jnp.concatenate(
            [w.reshape(part, columns, hidden).transpose(1, 0, 2) for w in (shared_gate, shared_up)],
            axis=2,
        )

        in_got = after(in_got, attn_out)
        inputs = after(x_low, in_got).astype(F32)
        after_attn = inputs + total(line_t.give([attn_out[i] for i in range(blocks)]))

        second_scale = lax.rsqrt(jnp.mean(after_attn * after_attn, axis=1, keepdims=True) + EPS)
        second_normed = after_attn * second_scale
        second_low = (second_normed * gain_second).astype(LOW)
        second_col = lax.all_gather(second_low, Z, axis=0, tiled=True)
        mat_down = all_rows(after(down_got, second_low))
        mat_down = side_by_side(mat_down, line_k.swap(mat_down, 1))
        mat_mine = all_rows(after(in_got, second_low))
        mat_other = line_k.swap(mat_mine, 1)
        shared_in = settle(line_z.give_from(after(shared_in, second_col)), col)

        def router(values):
            return jax.nn.softmax(dot(values, router_t.T), axis=1)

        router_probs = router(second_low)

        capacity = min(rows, rows * TOP * 4 // (3 * experts))
        slots = columns * capacity
        wanted = col * group + jnp.arange(group, dtype=jnp.int32)
        hits = jnp.any(routes_col[None] == wanted[:, None, None, None], axis=3)
        ranks = jnp.cumsum(hits.astype(jnp.int32), axis=2) - 1
        ranks = jnp.where(hits, ranks, -1)
        chosen = ranks[:, :, None, :] == jnp.arange(capacity, dtype=jnp.int32)[:, None]
        same = jnp.eye(columns, dtype=jnp.bool_)[None, :, None, :, None]
        spread = (
            (chosen[:, :, :, None, :] & same).reshape(group * slots, columns * rows).astype(LOW)
        )

        def dispatch(values):
            sent = dot(spread, values).astype(LOW).reshape(group, slots, width)
            return line_s.trade(sent).reshape(group * slots, width)

        def collect(values):
            return line_s.trade(values.reshape(group, slots, -1)).reshape(group * slots, -1)

        dy_slots = dispatch(dy_col)
        du_raw = dot(dy_slots, mat_down.T)
        second_slots = after(dispatch(after(second_col, dy_slots)), du_raw, mat_other)
        expert = col * group + spot
        gate = lax.dynamic_slice_in_dim(router(second_slots), expert, 1, axis=1)
        flag = jnp.stack([first.astype(jnp.int32), expert])
        hidden_low, grad_in, dgate = expert_forward(
            flag, second_slots, mat_mine, mat_other, du_raw, gate
        )
        wide = hidden_low.shape[1]

        cuts = -(-width // (2 * hidden))
        down_cuts = jnp.pad(shared_down, ((0, 0), (0, cuts * 2 * hidden - width)))
        shared_part = jnp.concatenate(
            [shared_in.reshape(columns * part, 2 * hidden)] + jnp.split(down_cuts, cuts, axis=1)
        )
        shared_all = lax.all_gather(after(shared_part, second_slots), (K, C, D), axis=0)
        grad_slots = expert_back(flag, grad_in, mat_mine, mat_other, dgate)

        shared_all = after(shared_all, grad_slots)
        mat_sin = shared_all[:, : columns * part].reshape(-1, columns, part, 2 * hidden)
        mat_sin = mat_sin.transpose(1, 0, 2, 3).reshape(width, 2 * hidden)
        mat_sdown = jnp.concatenate(jnp.split(shared_all[:, columns * part :], cuts, axis=1), axis=2)
        mat_sdown = mat_sdown[:, :, :width].reshape(hidden, width)
        second_late, dy_late = after((second_col, dy_col), grad_slots)
        shared_pre = dot(second_late, mat_sin)
        shared_a, shared_b = shared_pre[:, :hidden], shared_pre[:, hidden:]
        shared_sigma = jax.nn.sigmoid(shared_a)
        shared_low = (shared_a * shared_sigma * shared_b).astype(LOW)
        dsu = dot(dy_late, mat_sdown.T)
        dsa = (dsu * shared_b * swish_slope(shared_a, shared_sigma)).astype(LOW)
        dsb = (dsu * shared_a * shared_sigma).astype(LOW)
        dsab = jnp.concatenate([dsa, dsb], axis=1)

        routed = (dot(after(hidden_low, dsab), mat_down) * gate).astype(LOW)
        def both_parts(mine, other):
            return [mine, line_k.swap(other, 1)]

        def low_total(pieces):
            return total(pieces).astype(LOW)

        def shared_home(grad):
            lead, count, wide = grad.shape
            grad = grad.reshape(lead, cores, count // cores, wide)
            return both_parts(*in_order(first, grad[:, 0], grad[:, 1]))

        def by_owner(mine):
            lead, count, wide = mine.shape
            return mine.reshape(lead, blocks, count // blocks, wide).transpose(1, 0, 2, 3)

        slots_back = collect(grad_slots)
        grad_routed = dot(spread.T, after(slots_back, routed))
        grad_second = jnp.concatenate(
            [dot(dsab, mat_sin.T) + grad_routed[:, :width], grad_routed[:, width:]], axis=1
        )
        second_sent = grad_second.astype(LOW)
        grad_second = lax.psum_scatter(second_sent, Z, scatter_dimension=0, tiled=True).astype(F32)


        def send_home(mine):
            mine = mine.reshape(line_s.size, -1, mine.shape[-1])
            if rest:
                mine = lax.psum_scatter(mine, rest, scatter_dimension=1, tiled=True)
            return mine

        def home(got):
            got = got.reshape(cores, -1, *got.shape[1:])
            kept, other = in_order(first, got[0], got[1])
            return kept, line_k.swap(other, 1)

        weighted = (hidden_low.astype(F32) * gate).astype(LOW)
        slots_late = after(second_slots, grad_slots)
        grad_w = dot(slots_late.T, grad_in).astype(LOW)

        routed_back = collect(after(routed, grad_routed))
        grad_sin = dot(second_late.T, dsab).astype(LOW)
        grad_down = dot(weighted.T, dy_slots).astype(LOW)
        down_sums = low_total(both_parts(*column_halves(grad_down)))
        sin_sums = shared_home(grad_sin.reshape(columns, cores * blocks * part, 2 * hidden))
        in_sums = both_parts(grad_w[:, :wide], grad_w[:, wide:])
        in_sums = low_total(in_sums)
        sin_sums = by_owner(low_total(sin_sums))
        layer_sent = (dot(shared_low, mat_sdown) + dot(spread.T, routed_back)).astype(LOW)
        down_back = line_s.trade(send_home(down_sums))
        layer_out = lax.psum_scatter(layer_sent, Z, scatter_dimension=0, tiled=True)
        grad_sdown = dot(shared_low.T, after(dy_late, second_sent)).astype(LOW)
        sdown_sums = by_owner(low_total(shared_home(grad_sdown[None])))

        dprobs = grad_second[:, width : width + experts]
        dprobs = dprobs + grad_second[:, width + 64 : width + 64 + experts]
        dlogits = (
            router_probs * (dprobs - jnp.sum(dprobs * router_probs, axis=1, keepdims=True))
        ).astype(LOW)
        grad_router_t = dot(dlogits.T, second_low)
        grad_second = grad_second[:, :width] + dot(dlogits, router_t)

        grad_gain_second = jnp.sum(grad_second * second_normed, axis=0, keepdims=True)
        dy = dy_low.astype(F32)
        grad_after = dy + norm_back(grad_second, second_normed, second_scale, gain_second)
        grad_after_low = grad_after.astype(LOW)
        grad_after_low = jnp.concatenate(line_t.share(grad_after_low), axis=0)
        in_back = line_s.trade(send_home(in_sums))
        sin_back = line_t.trade(sin_sums)

        grad_made, grad_outmat = attention_back(grad_after_low, out_mat, kept, tables, extra)
        down_back, in_back, sin_back = after((down_back, in_back, sin_back), grad_made)
        layer_out = after_attn + layer_out.astype(F32)
        small_grads = jnp.concatenate([grad_router_t, grad_gain_second], axis=0).T
        small_grads = jnp.pad(small_grads, ((0, 0), (3 * span, extra - experts - 1)))
        grad_qkv = (dot(normed_low.T, grad_made) + small_grads).astype(LOW)
        grad_first = dot(grad_made, attn_mat[:, : 3 * span + extra].T).astype(LOW).reshape(blocks, rows, width)
        grad_first = total(line_t.give([grad_first[i] for i in range(blocks)]))
        local_normed = first_normed[:rows]
        grad_inputs = grad_after + norm_back(
            grad_first, local_normed, first_scale[:rows], gain_first
        )

        grad_edown = side_by_side(*home(down_back)).astype(F32)
        kept, came = home(in_back)
        grad_egate = jnp.where(first, kept, came).astype(F32)
        grad_eup = jnp.where(first, came, kept).astype(F32)
        grad_outmat = lax.psum_scatter(grad_outmat, (Z, K), scatter_dimension=0, tiled=True)
        back = [(there, here) for here, there in move]
        grad_outmat = lax.ppermute(grad_outmat, (Z, K, C, D), back).astype(F32)
        grad_qkv = lax.psum_scatter(grad_qkv, (Z, K), scatter_dimension=0, tiled=True)
        grad_qkv = line_t.trade(grad_qkv.reshape(blocks, part, 3 * span + extra))
        sdown_back = line_t.trade(sdown_sums)
        grad_sin = total([sin_back[i] for i in range(blocks)]).astype(LOW)
        grad_sin = settle(line_z.give_from(grad_sin), col)
        grad_sin = grad_sin.transpose(1, 0, 2).astype(F32)
        grad_sgate = grad_sin[:, :, :hidden].reshape(part, -1)
        grad_sup = grad_sin[:, :, hidden:].reshape(part, -1)

        grad_sdown = total([sdown_back[i, 0] for i in range(blocks)])
        grad_qkv = grad_qkv.astype(F32)
        small_grads = jnp.sum(grad_qkv[:, :, 3 * span :], axis=0)
        grad_qkv = grad_qkv[:, :, : 3 * span].reshape(blocks, part, 3, span)
        grad_qkv = grad_qkv.transpose(2, 1, 0, 3).reshape(3, part, width)

        grad_gain_first = sum(
            jnp.sum(grad_qkv[i] * w.astype(F32), axis=1)
            for i, w in enumerate((w_query, w_key, w_value))
        ) / gain_attn.astype(F32)

        return (
            layer_out[None],
            grad_inputs[None],
            grad_gain_first,
            grad_qkv[0],
            grad_qkv[1],
            grad_qkv[2],
            grad_outmat,
            small_grads[:, experts],
            small_grads[:, :experts],
            grad_sgate,
            grad_sup,
            grad_sdown,
            grad_egate,
            grad_eup,
            grad_edown,
        )

    return body


def solution(mesh):
    owners, blocks, halves = mesh.devices.shape
    mesh = Mesh(mesh.devices.reshape(owners // 2, 2, blocks, halves), (Z, K, C, D))
    every = P((Z, K, C, D))
    tokens = P((Z, K), (C, D))
    return jax.shard_map(
        make_body(mesh),
        mesh=mesh,
        in_specs=(tokens, P((Z, K)), tokens) + (every,) * 10 + (tokens,) * 4,
        out_specs=(tokens, tokens) + (every,) * 10 + (tokens,) * 3,
        check_vma=False,
    )
```

time: 836 us -> 830 us (level)
  matrix products: 195 us -> 114 us
  Pallas kernels: 0 us -> 71.4 us
  waiting for transfers between devices: 326 us -> 348 us
  starting transfers between devices: 111 us -> 98.4 us
  other arithmetic: 111 us -> 102 us
    all_to_all x9 -> x11, waiting for transfers between devices: 129 us -> 214 us  [trade(): lax.all_to_all(blocks, self.names, split_axis=0, concat_axis=0, tiled=True)]
    pallas_call x0 -> x4, Pallas kernels: none -> 71.4 us  [the longest x1 24.7 us: expert_forward(): pl.pallas_call(expert_kernel, grid=(wide // tile,), in_specs=[pl.BlockSpe...]
    dot_general x29 -> x20, matrix products: 179 us -> 114 us  [dot(): return jnp.dot(left, right, preferred_element_type=F32)]
    ppermute x56 -> x34, waiting for transfers between devices: 143 us -> 102 us  [swap(): lax.ppermute(value, self.names, [(i, i ^ delta) for i in range(self.size)])]
    ppermute x56 -> x34, starting transfers between devices: 60.1 us -> 38.9 us  [swap(): lax.ppermute(value, self.names, [(i, i ^ delta) for i in range(self.size)])]
    all_gather x1, waiting for transfers between devices: 19.9 us -> 2.77 us  [body(): attn_mat = lax.all_gather(attn_part, (Z, K), axis=0, tiled=True)]
    dot_general x5 -> x0, matrix products: 10.4 us -> none  [the longest x1 3.33 us: body(): jnp.einsum('hqk,qhd->khd', probs_low, grad_mixed, preferred_element_type=...]
    all_to_all x9 -> x11, starting transfers between devices: 45.4 us -> 54.9 us  [trade(): lax.all_to_all(blocks, self.names, split_axis=0, concat_axis=0, tiled=True)]
  transfers between devices with their start and end apart: 76 -> 55, of which waited for: 35 -> 27; matrix products, arithmetic and copies ran while one was open for 42% -> 28% of each run, Pallas kernels for 0% -> 9%
where the time goes in v2:
time: 830 us; the launch traced here: 820 us
  waiting for transfers between devices  348 us (42%)
  matrix products  114 us (14%)
  other arithmetic  102 us (12%)
  starting transfers between devices  98.4 us (12%)
  Pallas kernels  71.4 us (9%)
  local copies, waits for them, and re-layouts  61.9 us (7%)
  between operations  24 us (3%)
    all_to_all x11, waiting for transfers between devices, trade(): lax.all_to_all(blocks, self.names, split_axis=0, concat_axis=0, tiled=True)  214 us
    dot_general x20, matrix products, dot(): return jnp.dot(left, right, preferred_element_type=F32)  114 us
    ppermute x34, waiting for transfers between devices, swap(): lax.ppermute(value, self.names, [(i, i ^ delta) for i in range(self.size)])  102 us
    all_to_all x11, starting transfers between devices, trade(): lax.all_to_all(blocks, self.names, split_axis=0, concat_axis=0, tiled=True)  54.9 us
    ppermute x34, starting transfers between devices, swap(): lax.ppermute(value, self.names, [(i, i ^ delta) for i in range(self.size)])  38.9 us
    all_gather x1, waiting for transfers between devices, body(): second_col = lax.all_gather(second_low, Z, axis=0, tiled=True)  26.4 us
    select_n x11, other arithmetic, in_order(): return (jnp.where(first, mine, other), jnp.where(first, other, mine))  25.3 us
    pallas_call x1, Pallas kernels, expert_forward(): pl.pallas_call(expert_kernel, grid=(wide // tile,), in_specs=[pl.BlockSpe...  24.7 us
  transfers between devices with their start and end apart: 55, of which 27 were waited for; matrix products, arithmetic and copies ran while one was open for 28% of the time, Pallas kernels for 9%

profile of v2, /device:TPU:0, one launch (start us, length us, event | category | flops | bytes accessed | tf_op | source)
XLA Modules:
  0.0 820.3 jit_solution(17382652437350452105)
XLA Ops:
  15.4 3.4 collective-permute-start.8
  22.0 3.3 collective-permute-done.8
  26.2 5.1 collective-permute-done.10
  37.6 7.0 collective-permute-done
  46.6 4.7 all-to-all-start
  51.4 3.2 collective-permute-start.7
  66.9 3.3 broadcast_select_fusion.6
  74.5 23.8 %collective-permute-done.4 = bf16[128,2048]{1,0:T(8,128)(2,1)} collective-permute-done((bf16[128,2048]{1,0:T(8,128)(2,1)S(1)}, bf16[128,2048]{1,0:T(8,128)(2,1)}, u32[]{:S(2)}, u32[]{:S(2)}) %collective-permute-start.4) | collective-permute-done | bytes 524320 | tf_op jit(solution)/shard_map/ppermute | solution.py:29
  98.3 10.1 %collective-permute-done.3 = bf16[128,2048]{1,0:T(8,128)(2,1)} collective-permute-done((bf16[128,2048]{1,0:T(8,128)(2,1)S(1)}, bf16[128,2048]{1,0:T(8,128)(2,1)}, u32[]{:S(2)}, u32[]{:S(2)}) %collective-permute-start.3) | collective-permute-done | bytes 524320 | tf_op jit(solution)/shard_map/ppermute | solution.py:29
  108.4 5.2 all-to-all-start.1
  123.0 4.2 convert_multiply_fusion
  132.5 16.1 %shard_map.280 = (bf16[512,512]{1,0:T(8,128)(2,1)S(1)}, bf16[512,512]{1,0:T(8,128)(2,1)S(1)}, bf16[512,512]{1,0:T(8,128)(2,1)S(1)}, bf16[512,512]{1,0:T(8,128)(2,1)S(1)}, bf16[512,2048]{1,0:T(8,128)(2,1)S(1)}) custom-call(bf16[512,2048]{1,0:T(8,128)(2,1)} %get-tuple-element.179.normed, bf16[2048,2176]{1,0:T(8,128)(2,1)} %all-gather.6.cloned.1.call-done.w_q.w_k.w_v, ...), custom_call_target="tpu_custom_call" | custom-call | flops 4831838208 | bytes 14680064 | tf_op jit(solution)/shard_map/pallas_call | solution.py:141
  158.1 22.2 %all-to-all-done.1 = bf16[4,512,1408]{2,1,0:T(8,128)(2,1)} async-done(((bf16[4,512,1408]{2,1,0:T(8,128)(2,1)}), bf16[4,512,1408]{2,1,0:T(8,128)(2,1)}, u32[]{:S(2)}, u32[]{:S(2)}) %all-to-all-start.1) | async-done | bytes 5767200 | tf_op jit(solution)/shard_map/all_to_all | solution.py:42
  180.2 20.3 %collective-permute-done.12 = bf16[128,2048]{1,0:T(8,128)(2,1)} collective-permute-done((bf16[128,2048]{1,0:T(8,128)(2,1)}, bf16[128,2048]{1,0:T(8,128)(2,1)}, u32[]{:S(2)}, u32[]{:S(2)}) %collective-permute-start.12) | collective-permute-done | bytes 524320 | tf_op jit(solution)/shard_map/ppermute | solution.py:29
  205.4 6.1 convolution_convert_fusion.4
  211.5 5.3 all-to-all-start.2
  218.9 5.7 broadcast_select_fusion.2
  224.5 26.4 %all-gather.8.cloned.1.call-done = bf16[512,2048]{1,0:T(8,128)(2,1)} async-done(((bf16[128,2048]{1,0:T(8,128)(2,1)}), bf16[512,2048]{1,0:T(8,128)(2,1)}) %all-gather.8.cloned.1.call-update) | async-done | bytes 2097168 | tf_op jit(solution)/shard_map/all_gather | solution.py:470
  256.9 8.2 all-to-all-done.2
  265.1 5.9 convolution_convert_fusion.3
  271.1 4.8 all-to-all-start.3
  277.8 11.9 %fusion.5.raw = f32[1024,1408]{1,0:T(8,128)} fusion(bf16[1024,2048]{1,0:T(8,128)(2,1)} %bitcast.42, bf16[1408,1024]{1,0:T(8,128)(2,1)} %get-tuple-element.170, bf16[1408,1024]{1,0:T(8,128)(2,1)} %get-tuple-element.169), kind=kOutput, calls=%fused_computation.23 | convolution fusion | flops 5917114368 | bytes 15728640 | tf_op jit(solution)/shard_map/dot_general | solution.py:67
  289.6 33.9 %all-to-all-done.3 = bf16[4,256,2048]{2,1,0:T(8,128)(2,1)} async-done(((bf16[4,256,2048]{2,1,0:T(8,128)(2,1)}), bf16[4,256,2048]{2,1,0:T(8,128)(2,1)}, u32[]{:S(2)}, u32[]{:S(2)}) %all-to-all-start.3) | async-done | bytes 4194336 | tf_op jit(solution)/shard_map/all_to_all | solution.py:42
  323.6 3.4 fusion.53
  328.1 24.7 %shard_map.281 = (bf16[1024,1408]{1,0:T(8,128)(2,1)S(1)}, bf16[1024,2816]{1,0:T(8,128)(2,1)}, f32[1024,1]{1,0:T(8,128)S(1)}) custom-call(s32[2]{0:T(128)S(1)} %pad_add_fusion.2.flag, bf16[1024,2048]{1,0:T(8,128)(2,1)} %bitcast.44.slots, bf16[2048,1408]{1,0:T(8,128)(2,1)} %bitcast.46.mine, bf16[2048,1408]{1,0:T(8,128)(2,1)} %collective-permute-done.16.other, ...), custom_call_target="tpu_custom_call" | custom-call | flops 11811160064 | bytes 30146560 | tf_op jit(solution)/shard_map/pallas_call | solution.py:269
  354.7 17.9 %shard_map.282 = bf16[1024,2176]{1,0:T(8,128)(2,1)S(1)} custom-call(s32[2]{0:T(128)S(1)} %pad_add_fusion.2.flag, bf16[1024,2816]{1,0:T(8,128)(2,1)} %get-tuple-element.71.grads, bf16[2048,1408]{1,0:T(8,128)(2,1)} %bitcast.46.mine, bf16[2048,1408]{1,0:T(8,128)(2,1)} %collective-permute-done.16.other, f32[1024,1]{1,0:T(8,128)S(1)} %get-tuple-element.72.dgate), custom_call_target="tpu_custom_call" | custom-call | flops 11811160064 | bytes 21495808 | tf_op jit(solution)/shard_map/pallas_call | solution.py:316
  374.7 4.9 all-to-all-start.4
  379.8 3.4 all-gather.12.cloned.1.call-done
  392.6 3.4 fusion.56
  401.7 8.6 %multiply_convert_fusion = bf16[1024,2048]{1,0:T(8,128)(2,1)} fusion(bf16[1024,1408]{1,0:T(8,128)(2,1)S(1)} %copy-done.10, f32[1024]{0:T(1024)S(1)} %get-tuple-element.157, bf16[1408,1024]{1,0:T(8,128)(2,1)S(1)} %copy-done.32, bf16[1408,1024]{1,0:T(8,128)(2,1)S(1)} %copy-done.31), kind=kOutput, calls=%fused_computation.3 | convolution fusion | flops 5921308672 | bytes 12849152 | tf_op jit(solution)/shard_map/dot_general | solution.py:67
  410.2 20.0 %all-to-all-done.4 = bf16[4,256,2176]{2,1,0:T(8,128)(2,1)} async-done(((bf16[4,256,2176]{2,1,0:T(8,128)(2,1)}), bf16[4,256,2176]{2,1,0:T(8,128)(2,1)}, u32[]{:S(2)}, u32[]{:S(2)}) %all-to-all-start.4) | async-done | bytes 4456480 | tf_op jit(solution)/shard_map/all_to_all | solution.py:42
  430.2 5.1 fusion.13
  435.3 6.3 fusion.4
  443.3 5.0 all-to-all-start.5
  448.9 16.0 %convolution_convert_fusion = bf16[2048,2816]{1,0:T(8,128)(2,1)S(1)} fusion(bf16[1024,2048]{1,0:T(8,128)(2,1)} %bitcast.44.slots, bf16[1024,2816]{1,0:T(8,128)(2,1)} %get-tuple-element.71.grads), kind=kOutput, calls=%fused_computation.2 | convolution fusion | flops 11816927232 | bytes 21495808 | tf_op jit(solution)/shard_map/dot_general | solution.py:67
  464.9 3.2 slice.300
  470.9 24.3 %all-to-all-done.5 = bf16[4,256,2048]{2,1,0:T(8,128)(2,1)} async-done(((bf16[4,256,2048]{2,1,0:T(8,128)(2,1)}), bf16[4,256,2048]{2,1,0:T(8,128)(2,1)}, u32[]{:S(2)}, u32[]{:S(2)}) %all-to-all-start.5) | async-done | bytes 4194336 | tf_op jit(solution)/shard_map/all_to_all | solution.py:42
  495.3 4.9 fusion.11
  503.5 11.2 %convolution_convert_fusion.2 = bf16[1408,2048]{1,0:T(8,128)(2,1)} fusion(bf16[1024,2048]{1,0:T(8,128)(2,1)} %bitcast.42, bf16[1024,1408]{1,0:T(8,128)(2,1)} %copy-done.9, f32[1024]{0:T(1024)S(1)} %get-tuple-element.157), kind=kOutput, calls=%fused_computation.5 | convolution fusion | flops 5912788992 | bytes 12849152 | tf_op jit(solution)/shard_map/dot_general | solution.py:67
  523.1 10.3 %collective-permute-done.22 = bf16[128,2048]{1,0:T(8,128)(2,1)S(1)} collective-permute-done((bf16[128,2048]{1,0:T(8,128)(2,1)S(1)}, bf16[128,2048]{1,0:T(8,128)(2,1)S(1)}, u32[]{:S(2)}, u32[]{:S(2)}) %collective-permute-start.22) | collective-permute-done | bytes 524320 | tf_op jit(solution)/shard_map/ppermute | solution.py:29
  533.5 9.0 %collective-permute-done.21 = bf16[128,2048]{1,0:T(8,128)(2,1)S(1)} collective-permute-done((bf16[128,2048]{1,0:T(8,128)(2,1)S(1)}, bf16[128,2048]{1,0:T(8,128)(2,1)S(1)}, u32[]{:S(2)}, u32[]{:S(2)}) %collective-permute-start.21) | collective-permute-done | bytes 524320 | tf_op jit(solution)/shard_map/ppermute | solution.py:29
  544.1 12.7 %shard_map.283 = (bf16[512,1664]{1,0:T(8,128)(2,1)S(1)}, bf16[512,2048]{1,0:T(8,128)(2,1)}) custom-call(bf16[512,2048]{1,0:T(8,128)(2,1)} %pad_maximum_fusion.8.grad_out, bf16[512,2048]{1,0:T(8,128)(2,1)} %bitcast.245, bf16[512,512]{1,0:T(8,128)(2,1)S(1)} %copy-done.2, bf16[512,512]{1,0:T(8,128)(2,1)S(1)} %copy-done.4, bf16[512,512]{1,0:T(8,128)(2,1)S(1)} %copy-done.6, ...), custom_call_target="tpu_custom_call" | custom-call | flops 3489660928 | bytes 9961472 | tf_op jit(solution)/shard_map/pallas_call | solution.py:214
  556.8 7.2 add_convert_fusion.2
  564.0 4.6 all-to-all-start.7
  570.5 8.5 %add_convert_fusion = bf16[2048,1664]{1,0:T(8,128)(2,1)} fusion(f32[2048,17]{1,0:T(8,128)S(1)} %bitcast.277, bf16[512,2048]{1,0:T(8,128)(2,1)} %get-tuple-element.179.normed, bf16[512,1664]{1,0:T(8,128)(2,1)S(1)} %get-tuple-element.86), kind=kOutput, calls=%fused_computation | convolution fusion | flops 3496476672 | bytes 10756096 | tf_op jit(solution)/shard_map/dot_general | solution.py:67
  579.0 8.4 %add_convert_fusion.1 = bf16[2048,1408]{1,0:T(8,128)(2,1)} fusion(bf16[2048,1408]{1,0:T(8,128)(2,1)} %collective-permute-done.28, bf16[2048,2816]{1,0:T(8,128)(2,1)} %copy-done.19), kind=kLoop, calls=%fused_computation.1 | loop fusion | flops 11534336 | bytes 17301504 | tf_op jit(solution)/shard_map/convert_element_type | solution.py:540
  587.4 15.8 %all-to-all-done.7 = bf16[4,352,1024]{2,1,0:T(8,128)(2,1)} async-done(((bf16[4,352,1024]{2,1,0:T(8,128)(2,1)}), bf16[4,352,1024]{2,1,0:T(8,128)(2,1)}, u32[]{:S(2)}, u32[]{:S(2)}) %all-to-all-start.7) | async-done | bytes 2883616 | tf_op jit(solution)/shard_map/all_to_all | solution.py:42
  603.2 5.3 all-to-all-start.8
  608.6 5.5 convolution_convert_fusion.1
  620.4 5.2 collective-permute-done.33
  627.5 45.3 %all-to-all-done.8 = bf16[4,512,1408]{2,1,0:T(8,128)(2,1)} async-done(((bf16[4,512,1408]{2,1,0:T(8,128)(2,1)}), bf16[4,512,1408]{2,1,0:T(8,128)(2,1)}, u32[]{:S(2)}, u32[]{:S(2)}) %all-to-all-start.8) | async-done | bytes 5767200 | tf_op jit(solution)/shard_map/all_to_all | solution.py:42
  672.8 4.4 all-to-all-start.10
  677.2 4.6 fusion.2
  683.6 11.5 %all-to-all-done.10 = bf16[4,1,88,2048]{3,2,1,0:T(8,128)(2,1)} async-done(((bf16[4,1,88,2048]{3,2,1,0:T(8,128)(2,1)}), bf16[4,1,88,2048]{3,2,1,0:T(8,128)(2,1)}, u32[]{:S(2)}, u32[]{:S(2)}) %all-to-all-start.10) | async-done | bytes 1441824 | tf_op jit(solution)/shard_map/all_to_all | solution.py:42
  695.2 4.9 all-to-all-start.9
  702.4 7.2 fusion.6
  715.7 27.1 %all-to-all-done.9 = bf16[4,4,64,1408]{3,2,1,0:T(8,128)(2,1)} async-done(((bf16[4,4,64,1408]{3,2,1,0:T(8,128)(2,1)}), bf16[4,4,64,1408]{3,2,1,0:T(8,128)(2,1)}, u32[]{:S(2)}, u32[]{:S(2)}) %all-to-all-start.9) | async-done | bytes 2883616 | tf_op jit(solution)/shard_map/all_to_all | solution.py:42
  750.6 4.6 broadcast_select_fusion.3
  757.2 6.5 collective-permute-done.31
  773.3 3.3 maximum_convert_fusion
  776.6 4.0 add_bitcast_fusion
  782.2 5.8 all-to-all-start.6
  788.1 8.7 %select_convert_fusion = (f32[2,512,1408]{2,1,0:T(8,128)}, f32[2,512,1408]{2,1,0:T(8,128)}) fusion(bf16[2,512,1408]{2,1,0:T(8,128)(2,1)} %collective-permute-done.34, pred[]{:T(512)S(6)} %eq.50, bf16[4,512,1408]{2,1,0:T(8,128)(2,1)} %all-to-all-done.8), kind=kLoop, calls=%fused_computation.33 | loop fusion | flops 7208960 | bytes 20185088 | tf_op jit(solution)/shard_map/convert_element_type | solution.py:621
  797.6 5.7 all-to-all-done.6
  (364 shorter events, 157.8 us)
Async XLA Ops:
  7.2 113.0 %all-gather.6.cloned.1.call-start = ((), (), s32[]{:S(2)}) async-start(), calls=%async_computation.15 | async-start | bytes 10027008 | tf_op jit(solution)/shard_map/all_gather | solution.py:407
  7.2 24.1 %collective-permute-start.11 = (bf16[64,2048]{1,0:T(8,128)(2,1)}, bf16[64,2048]{1,0:T(8,128)(2,1)S(1)}, u32[]{:S(2)}, u32[]{:S(2)}) collective-permute-start(bf16[64,2048]{1,0:T(8,128)(2,1)} %param.24), channel_id=1, source_target_pairs={{0,0},{1,4},{2,8},{3,12},{4,16},{5,20},{6,24},{7,28},{8,1},{9,5},{... | collective-permute-start | bytes 786440 | tf_op jit(solution)/shard_map/ppermute | solution.py:403
  15.4 10.0 %collective-permute-start.8 = (bf16[64,1664]{1,0:T(8,128)(2,1)S(1)}, bf16[64,1664]{1,0:T(8,128)(2,1)S(1)}, u32[]{:S(2)}, u32[]{:S(2)}) collective-permute-start(bf16[64,1664]{1,0:T(8,128)(2,1)S(1)} %bitcast.287), channel_id=1, source_target_pairs={{0,1},{1,0},{2,3},{3,2},{4,5},{5,4},{6,7},{7,6},{8,9},{9,8},{10,11... | collective-permute-start | bytes 638984 | tf_op jit(solution)/shard_map/ppermute | solution.py:29
  18.8 7.4 collective-permute-start.9
  21.3 10.0 %collective-permute-start.10 = (bf16[64,1664]{1,0:T(8,128)(2,1)S(1)}, bf16[64,1664]{1,0:T(8,128)(2,1)S(1)}, u32[]{:S(2)}, u32[]{:S(2)}) collective-permute-start(bf16[64,1664]{1,0:T(8,128)(2,1)S(1)} %bitcast.285), channel_id=1, source_target_pairs={{0,3},{1,2},{2,1},{3,0},{4,7},{5,6},{6,5},{7,4},{8,11},{9,10},{10,... | collective-permute-start | bytes 638984 | tf_op jit(solution)/shard_map/ppermute | solution.py:29
  34.4 32.3 %collective-permute-start.1 = (bf16[2,512,1408]{2,1,0:T(8,128)(2,1)}, bf16[2,512,1408]{2,1,0:T(8,128)(2,1)}, u32[]{:S(2)}, u32[]{:S(2)}) collective-permute-start(bf16[2,512,1408]{2,1,0:T(8,128)(2,1)} %broadcast_select_fusion.7), channel_id=1, source_target_pairs={{0,4},{4,0},{1,5},{5,1},{2,6},{6,2},{3,7},{7,3},{8,12},{12,8},{9,1... | collective-permute-start | bytes 8650760 | tf_op jit(solution)/shard_map/ppermute | solution.py:29
  37.5 7.0 collective-permute-start
  46.6 20.0 %copy-start.53 = (s32[1,512]{1,0:T(1,128)S(1)}, s32[1,512]{1,0:T(1,128)}, u32[]{:S(2)}) copy-start(s32[1,512]{1,0:T(1,128)} %param.18) | copy-start | bytes 6148
  46.6 61.8 %all-to-all-start = ((bf16[4,352,1024]{2,1,0:T(8,128)(2,1)}), bf16[4,352,1024]{2,1,0:T(8,128)(2,1)}, u32[]{:S(2)}, u32[]{:S(2)}) async-start(bf16[4,352,1024]{2,1,0:T(8,128)(2,1)} %pad_maximum_fusion.5), calls=%async_computation | async-start | bytes 5767168 | tf_op jit(solution)/shard_map/all_to_all | solution.py:42
  51.4 18.9 %collective-permute-start.7 = (s32[128,6]{0,1:T(8,128)S(1)}, s32[128,6]{0,1:T(8,128)S(1)}, u32[]{:S(2)}, u32[]{:S(2)}) collective-permute-start(s32[128,6]{0,1:T(8,128)S(1)} %bitcast.293), channel_id=1, source_target_pairs={{0,24},{8,16},{16,8},{24,0},{1,25},{9,17},{17,9},{25,1},{2,26},{10... | collective-permute-start | bytes 9224 | tf_op jit(solution)/shard_map/ppermute | solution.py:29
  54.6 19.8 %collective-permute-start.6 = (s32[128,6]{0,1:T(8,128)S(1)}, s32[128,6]{0,1:T(8,128)S(1)}, u32[]{:S(2)}, u32[]{:S(2)}) collective-permute-start(s32[128,6]{0,1:T(8,128)S(1)} %bitcast.294), channel_id=1, source_target_pairs={{0,16},{8,24},{16,0},{24,8},{1,17},{9,25},{17,1},{25,9},{2,18},{10... | collective-permute-start | bytes 9224 | tf_op jit(solution)/shard_map/ppermute | solution.py:29
  54.9 43.4 %collective-permute-start.4 = (bf16[128,2048]{1,0:T(8,128)(2,1)S(1)}, bf16[128,2048]{1,0:T(8,128)(2,1)}, u32[]{:S(2)}, u32[]{:S(2)}) collective-permute-start(bf16[128,2048]{1,0:T(8,128)(2,1)S(1)} %bitcast.253), channel_id=1, source_target_pairs={{0,3},{1,2},{2,1},{3,0},{4,7},{5,6},{6,5},{7,4},{8,11},{9,10},{10,... | collective-permute-start | bytes 1572872 | tf_op jit(solution)/shard_map/ppermute | solution.py:29
  57.7 50.7 %collective-permute-start.3 = (bf16[128,2048]{1,0:T(8,128)(2,1)S(1)}, bf16[128,2048]{1,0:T(8,128)(2,1)}, u32[]{:S(2)}, u32[]{:S(2)}) collective-permute-start(bf16[128,2048]{1,0:T(8,128)(2,1)S(1)} %bitcast.254), channel_id=1, source_target_pairs={{0,2},{1,3},{2,0},{3,1},{4,6},{5,7},{6,4},{7,5},{8,10},{9,11},{10,... | collective-permute-start | bytes 1572872 | tf_op jit(solution)/shard_map/ppermute | solution.py:29
  66.7 41.7 %collective-permute-start.2 = (bf16[128,2048]{1,0:T(8,128)(2,1)S(1)}, bf16[128,2048]{1,0:T(8,128)(2,1)}, u32[]{:S(2)}, u32[]{:S(2)}) collective-permute-start(bf16[128,2048]{1,0:T(8,128)(2,1)S(1)} %bitcast.255), channel_id=1, source_target_pairs={{0,1},{1,0},{2,3},{3,2},{4,5},{5,4},{6,7},{7,6},{8,9},{9,8},{10,11... | collective-permute-start | bytes 1572872 | tf_op jit(solution)/shard_map/ppermute | solution.py:29
  70.3 4.2 collective-permute-start.5
  108.4 71.8 %all-to-all-start.1 = ((bf16[4,512,1408]{2,1,0:T(8,128)(2,1)}), bf16[4,512,1408]{2,1,0:T(8,128)(2,1)}, u32[]{:S(2)}, u32[]{:S(2)}) async-start(bf16[4,512,1408]{2,1,0:T(8,128)(2,1)} %pad_maximum_fusion), calls=%async_computation.1 | async-start | bytes 11534336 | tf_op jit(solution)/shard_map/all_to_all | solution.py:42
  113.6 91.8 %all-gather.10.cloned.1.call-start = ((), (), s32[]{:S(2)}) async-start(), calls=%async_computation.17 | async-start | bytes 2621440 | tf_op jit(solution)/shard_map/all_gather | solution.py:408
  120.2 130.7 %all-gather.8.cloned.1.call-start = ((), (), s32[]{:S(2)}) async-start(), calls=%async_computation.16 | async-start | bytes 2621440 | tf_op jit(solution)/shard_map/all_gather | solution.py:470
  123.0 79.6 %copy-start.49 = (f32[2048]{0:T(1024)}, f32[2048]{0:T(1024)S(1)}, u32[]{:S(2)}) copy-start(f32[2048]{0:T(1024)S(1)} %get-tuple-element.155) | copy-start | bytes 24580
  153.0 47.5 %collective-permute-start.12 = (bf16[128,2048]{1,0:T(8,128)(2,1)}, bf16[128,2048]{1,0:T(8,128)(2,1)}, u32[]{:S(2)}, u32[]{:S(2)}) collective-permute-start(bf16[128,2048]{1,0:T(8,128)(2,1)} %get-tuple-element.186), channel_id=1, source_target_pairs={{0,1},{1,0},{2,3},{3,2},{4,5},{5,4},{6,7},{7,6},{8,9},{9,8},{10,11... | collective-permute-start | bytes 1572872 | tf_op jit(solution)/shard_map/ppermute | solution.py:29
  154.6 45.9 %collective-permute-start.14 = (bf16[128,2048]{1,0:T(8,128)(2,1)}, bf16[128,2048]{1,0:T(8,128)(2,1)}, u32[]{:S(2)}, u32[]{:S(2)}) collective-permute-start(bf16[128,2048]{1,0:T(8,128)(2,1)} %get-tuple-element.187), channel_id=1, source_target_pairs={{0,3},{1,2},{2,1},{3,0},{4,7},{5,6},{6,5},{7,4},{8,11},{9,10},{10,... | collective-permute-start | bytes 1572872 | tf_op jit(solution)/shard_map/ppermute | solution.py:29
  156.0 44.6 %collective-permute-start.13 = (bf16[128,2048]{1,0:T(8,128)(2,1)}, bf16[128,2048]{1,0:T(8,128)(2,1)}, u32[]{:S(2)}, u32[]{:S(2)}) collective-permute-start(bf16[128,2048]{1,0:T(8,128)(2,1)} %get-tuple-element.188), channel_id=1, source_target_pairs={{0,2},{1,3},{2,0},{3,1},{4,6},{5,7},{6,4},{7,5},{8,10},{9,11},{10,... | collective-permute-start | bytes 1572872 | tf_op jit(solution)/shard_map/ppermute | solution.py:29
  204.5 14.3 %collective-permute-start.15 = (bf16[1408,1024]{1,0:T(8,128)(2,1)}, bf16[1408,1024]{1,0:T(8,128)(2,1)}, u32[]{:S(2)}, u32[]{:S(2)}) collective-permute-start(bf16[1408,1024]{1,0:T(8,128)(2,1)} %bitcast.45), channel_id=1, source_target_pairs={{0,4},{4,0},{1,5},{5,1},{2,6},{6,2},{3,7},{7,3},{8,12},{12,8},{9,1... | collective-permute-start | bytes 8650760 | tf_op jit(solution)/shard_map/ppermute | solution.py:29
  211.5 53.6 %all-to-all-start.2 = ((bf16[4,256,2048]{2,1,0:T(8,128)(2,1)}), bf16[4,256,2048]{2,1,0:T(8,128)(2,1)}, u32[]{:S(2)}, u32[]{:S(2)}) async-start(bf16[4,256,2048]{2,1,0:T(8,128)(2,1)} %bitcast.259), calls=%async_computation.2 | async-start | bytes 8388608 | tf_op jit(solution)/shard_map/all_to_all | solution.py:42
  216.8 72.8 %collective-permute-start.16 = (bf16[2048,1408]{1,0:T(8,128)(2,1)}, bf16[2048,1408]{1,0:T(8,128)(2,1)}, u32[]{:S(2)}, u32[]{:S(2)}) collective-permute-start(bf16[2048,1408]{1,0:T(8,128)(2,1)} %bitcast.46.mine), channel_id=1, source_target_pairs={{0,4},{4,0},{1,5},{5,1},{2,6},{6,2},{3,7},{7,3},{8,12},{12,8},{9,1... | collective-permute-start | bytes 17301512 | tf_op jit(solution)/shard_map/ppermute | solution.py:29
  224.5 40.6 %copy-start.45 = (pred[4,4,64,4,128]{4,3,2,1,0:T(4,128)(4,1)S(1)}, pred[4,4,64,4,128]{4,3,2,1,0:T(4,128)(4,1)}, u32[]{:S(2)}) copy-start(pred[4,4,64,4,128]{4,3,2,1,0:T(4,128)(4,1)} %copy-done.44) | copy-start | bytes 1572868
  252.5 24.1 %collective-permute-start.17 = (bf16[64,1408]{1,0:T(8,128)(2,1)S(1)}, bf16[64,1408]{1,0:T(8,128)(2,1)S(1)}, u32[]{:S(2)}, u32[]{:S(2)}) collective-permute-start(bf16[64,1408]{1,0:T(8,128)(2,1)S(1)} %bitcast.290), channel_id=1, source_target_pairs={{0,8},{8,0},{16,24},{24,16},{1,9},{9,1},{17,25},{25,17},{2,10},{10... | collective-permute-start | bytes 540680 | tf_op jit(solution)/shard_map/ppermute | solution.py:29
  252.5 24.0 %collective-permute-start.18 = (bf16[64,1408]{1,0:T(8,128)(2,1)S(1)}, bf16[64,1408]{1,0:T(8,128)(2,1)S(1)}, u32[]{:S(2)}, u32[]{:S(2)}) collective-permute-start(bf16[64,1408]{1,0:T(8,128)(2,1)S(1)} %bitcast.289), channel_id=1, source_target_pairs={{0,16},{8,24},{16,0},{24,8},{1,17},{9,25},{17,1},{25,9},{2,18},{10... | collective-permute-start | bytes 540680 | tf_op jit(solution)/shard_map/ppermute | solution.py:29
  254.2 22.4 %collective-permute-start.19 = (bf16[64,1408]{1,0:T(8,128)(2,1)S(1)}, bf16[64,1408]{1,0:T(8,128)(2,1)S(1)}, u32[]{:S(2)}, u32[]{:S(2)}) collective-permute-start(bf16[64,1408]{1,0:T(8,128)(2,1)S(1)} %bitcast.288), channel_id=1, source_target_pairs={{0,24},{8,16},{16,8},{24,0},{1,25},{9,17},{17,9},{25,1},{2,26},{10... | collective-permute-start | bytes 540680 | tf_op jit(solution)/shard_map/ppermute | solution.py:29
  271.1 52.4 %all-to-all-start.3 = ((bf16[4,256,2048]{2,1,0:T(8,128)(2,1)}), bf16[4,256,2048]{2,1,0:T(8,128)(2,1)}, u32[]{:S(2)}, u32[]{:S(2)}) async-start(bf16[4,256,2048]{2,1,0:T(8,128)(2,1)} %bitcast.261), calls=%async_computation.3 | async-start | bytes 8388608 | tf_op jit(solution)/shard_map/all_to_all | solution.py:42
  275.9 107.4 %all-gather.12.cloned.1.call-start = ((), (), s32[]{:S(2)}) async-start(), calls=%async_computation.22 | async-start | bytes 10948608 | tf_op jit(solution)/shard_map/all_gather | solution.py:517
  277.8 45.8 %copy-start.17 = (bf16[128,2048]{0,1:T(8,128)(2,1)S(1)}, bf16[128,2048]{0,1:T(8,128)(2,1)}, u32[]{:S(2)}) copy-start(bf16[128,2048]{0,1:T(8,128)(2,1)} %copy-done.16) | copy-start | bytes 1572868
  374.7 55.5 %all-to-all-start.4 = ((bf16[4,256,2176]{2,1,0:T(8,128)(2,1)}), bf16[4,256,2176]{2,1,0:T(8,128)(2,1)}, u32[]{:S(2)}, u32[]{:S(2)}) async-start(bf16[4,256,2176]{2,1,0:T(8,128)(2,1)} %bitcast.226), calls=%async_computation.4 | async-start | bytes 8912896 | tf_op jit(solution)/shard_map/all_to_all | solution.py:42
  379.6 135.0 %reduce-scatter.7.cloned.1.call-start = ((), (), s32[]{:S(2)}) async-start(), calls=%async_computation.19 | async-start | bytes 2785280 | tf_op jit(solution)/shard_map/reduce_scatter | solution.py:557
  401.7 28.6 %copy-start.46 = (pred[4,4,64,4,128]{4,3,2,1,0:T(4,128)(4,1)S(1)}, pred[4,4,64,4,128]{4,3,2,1,0:T(4,128)(4,1)}, u32[]{:S(2)}) copy-start(pred[4,4,64,4,128]{4,3,2,1,0:T(4,128)(4,1)} %copy-done.44) | copy-start | bytes 1572868
  443.3 52.0 %all-to-all-start.5 = ((bf16[4,256,2048]{2,1,0:T(8,128)(2,1)}), bf16[4,256,2048]{2,1,0:T(8,128)(2,1)}, u32[]{:S(2)}, u32[]{:S(2)}) async-start(bf16[4,256,2048]{2,1,0:T(8,128)(2,1)} %bitcast.260), calls=%async_computation.5 | async-start | bytes 8388608 | tf_op jit(solution)/shard_map/all_to_all | solution.py:42
  448.2 328.3 %reduce-scatter.5.cloned.1.call-start = ((), (), s32[]{:S(2)}) async-start(), calls=%async_computation.18 | async-start | bytes 2621440 | tf_op jit(solution)/shard_map/reduce_scatter | solution.py:585
  470.9 108.1 %collective-permute-start.28 = (bf16[2048,1408]{1,0:T(8,128)(2,1)}, bf16[2048,1408]{1,0:T(8,128)(2,1)}, u32[]{:S(2)}, u32[]{:S(2)}) collective-permute-start(bf16[2048,1408]{1,0:T(8,128)(2,1)} %slice.300), channel_id=1, source_target_pairs={{0,4},{4,0},{1,5},{5,1},{2,6},{6,2},{3,7},{7,3},{8,12},{12,8},{9,1... | collective-permute-start | bytes 17301512 | tf_op jit(solution)/shard_map/ppermute | solution.py:29
  503.4 277.2 %reduce-scatter.11.cloned.1.call-start = ((), (), s32[]{:S(2)}) async-start(), calls=%async_computation.21 | async-start | bytes 2359296 | tf_op jit(solution)/shard_map/reduce_scatter | solution.py:622
  517.7 15.8 %collective-permute-start.22 = (bf16[128,2048]{1,0:T(8,128)(2,1)S(1)}, bf16[128,2048]{1,0:T(8,128)(2,1)S(1)}, u32[]{:S(2)}, u32[]{:S(2)}) collective-permute-start(bf16[128,2048]{1,0:T(8,128)(2,1)S(1)} %fusion.43), channel_id=1, source_target_pairs={{0,3},{1,2},{2,1},{3,0},{4,7},{5,6},{6,5},{7,4},{8,11},{9,10},{10,... | collective-permute-start | bytes 1572872 | tf_op jit(solution)/shard_map/ppermute | solution.py:29
  519.1 23.3 %collective-permute-start.21 = (bf16[128,2048]{1,0:T(8,128)(2,1)S(1)}, bf16[128,2048]{1,0:T(8,128)(2,1)S(1)}, u32[]{:S(2)}, u32[]{:S(2)}) collective-permute-start(bf16[128,2048]{1,0:T(8,128)(2,1)S(1)} %fusion.43), channel_id=1, source_target_pairs={{0,2},{1,3},{2,0},{3,1},{4,6},{5,7},{6,4},{7,5},{8,10},{9,11},{10,... | collective-permute-start | bytes 1572872 | tf_op jit(solution)/shard_map/ppermute | solution.py:29
  520.6 22.0 %collective-permute-start.20 = (bf16[128,2048]{1,0:T(8,128)(2,1)S(1)}, bf16[128,2048]{1,0:T(8,128)(2,1)S(1)}, u32[]{:S(2)}, u32[]{:S(2)}) collective-permute-start(bf16[128,2048]{1,0:T(8,128)(2,1)S(1)} %fusion.43), channel_id=1, source_target_pairs={{0,1},{1,0},{2,3},{3,2},{4,5},{5,4},{6,7},{7,6},{8,9},{9,8},{10,11... | collective-permute-start | bytes 1572872 | tf_op jit(solution)/shard_map/ppermute | solution.py:29
  523.0 21.1 %copy-start.2 = (bf16[512,512]{1,0:T(8,128)(2,1)S(1)}, bf16[512,512]{1,0:T(8,128)(2,1)}, u32[]{:S(2)}) copy-start(bf16[512,512]{1,0:T(8,128)(2,1)} %copy-done.1) | copy-start | bytes 1572868
  523.0 21.1 %copy-start.4 = (bf16[512,512]{1,0:T(8,128)(2,1)S(1)}, bf16[512,512]{1,0:T(8,128)(2,1)}, u32[]{:S(2)}) copy-start(bf16[512,512]{1,0:T(8,128)(2,1)} %copy-done.3) | copy-start | bytes 1572868
  523.0 21.1 %copy-start.6 = (bf16[512,512]{1,0:T(8,128)(2,1)S(1)}, bf16[512,512]{1,0:T(8,128)(2,1)}, u32[]{:S(2)}) copy-start(bf16[512,512]{1,0:T(8,128)(2,1)} %copy-done.5) | copy-start | bytes 1572868
  523.0 21.1 %copy-start.8 = (bf16[512,512]{1,0:T(8,128)(2,1)S(1)}, bf16[512,512]{1,0:T(8,128)(2,1)}, u32[]{:S(2)}) copy-start(bf16[512,512]{1,0:T(8,128)(2,1)} %copy-done.7) | copy-start | bytes 1572868
  523.0 33.7 %collective-permute-start.27 = (bf16[1408,1024]{1,0:T(8,128)(2,1)}, bf16[1408,1024]{1,0:T(8,128)(2,1)}, u32[]{:S(2)}, u32[]{:S(2)}) collective-permute-start(bf16[1408,1024]{1,0:T(8,128)(2,1)} %broadcast_select_fusion), channel_id=1, source_target_pairs={{0,4},{4,0},{1,5},{5,1},{2,6},{6,2},{3,7},{7,3},{8,12},{12,8},{9,1... | collective-permute-start | bytes 8650760 | tf_op jit(solution)/shard_map/ppermute | solution.py:29
  564.0 39.2 %all-to-all-start.7 = ((bf16[4,352,1024]{2,1,0:T(8,128)(2,1)}), bf16[4,352,1024]{2,1,0:T(8,128)(2,1)}, u32[]{:S(2)}, u32[]{:S(2)}) async-start(bf16[4,352,1024]{2,1,0:T(8,128)(2,1)} %bitcast.240), calls=%async_computation.11 | async-start | bytes 5767168 | tf_op jit(solution)/shard_map/all_to_all | solution.py:42
  568.6 213.6 %reduce-scatter.9.cloned.1.call-start = ((), (), s32[]{:S(2)}) async-start(), calls=%async_computation.20 | async-start | bytes 7667712 | tf_op jit(solution)/shard_map/reduce_scatter | solution.py:625
  603.2 69.6 %all-to-all-start.8 = ((bf16[4,512,1408]{2,1,0:T(8,128)(2,1)}), bf16[4,512,1408]{2,1,0:T(8,128)(2,1)}, u32[]{:S(2)}, u32[]{:S(2)}) async-start(bf16[4,512,1408]{2,1,0:T(8,128)(2,1)} %bitcast.236), calls=%async_computation.12 | async-start | bytes 11534336 | tf_op jit(solution)/shard_map/all_to_all | solution.py:42
  618.0 59.2 %collective-permute-start.29 = (bf16[4,256,1408]{2,1,0:T(8,128)(2,1)}, bf16[4,256,1408]{2,1,0:T(8,128)(2,1)}, u32[]{:S(2)}, u32[]{:S(2)}) collective-permute-start(bf16[4,256,1408]{2,1,0:T(8,128)(2,1)} %select_bitcast_fusion), channel_id=1, source_target_pairs={{0,4},{4,0},{1,5},{5,1},{2,6},{6,2},{3,7},{7,3},{8,12},{12,8},{9,1... | collective-permute-start | bytes 8650760 | tf_op jit(solution)/shard_map/ppermute | solution.py:29
  619.9 5.8 collective-permute-start.33
  672.8 22.4 %all-to-all-start.10 = ((bf16[4,1,88,2048]{3,2,1,0:T(8,128)(2,1)}), bf16[4,1,88,2048]{3,2,1,0:T(8,128)(2,1)}, u32[]{:S(2)}, u32[]{:S(2)}) async-start(bf16[4,1,88,2048]{3,2,1,0:T(8,128)(2,1)} %bitcast.250), calls=%async_computation.14 | async-start | bytes 2883584 | tf_op jit(solution)/shard_map/all_to_all | solution.py:42
  695.2 47.6 %all-to-all-start.9 = ((bf16[4,4,64,1408]{3,2,1,0:T(8,128)(2,1)}), bf16[4,4,64,1408]{3,2,1,0:T(8,128)(2,1)}, u32[]{:S(2)}, u32[]{:S(2)}) async-start(bf16[4,4,64,1408]{3,2,1,0:T(8,128)(2,1)} %copy.201), calls=%async_computation.13 | async-start | bytes 5767168 | tf_op jit(solution)/shard_map/all_to_all | solution.py:42
  712.2 56.3 %collective-permute-start.23 = (bf16[128,2048]{1,0:T(8,128)(2,1)}, bf16[128,2048]{1,0:T(8,128)(2,1)S(1)}, u32[]{:S(2)}, u32[]{:S(2)}) collective-permute-start(bf16[128,2048]{1,0:T(8,128)(2,1)} %get-tuple-element.183), channel_id=1, source_target_pairs={{0,1},{1,0},{2,3},{3,2},{4,5},{5,4},{6,7},{7,6},{8,9},{9,8},{10,11... | collective-permute-start | bytes 1572872 | tf_op jit(solution)/shard_map/ppermute | solution.py:29
  714.2 54.3 %collective-permute-start.25 = (bf16[128,2048]{1,0:T(8,128)(2,1)}, bf16[128,2048]{1,0:T(8,128)(2,1)S(1)}, u32[]{:S(2)}, u32[]{:S(2)}) collective-permute-start(bf16[128,2048]{1,0:T(8,128)(2,1)} %get-tuple-element.184), channel_id=1, source_target_pairs={{0,3},{1,2},{2,1},{3,0},{4,7},{5,6},{6,5},{7,4},{8,11},{9,10},{10,... | collective-permute-start | bytes 1572872 | tf_op jit(solution)/shard_map/ppermute | solution.py:29
  715.6 52.9 %collective-permute-start.24 = (bf16[128,2048]{1,0:T(8,128)(2,1)}, bf16[128,2048]{1,0:T(8,128)(2,1)S(1)}, u32[]{:S(2)}, u32[]{:S(2)}) collective-permute-start(bf16[128,2048]{1,0:T(8,128)(2,1)} %get-tuple-element.185), channel_id=1, source_target_pairs={{0,2},{1,3},{2,0},{3,1},{4,6},{5,7},{6,4},{7,5},{8,10},{9,11},{10,... | collective-permute-start | bytes 1572872 | tf_op jit(solution)/shard_map/ppermute | solution.py:29
  745.0 18.7 %collective-permute-start.32 = (bf16[64,1408]{1,0:T(8,128)(2,1)S(1)}, bf16[64,1408]{1,0:T(8,128)(2,1)S(1)}, u32[]{:S(2)}, u32[]{:S(2)}) collective-permute-start(bf16[64,1408]{1,0:T(8,128)(2,1)S(1)} %get-tuple-element.197), channel_id=1, source_target_pairs={{0,24},{8,16},{16,8},{24,0},{1,25},{9,17},{17,9},{25,1},{2,26},{10... | collective-permute-start | bytes 540680 | tf_op jit(solution)/shard_map/ppermute | solution.py:29
  747.6 7.8 collective-permute-start.30
  755.3 8.3 %collective-permute-start.31 = (bf16[64,1408]{1,0:T(8,128)(2,1)S(1)}, bf16[64,1408]{1,0:T(8,128)(2,1)S(1)}, u32[]{:S(2)}, u32[]{:S(2)}) collective-permute-start(bf16[64,1408]{1,0:T(8,128)(2,1)S(1)} %get-tuple-element.198), channel_id=1, source_target_pairs={{0,16},{8,24},{16,0},{24,8},{1,17},{9,25},{17,1},{25,9},{2,18},{10... | collective-permute-start | bytes 540680 | tf_op jit(solution)/shard_map/ppermute | solution.py:29
  763.7 7.0 collective-permute-start.35
  763.7 24.3 %collective-permute-start.34 = (bf16[2,512,1408]{2,1,0:T(8,128)(2,1)}, bf16[2,512,1408]{2,1,0:T(8,128)(2,1)}, u32[]{:S(2)}, u32[]{:S(2)}) collective-permute-start(bf16[2,512,1408]{2,1,0:T(8,128)(2,1)} %broadcast_select_fusion.3), channel_id=1, source_target_pairs={{0,4},{4,0},{1,5},{5,1},{2,6},{6,2},{3,7},{7,3},{8,12},{12,8},{9,1... | collective-permute-start | bytes 8650760 | tf_op jit(solution)/shard_map/ppermute | solution.py:29
  780.6 16.2 %collective-permute-start.26 = (bf16[64,2048]{1,0:T(8,128)(2,1)}, bf16[64,2048]{1,0:T(8,128)(2,1)S(1)}, u32[]{:S(2)}, u32[]{:S(2)}) collective-permute-start(bf16[64,2048]{1,0:T(8,128)(2,1)} %reduce-scatter.11.cloned.1.call-done), channel_id=1, source_target_pairs={{0,0},{4,1},{8,2},{12,3},{16,4},{20,5},{24,6},{28,7},{1,8},{5,9},{... | collective-permute-start | bytes 786440 | tf_op jit(solution)/shard_map/ppermute | solution.py:624
  782.2 21.2 %all-to-all-start.6 = ((bf16[4,64,1664]{2,1,0:T(8,128)(2,1)}), bf16[4,64,1664]{2,1,0:T(8,128)(2,1)S(1)}, u32[]{:S(2)}, u32[]{:S(2)}) async-start(bf16[4,64,1664]{2,1,0:T(8,128)(2,1)} %bitcast.278), calls=%async_computation.9 | async-start | bytes 1703936 | tf_op jit(solution)/shard_map/all_to_all | solution.py:42
  (57 other events, 233.8 us)
Sparse Core Ops, SparseCore 0:
  32.6 87.5 all-gather.5
  121.7 44.3 all-gather.9
  205.5 45.3 all-gather.7
  323.6 59.5 all-gather.11
  443.4 44.6 reduce-scatter.6
  503.5 42.9 reduce-scatter.4
  556.9 35.8 reduce-scatter.10
  595.2 73.3 reduce-scatter.8

commit v3 on v2

--- a/solution.py
+++ b/solution.py
@@ -573,18 +573,10 @@
         grad_w = dot(slots_late.T, grad_in).astype(LOW)
 
         routed_back = collect(after(routed, grad_routed))
-        grad_sin = dot(second_late.T, dsab).astype(LOW)
         grad_down = dot(weighted.T, dy_slots).astype(LOW)
+        grad_second, grad_w = lax.optimization_barrier((grad_second, grad_w))
+        routed_back, grad_down = lax.optimization_barrier((routed_back, grad_down))
         down_sums = low_total(both_parts(*column_halves(grad_down)))
-        sin_sums = shared_home(grad_sin.reshape(columns, cores * blocks * part, 2 * hidden))
-        in_sums = both_parts(grad_w[:, :wide], grad_w[:, wide:])
-        in_sums = low_total(in_sums)
-        sin_sums = by_owner(low_total(sin_sums))
-        layer_sent = (dot(shared_low, mat_sdown) + dot(spread.T, routed_back)).astype(LOW)
-        down_back = line_s.trade(send_home(down_sums))
-        layer_out = lax.psum_scatter(layer_sent, Z, scatter_dimension=0, tiled=True)
-        grad_sdown = dot(shared_low.T, after(dy_late, second_sent)).astype(LOW)
-        sdown_sums = by_owner(low_total(shared_home(grad_sdown[None])))
 
         dprobs = grad_second[:, width : width + experts]
         dprobs = dprobs + grad_second[:, width + 64 : width + 64 + experts]
@@ -597,34 +589,52 @@
         grad_gain_second = jnp.sum(grad_second * second_normed, axis=0, keepdims=True)
         dy = dy_low.astype(F32)
         grad_after = dy + norm_back(grad_second, second_normed, second_scale, gain_second)
-        grad_after_low = grad_after.astype(LOW)
+        grad_after_low, routed_back = lax.optimization_barrier(
+            (grad_after.astype(LOW), routed_back)
+        )
         grad_after_low = jnp.concatenate(line_t.share(grad_after_low), axis=0)
-        in_back = line_s.trade(send_home(in_sums))
-        sin_back = line_t.trade(sin_sums)
-
         grad_made, grad_outmat = attention_back(grad_after_low, out_mat, kept, tables, extra)
-        down_back, in_back, sin_back = after((down_back, in_back, sin_back), grad_made)
-        layer_out = after_attn + layer_out.astype(F32)
         small_grads = jnp.concatenate([grad_router_t, grad_gain_second], axis=0).T
         small_grads = jnp.pad(small_grads, ((0, 0), (3 * span, extra - experts - 1)))
         grad_qkv = (dot(normed_low.T, grad_made) + small_grads).astype(LOW)
         grad_first = dot(grad_made, attn_mat[:, : 3 * span + extra].T).astype(LOW).reshape(blocks, rows, width)
+        grad_w_other = line_k.swap(grad_w[:, wide:], 1)
+        grad_qkv, grad_first, dsab, grad_w, grad_w_other = lax.optimization_barrier(
+            (grad_qkv, grad_first, dsab, grad_w, grad_w_other)
+        )
+        in_back = line_s.trade(send_home(low_total([grad_w[:, :wide], grad_w_other])))
         grad_first = total(line_t.give([grad_first[i] for i in range(blocks)]))
+        grad_first, dsab, routed_back = lax.optimization_barrier((grad_first, dsab, routed_back))
+        layer_sent = (dot(shared_low, mat_sdown) + dot(spread.T, routed_back)).astype(LOW)
+        layer_out = lax.psum_scatter(layer_sent, Z, scatter_dimension=0, tiled=True)
+        layer_out = after_attn + layer_out.astype(F32)
+        grad_sin = dot(second_late.T, dsab).astype(LOW)
+        grad_sdown = dot(shared_low.T, dy_late).astype(LOW)
+        sin_sums = shared_home(grad_sin.reshape(columns, cores * blocks * part, 2 * hidden))
+        sin_sums = by_owner(low_total(sin_sums))
+        sdown_sums = by_owner(low_total(shared_home(grad_sdown[None])))
         local_normed = first_normed[:rows]
         grad_inputs = grad_after + norm_back(
             grad_first, local_normed, first_scale[:rows], gain_first
         )
 
-        grad_edown = side_by_side(*home(down_back)).astype(F32)
-        kept, came = home(in_back)
-        grad_egate = jnp.where(first, kept, came).astype(F32)
-        grad_eup = jnp.where(first, came, kept).astype(F32)
         grad_outmat = lax.psum_scatter(grad_outmat, (Z, K), scatter_dimension=0, tiled=True)
         back = [(there, here) for here, there in move]
         grad_outmat = lax.ppermute(grad_outmat, (Z, K, C, D), back).astype(F32)
         grad_qkv = lax.psum_scatter(grad_qkv, (Z, K), scatter_dimension=0, tiled=True)
+        grad_qkv, in_back = lax.optimization_barrier((grad_qkv, in_back))
         grad_qkv = line_t.trade(grad_qkv.reshape(blocks, part, 3 * span + extra))
+        kept, came = home(in_back)
+        grad_egate = jnp.where(first, kept, came).astype(F32)
+        grad_eup = jnp.where(first, came, kept).astype(F32)
+        grad_qkv, down_sums, sin_sums, sdown_sums = lax.optimization_barrier(
+            (grad_qkv, down_sums, sin_sums, sdown_sums)
+        )
+        sin_back = line_t.trade(sin_sums)
+        sin_back, down_sums, sdown_sums = lax.optimization_barrier((sin_back, down_sums, sdown_sums))
         sdown_back = line_t.trade(sdown_sums)
+        down_back = line_s.trade(send_home(down_sums))
+        grad_edown = side_by_side(*home(down_back)).astype(F32)
         grad_sin = total([sin_back[i] for i in range(blocks)]).astype(LOW)
         grad_sin = settle(line_z.give_from(grad_sin), col)
         grad_sin = grad_sin.transpose(1, 0, 2).astype(F32)

time: 830 us -> 826 us (level)
  waiting for transfers between devices: 348 us -> 325 us
  local copies, waits for them, and re-layouts: 61.9 us -> 72.3 us
  other arithmetic: 102 us -> 111 us
    all_to_all x11, waiting for transfers between devices: 214 us -> 159 us  [trade(): lax.all_to_all(blocks, self.names, split_axis=0, concat_axis=0, tiled=True)]
    reduce_scatter x1, waiting for transfers between devices: 0.01 us -> 18 us  [body(): layer_out = lax.psum_scatter(layer_sent, Z, scatter_dimension=0, tiled=True)]
    unnamed x141 -> x139, local copies, waits for them, and re-layouts: 22.8 us -> 18.1 us
  transfers between devices with their start and end apart: 55 -> 55, of which waited for: 27 -> 30; matrix products, arithmetic and copies ran while one was open for 28% -> 31% of each run, Pallas kernels for 9% -> 9%
where the time goes in v3:
time: 826 us; the launch traced here: 816 us
  waiting for transfers between devices  325 us (39%)
  matrix products  120 us (15%)
  other arithmetic  111 us (13%)
  starting transfers between devices  91.5 us (11%)
  local copies, waits for them, and re-layouts  72.3 us (9%)
  Pallas kernels  72.2 us (9%)
  between operations  23.8 us (3%)
    all_to_all x11, waiting for transfers between devices, trade(): lax.all_to_all(blocks, self.names, split_axis=0, concat_axis=0, tiled=True)  159 us
    dot_general x20, matrix products, dot(): return jnp.dot(left, right, preferred_element_type=F32)  120 us
    ppermute x34, waiting for transfers between devices, swap(): lax.ppermute(value, self.names, [(i, i ^ delta) for i in range(self.size)])  110 us
    all_to_all x11, starting transfers between devices, trade(): lax.all_to_all(blocks, self.names, split_axis=0, concat_axis=0, tiled=True)  53.6 us
    ppermute x34, starting transfers between devices, swap(): lax.ppermute(value, self.names, [(i, i ^ delta) for i in range(self.size)])  35 us
    all_gather x1, waiting for transfers between devices, body(): second_col = lax.all_gather(second_low, Z, axis=0, tiled=True)  26.7 us
    pallas_call x1, Pallas kernels, expert_forward(): pl.pallas_call(expert_kernel, grid=(wide // tile,), in_specs=[pl.BlockSpe...  25.3 us
    convert_element_type x4, other arithmetic, low_total(): return total(pieces).astype(LOW)  25.1 us
  transfers between devices with their start and end apart: 55, of which 30 were waited for; matrix products, arithmetic and copies ran while one was open for 31% of the time, Pallas kernels for 9%

profile of v3, /device:TPU:0, one launch (start us, length us, event | category | flops | bytes accessed | tf_op | source)
XLA Modules:
  0.0 816.3 jit_solution(3611100907196207121)
XLA Ops:
  25.1 7.7 collective-permute-done.10
  37.1 6.2 collective-permute-done
  45.4 4.7 all-to-all-start
  67.5 3.4 broadcast_select_fusion.6
  76.6 20.0 %collective-permute-done.2 = bf16[128,2048]{1,0:T(8,128)(2,1)} collective-permute-done((bf16[128,2048]{1,0:T(8,128)(2,1)S(1)}, bf16[128,2048]{1,0:T(8,128)(2,1)}, u32[]{:S(2)}, u32[]{:S(2)}) %collective-permute-start.2) | collective-permute-done | bytes 524320 | tf_op jit(solution)/shard_map/ppermute | solution.py:29
  96.8 11.4 %collective-permute-done.4 = bf16[128,2048]{1,0:T(8,128)(2,1)} collective-permute-done((bf16[128,2048]{1,0:T(8,128)(2,1)S(1)}, bf16[128,2048]{1,0:T(8,128)(2,1)}, u32[]{:S(2)}, u32[]{:S(2)}) %collective-permute-start.4) | collective-permute-done | bytes 524320 | tf_op jit(solution)/shard_map/ppermute | solution.py:29
  108.2 5.2 all-to-all-start.1
  117.2 4.9 all-gather.6.cloned.1.call-done.w_q.w_k.w_v
  125.0 4.1 convert_multiply_fusion
  134.4 16.1 %shard_map.280 = (bf16[512,512]{1,0:T(8,128)(2,1)S(1)}, bf16[512,512]{1,0:T(8,128)(2,1)S(1)}, bf16[512,512]{1,0:T(8,128)(2,1)S(1)}, bf16[512,512]{1,0:T(8,128)(2,1)S(1)}, bf16[512,2048]{1,0:T(8,128)(2,1)S(1)}) custom-call(bf16[512,2048]{1,0:T(8,128)(2,1)} %get-tuple-element.217.normed, bf16[2048,2176]{1,0:T(8,128)(2,1)} %all-gather.6.cloned.1.call-done.w_q.w_k.w_v, ...), custom_call_target="tpu_custom_call" | custom-call | flops 4831838208 | bytes 14680064 | tf_op jit(solution)/shard_map/pallas_call | solution.py:141
  159.9 19.1 %all-to-all-done.1 = bf16[4,512,1408]{2,1,0:T(8,128)(2,1)} async-done(((bf16[4,512,1408]{2,1,0:T(8,128)(2,1)}), bf16[4,512,1408]{2,1,0:T(8,128)(2,1)}, u32[]{:S(2)}, u32[]{:S(2)}) %all-to-all-start.1) | async-done | bytes 5767200 | tf_op jit(solution)/shard_map/all_to_all | solution.py:42
  179.1 10.2 %collective-permute-done.12 = bf16[128,2048]{1,0:T(8,128)(2,1)} collective-permute-done((bf16[128,2048]{1,0:T(8,128)(2,1)}, bf16[128,2048]{1,0:T(8,128)(2,1)}, u32[]{:S(2)}, u32[]{:S(2)}) %collective-permute-start.12) | collective-permute-done | bytes 524320 | tf_op jit(solution)/shard_map/ppermute | solution.py:29
  190.3 10.8 %collective-permute-done.14 = bf16[128,2048]{1,0:T(8,128)(2,1)} collective-permute-done((bf16[128,2048]{1,0:T(8,128)(2,1)}, bf16[128,2048]{1,0:T(8,128)(2,1)}, u32[]{:S(2)}, u32[]{:S(2)}) %collective-permute-start.14) | collective-permute-done | bytes 524320 | tf_op jit(solution)/shard_map/ppermute | solution.py:29
  205.9 6.1 convolution_convert_fusion.4
  212.0 5.6 all-to-all-start.2
  219.6 5.7 broadcast_select_fusion.2
  225.3 26.7 %all-gather.8.cloned.1.call-done = bf16[512,2048]{1,0:T(8,128)(2,1)} async-done(((bf16[128,2048]{1,0:T(8,128)(2,1)}), bf16[512,2048]{1,0:T(8,128)(2,1)}) %all-gather.8.cloned.1.call-update) | async-done | bytes 2097168 | tf_op jit(solution)/shard_map/all_gather | solution.py:470
  258.2 7.7 all-to-all-done.2
  265.9 5.9 convolution_convert_fusion.3
  271.8 4.9 all-to-all-start.3
  278.1 11.9 %fusion.5.raw = f32[1024,1408]{1,0:T(8,128)} fusion(bf16[1024,2048]{1,0:T(8,128)(2,1)} %bitcast.42, bf16[1408,1024]{1,0:T(8,128)(2,1)} %get-tuple-element.208, bf16[1408,1024]{1,0:T(8,128)(2,1)} %get-tuple-element.207), kind=kOutput, calls=%fused_computation.23 | convolution fusion | flops 5917114368 | bytes 15728640 | tf_op jit(solution)/shard_map/dot_general | solution.py:67
  290.0 34.3 %all-to-all-done.3 = bf16[4,256,2048]{2,1,0:T(8,128)(2,1)} async-done(((bf16[4,256,2048]{2,1,0:T(8,128)(2,1)}), bf16[4,256,2048]{2,1,0:T(8,128)(2,1)}, u32[]{:S(2)}, u32[]{:S(2)}) %all-to-all-start.3) | async-done | bytes 4194336 | tf_op jit(solution)/shard_map/all_to_all | solution.py:42
  325.0 3.4 fusion.54
  331.3 25.3 %shard_map.281 = (bf16[1024,1408]{1,0:T(8,128)(2,1)S(1)}, bf16[1024,2816]{1,0:T(8,128)(2,1)}, f32[1024,1]{1,0:T(8,128)S(1)}) custom-call(s32[2]{0:T(128)S(1)} %pad_add_fusion.2.flag, bf16[1024,2048]{1,0:T(8,128)(2,1)} %bitcast.44.slots, bf16[2048,1408]{1,0:T(8,128)(2,1)} %bitcast.46.mine, bf16[2048,1408]{1,0:T(8,128)(2,1)} %collective-permute-done.16.other, ...), custom_call_target="tpu_custom_call" | custom-call | flops 11811160064 | bytes 30146560 | tf_op jit(solution)/shard_map/pallas_call | solution.py:269
  358.2 17.9 %shard_map.282 = bf16[1024,2176]{1,0:T(8,128)(2,1)S(1)} custom-call(s32[2]{0:T(128)S(1)} %pad_add_fusion.2.flag, bf16[1024,2816]{1,0:T(8,128)(2,1)} %get-tuple-element.90.grads, bf16[2048,1408]{1,0:T(8,128)(2,1)} %bitcast.46.mine, bf16[2048,1408]{1,0:T(8,128)(2,1)} %collective-permute-done.16.other, f32[1024,1]{1,0:T(8,128)S(1)} %get-tuple-element.91.dgate), custom_call_target="tpu_custom_call" | custom-call | flops 11811160064 | bytes 21495808 | tf_op jit(solution)/shard_map/pallas_call | solution.py:316
  378.2 5.1 all-to-all-start.4
  394.6 3.4 fusion.57
  403.6 8.4 %multiply_convert_fusion = bf16[1024,2048]{1,0:T(8,128)(2,1)} fusion(bf16[1024,1408]{1,0:T(8,128)(2,1)S(1)} %copy-done.10, f32[1024]{0:T(1024)S(1)} %get-tuple-element.195, bf16[1408,1024]{1,0:T(8,128)(2,1)S(1)} %copy-done.29, bf16[1408,1024]{1,0:T(8,128)(2,1)S(1)} %copy-done.28), kind=kOutput, calls=%fused_computation.3 | convolution fusion | flops 5921308672 | bytes 12849152 | tf_op jit(solution)/shard_map/dot_general | solution.py:67
  412.0 21.5 %all-to-all-done.4 = bf16[4,256,2176]{2,1,0:T(8,128)(2,1)} async-done(((bf16[4,256,2176]{2,1,0:T(8,128)(2,1)}), bf16[4,256,2176]{2,1,0:T(8,128)(2,1)}, u32[]{:S(2)}, u32[]{:S(2)}) %all-to-all-start.4) | async-done | bytes 4456480 | tf_op jit(solution)/shard_map/all_to_all | solution.py:42
  433.5 5.1 fusion.13
  438.6 7.7 fusion.4
  446.3 4.9 all-to-all-start.5
  454.5 10.7 %convolution_convert_fusion.2 = bf16[1408,2048]{1,0:T(8,128)(2,1)} fusion(bf16[1024,2048]{1,0:T(8,128)(2,1)} %bitcast.42, bf16[1024,1408]{1,0:T(8,128)(2,1)} %copy-done.9, f32[1024]{0:T(1024)S(1)} %get-tuple-element.195), kind=kOutput, calls=%fused_computation.5 | convolution fusion | flops 5912788992 | bytes 12849152 | tf_op jit(solution)/shard_map/dot_general | solution.py:67
  465.2 18.3 %convolution_convert_fusion = bf16[2048,2816]{1,0:T(8,128)(2,1)} fusion(bf16[1024,2048]{1,0:T(8,128)(2,1)} %bitcast.44.slots, bf16[1024,2816]{1,0:T(8,128)(2,1)} %get-tuple-element.90.grads), kind=kOutput, calls=%fused_computation.2 | convolution fusion | flops 11816927232 | bytes 21495808 | tf_op jit(solution)/shard_map/dot_general | solution.py:67
  483.5 14.5 %all-to-all-done.5 = bf16[4,256,2048]{2,1,0:T(8,128)(2,1)} async-done(((bf16[4,256,2048]{2,1,0:T(8,128)(2,1)}), bf16[4,256,2048]{2,1,0:T(8,128)(2,1)}, u32[]{:S(2)}, u32[]{:S(2)}) %all-to-all-start.5) | async-done | bytes 4194336 | tf_op jit(solution)/shard_map/all_to_all | solution.py:42
  498.0 5.0 reduce-scatter.5.cloned.1.call-done
  504.9 6.0 slice.233
  514.9 10.8 %collective-permute-done.20 = bf16[128,2048]{1,0:T(8,128)(2,1)S(1)} collective-permute-done((bf16[128,2048]{1,0:T(8,128)(2,1)S(1)}, bf16[128,2048]{1,0:T(8,128)(2,1)S(1)}, u32[]{:S(2)}, u32[]{:S(2)}) %collective-permute-start.20) | collective-permute-done | bytes 524320 | tf_op jit(solution)/shard_map/ppermute | solution.py:29
  527.7 10.5 %collective-permute-done.22 = bf16[128,2048]{1,0:T(8,128)(2,1)S(1)} collective-permute-done((bf16[128,2048]{1,0:T(8,128)(2,1)S(1)}, bf16[128,2048]{1,0:T(8,128)(2,1)S(1)}, u32[]{:S(2)}, u32[]{:S(2)}) %collective-permute-start.22) | collective-permute-done | bytes 524320 | tf_op jit(solution)/shard_map/ppermute | solution.py:29
  539.6 12.8 %shard_map.283 = (bf16[512,1664]{1,0:T(8,128)(2,1)S(1)}, bf16[512,2048]{1,0:T(8,128)(2,1)}) custom-call(bf16[512,2048]{1,0:T(8,128)(2,1)} %pad_maximum_fusion.8.grad_out, bf16[512,2048]{1,0:T(8,128)(2,1)} %bitcast.257, bf16[512,512]{1,0:T(8,128)(2,1)S(1)} %copy-done.2, bf16[512,512]{1,0:T(8,128)(2,1)S(1)} %copy-done.4, bf16[512,512]{1,0:T(8,128)(2,1)S(1)} %copy-done.6, ...), custom_call_target="tpu_custom_call" | custom-call | flops 3489660928 | bytes 9961472 | tf_op jit(solution)/shard_map/pallas_call | solution.py:214
  554.2 8.4 %add_convert_fusion = bf16[2048,1664]{1,0:T(8,128)(2,1)} fusion(f32[2048,17]{1,0:T(8,128)S(1)} %bitcast.291, bf16[512,2048]{1,0:T(8,128)(2,1)} %get-tuple-element.217.normed, bf16[512,1664]{1,0:T(8,128)(2,1)S(1)} %get-tuple-element.109), kind=kOutput, calls=%fused_computation | convolution fusion | flops 3496476672 | bytes 10756096 | tf_op jit(solution)/shard_map/dot_general | solution.py:67
  562.6 8.2 %fusion.6 = bf16[512,2048]{1,0:T(8,128)(2,1)} fusion(bf16[512,1664]{1,0:T(8,128)(2,1)S(1)} %get-tuple-element.109, bf16[2048,2176]{1,0:T(8,128)(2,1)} %all-gather.6.cloned.1.call-done.w_q.w_k.w_v), kind=kOutput, calls=%fused_computation.25 | convolution fusion | flops 3490709504 | bytes 10616832 | tf_op jit(solution)/shard_map/dot_general | solution.py:67
  570.9 3.7 convolution_convert_fusion.5
  582.9 8.4 %add_convert_fusion.1 = bf16[2048,1408]{1,0:T(8,128)(2,1)} fusion(bf16[2048,1408]{1,0:T(8,128)(2,1)} %collective-permute-done.23, bf16[2048,2816]{1,0:T(8,128)(2,1)} %convolution_convert_fusion), kind=kLoop, calls=%fused_computation.1 | loop fusion | flops 11534336 | bytes 17301504 | tf_op jit(solution)/shard_map/convert_element_type | solution.py:540
  591.4 5.2 all-to-all-start.6
  596.6 10.8 %collective-permute-done.26 = bf16[128,2048]{1,0:T(8,128)(2,1)} collective-permute-done((bf16[128,2048]{1,0:T(8,128)(2,1)}, bf16[128,2048]{1,0:T(8,128)(2,1)}, u32[]{:S(2)}, u32[]{:S(2)}) %collective-permute-start.26) | collective-permute-done | bytes 524320 | tf_op jit(solution)/shard_map/ppermute | solution.py:29
  610.1 5.5 convolution_convert_fusion.1
  619.0 4.9 fusion.11
  632.2 7.3 add_convert_fusion.2
  641.7 36.4 %all-to-all-done.6 = bf16[4,512,1408]{2,1,0:T(8,128)(2,1)} async-done(((bf16[4,512,1408]{2,1,0:T(8,128)(2,1)}), bf16[4,512,1408]{2,1,0:T(8,128)(2,1)}, u32[]{:S(2)}, u32[]{:S(2)}) %all-to-all-start.6) | async-done | bytes 5767200 | tf_op jit(solution)/shard_map/all_to_all | solution.py:42
  678.1 5.1 all-to-all-start.7
  683.2 6.2 fusion.2
  689.4 6.4 all-to-all-done.7
  695.8 3.7 copy.201
  699.5 4.9 all-to-all-start.8
  704.4 4.7 broadcast_select_fusion.3
  709.1 18.0 %reduce-scatter.7.cloned.1.call-done = bf16[128,2048]{1,0:T(8,128)(2,1)} async-done(((bf16[512,2048]{1,0:T(8,128)(2,1)}), bf16[128,2048]{1,0:T(8,128)(2,1)}) %reduce-scatter.7.cloned.1.call-update) | async-done | bytes 524304 | tf_op jit(solution)/shard_map/reduce_scatter | solution.py:609
  727.1 3.4 add_bitcast_fusion
  742.3 3.7 all-to-all-start.10
  754.2 8.7 %select_convert_fusion = (f32[2,512,1408]{2,1,0:T(8,128)}, f32[2,512,1408]{2,1,0:T(8,128)}) fusion(bf16[2,512,1408]{2,1,0:T(8,128)(2,1)} %collective-permute-done.34, pred[]{:T(512)S(6)} %eq.50, bf16[4,512,1408]{2,1,0:T(8,128)(2,1)} %all-to-all-done.6), kind=kLoop, calls=%fused_computation.33 | loop fusion | flops 7208960 | bytes 20185088 | tf_op jit(solution)/shard_map/convert_element_type | solution.py:629
  765.0 14.3 %all-to-all-done.10 = bf16[4,352,1024]{2,1,0:T(8,128)(2,1)S(1)} async-done(((bf16[4,352,1024]{2,1,0:T(8,128)(2,1)}), bf16[4,352,1024]{2,1,0:T(8,128)(2,1)S(1)}, u32[]{:S(2)}, u32[]{:S(2)}) %all-to-all-start.10) | async-done | bytes 2883616 | tf_op jit(solution)/shard_map/all_to_all | solution.py:42
  779.3 4.3 all-to-all-start.9
  797.0 4.7 all-to-all-done.9
  805.7 3.3 maximum_convert_fusion
  (364 shorter events, 178.4 us)
Async XLA Ops:
  7.2 114.9 %all-gather.6.cloned.1.call-start = ((), (), s32[]{:S(2)}) async-start(), calls=%async_computation.15 | async-start | bytes 10027008 | tf_op jit(solution)/shard_map/all_gather | solution.py:407
  13.8 8.3 %collective-permute-start.8 = (bf16[64,1664]{1,0:T(8,128)(2,1)S(1)}, bf16[64,1664]{1,0:T(8,128)(2,1)S(1)}, u32[]{:S(2)}, u32[]{:S(2)}) collective-permute-start(bf16[64,1664]{1,0:T(8,128)(2,1)S(1)} %bitcast.301), channel_id=1, source_target_pairs={{0,1},{1,0},{2,3},{3,2},{4,5},{5,4},{6,7},{7,6},{8,9},{9,8},{10,11... | collective-permute-start | bytes 638984 | tf_op jit(solution)/shard_map/ppermute | solution.py:29
  16.8 8.2 %collective-permute-start.9 = (bf16[64,1664]{1,0:T(8,128)(2,1)S(1)}, bf16[64,1664]{1,0:T(8,128)(2,1)S(1)}, u32[]{:S(2)}, u32[]{:S(2)}) collective-permute-start(bf16[64,1664]{1,0:T(8,128)(2,1)S(1)} %bitcast.300), channel_id=1, source_target_pairs={{0,2},{1,3},{2,0},{3,1},{4,6},{5,7},{6,4},{7,5},{8,10},{9,11},{10,... | collective-permute-start | bytes 638984 | tf_op jit(solution)/shard_map/ppermute | solution.py:29
  18.4 14.4 %collective-permute-start.10 = (bf16[64,1664]{1,0:T(8,128)(2,1)S(1)}, bf16[64,1664]{1,0:T(8,128)(2,1)S(1)}, u32[]{:S(2)}, u32[]{:S(2)}) collective-permute-start(bf16[64,1664]{1,0:T(8,128)(2,1)S(1)} %bitcast.299), channel_id=1, source_target_pairs={{0,3},{1,2},{2,1},{3,0},{4,7},{5,6},{6,5},{7,4},{8,11},{9,10},{10,... | collective-permute-start | bytes 638984 | tf_op jit(solution)/shard_map/ppermute | solution.py:29
  18.5 14.4 %collective-permute-start.11 = (bf16[64,2048]{1,0:T(8,128)(2,1)S(1)}, bf16[64,2048]{1,0:T(8,128)(2,1)S(1)}, u32[]{:S(2)}, u32[]{:S(2)}) collective-permute-start(bf16[64,2048]{1,0:T(8,128)(2,1)S(1)} %copy-done.59), channel_id=1, source_target_pairs={{0,0},{1,4},{2,8},{3,12},{4,16},{5,20},{6,24},{7,28},{8,1},{9,5},{... | collective-permute-start | bytes 786440 | tf_op jit(solution)/shard_map/ppermute | solution.py:403
  35.9 29.0 %collective-permute-start.1 = (bf16[2,512,1408]{2,1,0:T(8,128)(2,1)}, bf16[2,512,1408]{2,1,0:T(8,128)(2,1)}, u32[]{:S(2)}, u32[]{:S(2)}) collective-permute-start(bf16[2,512,1408]{2,1,0:T(8,128)(2,1)} %broadcast_select_fusion.7), channel_id=1, source_target_pairs={{0,4},{4,0},{1,5},{5,1},{2,6},{6,2},{3,7},{7,3},{8,12},{12,8},{9,1... | collective-permute-start | bytes 8650760 | tf_op jit(solution)/shard_map/ppermute | solution.py:29
  37.0 6.2 collective-permute-start
  45.4 62.7 %all-to-all-start = ((bf16[4,352,1024]{2,1,0:T(8,128)(2,1)}), bf16[4,352,1024]{2,1,0:T(8,128)(2,1)}, u32[]{:S(2)}, u32[]{:S(2)}) async-start(bf16[4,352,1024]{2,1,0:T(8,128)(2,1)} %pad_maximum_fusion.5), calls=%async_computation | async-start | bytes 5767168 | tf_op jit(solution)/shard_map/all_to_all | solution.py:42
  50.2 46.4 %collective-permute-start.2 = (bf16[128,2048]{1,0:T(8,128)(2,1)S(1)}, bf16[128,2048]{1,0:T(8,128)(2,1)}, u32[]{:S(2)}, u32[]{:S(2)}) collective-permute-start(bf16[128,2048]{1,0:T(8,128)(2,1)S(1)} %bitcast.265), channel_id=1, source_target_pairs={{0,1},{1,0},{2,3},{3,2},{4,5},{5,4},{6,7},{7,6},{8,9},{9,8},{10,11... | collective-permute-start | bytes 1572872 | tf_op jit(solution)/shard_map/ppermute | solution.py:29
  53.0 43.8 %collective-permute-start.3 = (bf16[128,2048]{1,0:T(8,128)(2,1)S(1)}, bf16[128,2048]{1,0:T(8,128)(2,1)}, u32[]{:S(2)}, u32[]{:S(2)}) collective-permute-start(bf16[128,2048]{1,0:T(8,128)(2,1)S(1)} %bitcast.266), channel_id=1, source_target_pairs={{0,2},{1,3},{2,0},{3,1},{4,6},{5,7},{6,4},{7,5},{8,10},{9,11},{10,... | collective-permute-start | bytes 1572872 | tf_op jit(solution)/shard_map/ppermute | solution.py:29
  54.1 54.0 %collective-permute-start.4 = (bf16[128,2048]{1,0:T(8,128)(2,1)S(1)}, bf16[128,2048]{1,0:T(8,128)(2,1)}, u32[]{:S(2)}, u32[]{:S(2)}) collective-permute-start(bf16[128,2048]{1,0:T(8,128)(2,1)S(1)} %bitcast.267), channel_id=1, source_target_pairs={{0,3},{1,2},{2,1},{3,0},{4,7},{5,6},{6,5},{7,4},{8,11},{9,10},{10,... | collective-permute-start | bytes 1572872 | tf_op jit(solution)/shard_map/ppermute | solution.py:29
  54.5 16.4 %collective-permute-start.5 = (s32[128,6]{0,1:T(8,128)S(1)}, s32[128,6]{0,1:T(8,128)S(1)}, u32[]{:S(2)}, u32[]{:S(2)}) collective-permute-start(s32[128,6]{0,1:T(8,128)S(1)} %bitcast.307), channel_id=1, source_target_pairs={{0,8},{8,0},{16,24},{24,16},{1,9},{9,1},{17,25},{25,17},{2,10},{10... | collective-permute-start | bytes 9224 | tf_op jit(solution)/shard_map/ppermute | solution.py:29
  64.9 9.8 %collective-permute-start.6 = (s32[128,6]{0,1:T(8,128)S(1)}, s32[128,6]{0,1:T(8,128)S(1)}, u32[]{:S(2)}, u32[]{:S(2)}) collective-permute-start(s32[128,6]{0,1:T(8,128)S(1)} %bitcast.308), channel_id=1, source_target_pairs={{0,16},{8,24},{16,0},{24,8},{1,17},{9,25},{17,1},{25,9},{2,18},{10... | collective-permute-start | bytes 9224 | tf_op jit(solution)/shard_map/ppermute | solution.py:29
  70.9 5.7 collective-permute-start.7
  108.2 70.9 %all-to-all-start.1 = ((bf16[4,512,1408]{2,1,0:T(8,128)(2,1)}), bf16[4,512,1408]{2,1,0:T(8,128)(2,1)}, u32[]{:S(2)}, u32[]{:S(2)}) async-start(bf16[4,512,1408]{2,1,0:T(8,128)(2,1)} %pad_maximum_fusion), calls=%async_computation.1 | async-start | bytes 11534336 | tf_op jit(solution)/shard_map/all_to_all | solution.py:42
  113.4 92.5 %all-gather.10.cloned.1.call-start = ((), (), s32[]{:S(2)}) async-start(), calls=%async_computation.17 | async-start | bytes 2621440 | tf_op jit(solution)/shard_map/all_gather | solution.py:408
  122.1 129.9 %all-gather.8.cloned.1.call-start = ((), (), s32[]{:S(2)}) async-start(), calls=%async_computation.16 | async-start | bytes 2621440 | tf_op jit(solution)/shard_map/all_gather | solution.py:470
  124.9 78.2 %copy-start.47 = (f32[2048]{0:T(1024)}, f32[2048]{0:T(1024)S(1)}, u32[]{:S(2)}) copy-start(f32[2048]{0:T(1024)S(1)} %get-tuple-element.193) | copy-start | bytes 24580
  154.9 34.4 %collective-permute-start.12 = (bf16[128,2048]{1,0:T(8,128)(2,1)}, bf16[128,2048]{1,0:T(8,128)(2,1)}, u32[]{:S(2)}, u32[]{:S(2)}) collective-permute-start(bf16[128,2048]{1,0:T(8,128)(2,1)} %get-tuple-element.224), channel_id=1, source_target_pairs={{0,1},{1,0},{2,3},{3,2},{4,5},{5,4},{6,7},{7,6},{8,9},{9,8},{10,11... | collective-permute-start | bytes 1572872 | tf_op jit(solution)/shard_map/ppermute | solution.py:29
  156.4 33.9 %collective-permute-start.13 = (bf16[128,2048]{1,0:T(8,128)(2,1)}, bf16[128,2048]{1,0:T(8,128)(2,1)}, u32[]{:S(2)}, u32[]{:S(2)}) collective-permute-start(bf16[128,2048]{1,0:T(8,128)(2,1)} %get-tuple-element.226), channel_id=1, source_target_pairs={{0,2},{1,3},{2,0},{3,1},{4,6},{5,7},{6,4},{7,5},{8,10},{9,11},{10,... | collective-permute-start | bytes 1572872 | tf_op jit(solution)/shard_map/ppermute | solution.py:29
  157.9 43.2 %collective-permute-start.14 = (bf16[128,2048]{1,0:T(8,128)(2,1)}, bf16[128,2048]{1,0:T(8,128)(2,1)}, u32[]{:S(2)}, u32[]{:S(2)}) collective-permute-start(bf16[128,2048]{1,0:T(8,128)(2,1)} %get-tuple-element.225), channel_id=1, source_target_pairs={{0,3},{1,2},{2,1},{3,0},{4,7},{5,6},{6,5},{7,4},{8,11},{9,10},{10,... | collective-permute-start | bytes 1572872 | tf_op jit(solution)/shard_map/ppermute | solution.py:29
  205.0 14.6 %collective-permute-start.15 = (bf16[1408,1024]{1,0:T(8,128)(2,1)}, bf16[1408,1024]{1,0:T(8,128)(2,1)}, u32[]{:S(2)}, u32[]{:S(2)}) collective-permute-start(bf16[1408,1024]{1,0:T(8,128)(2,1)} %bitcast.45), channel_id=1, source_target_pairs={{0,4},{4,0},{1,5},{5,1},{2,6},{6,2},{3,7},{7,3},{8,12},{12,8},{9,1... | collective-permute-start | bytes 8650760 | tf_op jit(solution)/shard_map/ppermute | solution.py:29
  212.0 53.9 %all-to-all-start.2 = ((bf16[4,256,2048]{2,1,0:T(8,128)(2,1)}), bf16[4,256,2048]{2,1,0:T(8,128)(2,1)}, u32[]{:S(2)}, u32[]{:S(2)}) async-start(bf16[4,256,2048]{2,1,0:T(8,128)(2,1)} %bitcast.271), calls=%async_computation.2 | async-start | bytes 8388608 | tf_op jit(solution)/shard_map/all_to_all | solution.py:42
  217.5 72.5 %collective-permute-start.16 = (bf16[2048,1408]{1,0:T(8,128)(2,1)}, bf16[2048,1408]{1,0:T(8,128)(2,1)}, u32[]{:S(2)}, u32[]{:S(2)}) collective-permute-start(bf16[2048,1408]{1,0:T(8,128)(2,1)} %bitcast.46.mine), channel_id=1, source_target_pairs={{0,4},{4,0},{1,5},{5,1},{2,6},{6,2},{3,7},{7,3},{8,12},{12,8},{9,1... | collective-permute-start | bytes 17301512 | tf_op jit(solution)/shard_map/ppermute | solution.py:29
  225.3 40.6 %copy-start.42 = (pred[4,4,64,4,128]{4,3,2,1,0:T(4,128)(4,1)S(1)}, pred[4,4,64,4,128]{4,3,2,1,0:T(4,128)(4,1)}, u32[]{:S(2)}) copy-start(pred[4,4,64,4,128]{4,3,2,1,0:T(4,128)(4,1)} %copy-done.41) | copy-start | bytes 1572868
  253.5 23.3 %collective-permute-start.17 = (bf16[64,1408]{1,0:T(8,128)(2,1)S(1)}, bf16[64,1408]{1,0:T(8,128)(2,1)S(1)}, u32[]{:S(2)}, u32[]{:S(2)}) collective-permute-start(bf16[64,1408]{1,0:T(8,128)(2,1)S(1)} %bitcast.304), channel_id=1, source_target_pairs={{0,8},{8,0},{16,24},{24,16},{1,9},{9,1},{17,25},{25,17},{2,10},{10... | collective-permute-start | bytes 540680 | tf_op jit(solution)/shard_map/ppermute | solution.py:29
  253.6 23.3 %collective-permute-start.18 = (bf16[64,1408]{1,0:T(8,128)(2,1)S(1)}, bf16[64,1408]{1,0:T(8,128)(2,1)S(1)}, u32[]{:S(2)}, u32[]{:S(2)}) collective-permute-start(bf16[64,1408]{1,0:T(8,128)(2,1)S(1)} %bitcast.303), channel_id=1, source_target_pairs={{0,16},{8,24},{16,0},{24,8},{1,17},{9,25},{17,1},{25,9},{2,18},{10... | collective-permute-start | bytes 540680 | tf_op jit(solution)/shard_map/ppermute | solution.py:29
  255.4 21.5 %collective-permute-start.19 = (bf16[64,1408]{1,0:T(8,128)(2,1)S(1)}, bf16[64,1408]{1,0:T(8,128)(2,1)S(1)}, u32[]{:S(2)}, u32[]{:S(2)}) collective-permute-start(bf16[64,1408]{1,0:T(8,128)(2,1)S(1)} %bitcast.302), channel_id=1, source_target_pairs={{0,24},{8,16},{16,8},{24,0},{1,25},{9,17},{17,9},{25,1},{2,26},{10... | collective-permute-start | bytes 540680 | tf_op jit(solution)/shard_map/ppermute | solution.py:29
  271.8 52.5 %all-to-all-start.3 = ((bf16[4,256,2048]{2,1,0:T(8,128)(2,1)}), bf16[4,256,2048]{2,1,0:T(8,128)(2,1)}, u32[]{:S(2)}, u32[]{:S(2)}) async-start(bf16[4,256,2048]{2,1,0:T(8,128)(2,1)} %bitcast.272), calls=%async_computation.3 | async-start | bytes 8388608 | tf_op jit(solution)/shard_map/all_to_all | solution.py:42
  276.7 108.5 %all-gather.12.cloned.1.call-start = ((), (), s32[]{:S(2)}) async-start(), calls=%async_computation.22 | async-start | bytes 10948608 | tf_op jit(solution)/shard_map/all_gather | solution.py:517
  278.1 46.3 %copy-start.16 = (bf16[128,2048]{0,1:T(8,128)(2,1)S(1)}, bf16[128,2048]{0,1:T(8,128)(2,1)}, u32[]{:S(2)}) copy-start(bf16[128,2048]{0,1:T(8,128)(2,1)} %copy-done.15) | copy-start | bytes 1572868
  278.1 46.3 %copy-start.20 = (bf16[128,2048]{1,0:T(8,128)(2,1)S(1)}, bf16[128,2048]{1,0:T(8,128)(2,1)}, u32[]{:S(2)}) copy-start(bf16[128,2048]{1,0:T(8,128)(2,1)} %multiply_convert_fusion.7) | copy-start | bytes 1572868
  378.2 55.3 %all-to-all-start.4 = ((bf16[4,256,2176]{2,1,0:T(8,128)(2,1)}), bf16[4,256,2176]{2,1,0:T(8,128)(2,1)}, u32[]{:S(2)}, u32[]{:S(2)}) async-start(bf16[4,256,2176]{2,1,0:T(8,128)(2,1)} %bitcast.236), calls=%async_computation.4 | async-start | bytes 8912896 | tf_op jit(solution)/shard_map/all_to_all | solution.py:42
  403.6 29.9 %copy-start.43 = (pred[4,4,64,4,128]{4,3,2,1,0:T(4,128)(4,1)S(1)}, pred[4,4,64,4,128]{4,3,2,1,0:T(4,128)(4,1)}, u32[]{:S(2)}) copy-start(pred[4,4,64,4,128]{4,3,2,1,0:T(4,128)(4,1)} %copy-done.41) | copy-start | bytes 1572868
  446.3 51.6 %all-to-all-start.5 = ((bf16[4,256,2048]{2,1,0:T(8,128)(2,1)}), bf16[4,256,2048]{2,1,0:T(8,128)(2,1)}, u32[]{:S(2)}, u32[]{:S(2)}) async-start(bf16[4,256,2048]{2,1,0:T(8,128)(2,1)} %bitcast.273), calls=%async_computation.6 | async-start | bytes 8388608 | tf_op jit(solution)/shard_map/all_to_all | solution.py:42
  451.2 51.7 %reduce-scatter.5.cloned.1.call-start = ((), (), s32[]{:S(2)}) async-start(), calls=%async_computation.18 | async-start | bytes 2785280 | tf_op jit(solution)/shard_map/reduce_scatter | solution.py:557
  454.4 176.0 %reduce-scatter.11.cloned.1.call-start = ((), (), s32[]{:S(2)}) async-start(), calls=%async_computation.21 | async-start | bytes 2359296 | tf_op jit(solution)/shard_map/reduce_scatter | solution.py:621
  465.2 39.1 %copy-start.13 = (f32[128,2048]{1,0:T(8,128)S(1)}, f32[128,2048]{1,0:T(8,128)}, u32[]{:S(2)}) copy-start(f32[128,2048]{1,0:T(8,128)} %copy-done.12) | copy-start | bytes 3145732
  465.2 39.1 %copy-start.48 = (f32[2048]{0:T(1024)S(1)}, f32[2048]{0:T(1024)}, u32[]{:S(2)}) copy-start(f32[2048]{0:T(1024)} %copy-done.47) | copy-start | bytes 24580
  465.2 39.1 %copy-start.54 = (f32[128]{0:T(128)S(1)}, f32[128]{0:T(128)}, u32[]{:S(2)}) copy-start(f32[128]{0:T(128)} %copy-done.53) | copy-start | bytes 1540
  510.9 59.9 %collective-permute-start.23 = (bf16[2048,1408]{1,0:T(8,128)(2,1)}, bf16[2048,1408]{1,0:T(8,128)(2,1)}, u32[]{:S(2)}, u32[]{:S(2)}) collective-permute-start(bf16[2048,1408]{1,0:T(8,128)(2,1)} %slice.233), channel_id=1, source_target_pairs={{0,4},{4,0},{1,5},{5,1},{2,6},{6,2},{3,7},{7,3},{8,12},{12,8},{9,1... | collective-permute-start | bytes 17301512 | tf_op jit(solution)/shard_map/ppermute | solution.py:29
  511.3 28.3 %copy-start.2 = (bf16[512,512]{1,0:T(8,128)(2,1)S(1)}, bf16[512,512]{1,0:T(8,128)(2,1)}, u32[]{:S(2)}) copy-start(bf16[512,512]{1,0:T(8,128)(2,1)} %copy-done.1) | copy-start | bytes 1572868
  511.4 14.4 %collective-permute-start.20 = (bf16[128,2048]{1,0:T(8,128)(2,1)S(1)}, bf16[128,2048]{1,0:T(8,128)(2,1)S(1)}, u32[]{:S(2)}, u32[]{:S(2)}) collective-permute-start(bf16[128,2048]{1,0:T(8,128)(2,1)S(1)} %fusion.45), channel_id=1, source_target_pairs={{0,1},{1,0},{2,3},{3,2},{4,5},{5,4},{6,7},{7,6},{8,9},{9,8},{10,11... | collective-permute-start | bytes 1572872 | tf_op jit(solution)/shard_map/ppermute | solution.py:29
  512.9 14.8 %collective-permute-start.21 = (bf16[128,2048]{1,0:T(8,128)(2,1)S(1)}, bf16[128,2048]{1,0:T(8,128)(2,1)S(1)}, u32[]{:S(2)}, u32[]{:S(2)}) collective-permute-start(bf16[128,2048]{1,0:T(8,128)(2,1)S(1)} %fusion.45), channel_id=1, source_target_pairs={{0,2},{1,3},{2,0},{3,1},{4,6},{5,7},{6,4},{7,5},{8,10},{9,11},{10,... | collective-permute-start | bytes 1572872 | tf_op jit(solution)/shard_map/ppermute | solution.py:29
  514.4 23.8 %collective-permute-start.22 = (bf16[128,2048]{1,0:T(8,128)(2,1)S(1)}, bf16[128,2048]{1,0:T(8,128)(2,1)S(1)}, u32[]{:S(2)}, u32[]{:S(2)}) collective-permute-start(bf16[128,2048]{1,0:T(8,128)(2,1)S(1)} %fusion.45), channel_id=1, source_target_pairs={{0,3},{1,2},{2,1},{3,0},{4,7},{5,6},{6,5},{7,4},{8,11},{9,10},{10,... | collective-permute-start | bytes 1572872 | tf_op jit(solution)/shard_map/ppermute | solution.py:29
  552.5 125.6 %reduce-scatter.9.cloned.1.call-start = ((), (), s32[]{:S(2)}) async-start(), calls=%async_computation.20 | async-start | bytes 7667712 | tf_op jit(solution)/shard_map/reduce_scatter | solution.py:624
  575.9 51.3 %collective-permute-start.29 = (bf16[1,352,2048]{2,1,0:T(8,128)(2,1)}, bf16[1,352,2048]{2,1,0:T(8,128)(2,1)}, u32[]{:S(2)}, u32[]{:S(2)}) collective-permute-start(bf16[1,352,2048]{2,1,0:T(8,128)(2,1)} %select_bitcast_fusion.1), channel_id=1, source_target_pairs={{0,4},{4,0},{1,5},{5,1},{2,6},{6,2},{3,7},{7,3},{8,12},{12,8},{9,1... | collective-permute-start | bytes 4325384 | tf_op jit(solution)/shard_map/ppermute | solution.py:29
  577.8 54.4 %collective-permute-start.27 = (bf16[1408,1024]{1,0:T(8,128)(2,1)}, bf16[1408,1024]{1,0:T(8,128)(2,1)}, u32[]{:S(2)}, u32[]{:S(2)}) collective-permute-start(bf16[1408,1024]{1,0:T(8,128)(2,1)} %broadcast_select_fusion), channel_id=1, source_target_pairs={{0,4},{4,0},{1,5},{5,1},{2,6},{6,2},{3,7},{7,3},{8,12},{12,8},{9,1... | collective-permute-start | bytes 8650760 | tf_op jit(solution)/shard_map/ppermute | solution.py:29
  579.4 17.2 %collective-permute-start.24 = (bf16[128,2048]{1,0:T(8,128)(2,1)}, bf16[128,2048]{1,0:T(8,128)(2,1)S(1)}, u32[]{:S(2)}, u32[]{:S(2)}) collective-permute-start(bf16[128,2048]{1,0:T(8,128)(2,1)} %get-tuple-element.221), channel_id=1, source_target_pairs={{0,1},{1,0},{2,3},{3,2},{4,5},{5,4},{6,7},{7,6},{8,9},{9,8},{10,11... | collective-permute-start | bytes 1572872 | tf_op jit(solution)/shard_map/ppermute | solution.py:29
  580.9 15.7 %collective-permute-start.25 = (bf16[128,2048]{1,0:T(8,128)(2,1)}, bf16[128,2048]{1,0:T(8,128)(2,1)}, u32[]{:S(2)}, u32[]{:S(2)}) collective-permute-start(bf16[128,2048]{1,0:T(8,128)(2,1)} %get-tuple-element.223), channel_id=1, source_target_pairs={{0,2},{1,3},{2,0},{3,1},{4,6},{5,7},{6,4},{7,5},{8,10},{9,11},{10,... | collective-permute-start | bytes 1572872 | tf_op jit(solution)/shard_map/ppermute | solution.py:29
  582.4 25.0 %collective-permute-start.26 = (bf16[128,2048]{1,0:T(8,128)(2,1)}, bf16[128,2048]{1,0:T(8,128)(2,1)}, u32[]{:S(2)}, u32[]{:S(2)}) collective-permute-start(bf16[128,2048]{1,0:T(8,128)(2,1)} %get-tuple-element.222), channel_id=1, source_target_pairs={{0,3},{1,2},{2,1},{3,0},{4,7},{5,6},{6,5},{7,4},{8,11},{9,10},{10,... | collective-permute-start | bytes 1572872 | tf_op jit(solution)/shard_map/ppermute | solution.py:29
  591.4 86.7 %all-to-all-start.6 = ((bf16[4,512,1408]{2,1,0:T(8,128)(2,1)}), bf16[4,512,1408]{2,1,0:T(8,128)(2,1)}, u32[]{:S(2)}, u32[]{:S(2)}) async-start(bf16[4,512,1408]{2,1,0:T(8,128)(2,1)} %bitcast.246), calls=%async_computation.9 | async-start | bytes 11534336 | tf_op jit(solution)/shard_map/all_to_all | solution.py:42
  596.5 130.5 %reduce-scatter.7.cloned.1.call-start = ((), (), s32[]{:S(2)}) async-start(), calls=%async_computation.19 | async-start | bytes 2621440 | tf_op jit(solution)/shard_map/reduce_scatter | solution.py:609
  619.0 64.2 %collective-permute-start.28 = (bf16[4,256,1408]{2,1,0:T(8,128)(2,1)}, bf16[4,256,1408]{2,1,0:T(8,128)(2,1)}, u32[]{:S(2)}, u32[]{:S(2)}) collective-permute-start(bf16[4,256,1408]{2,1,0:T(8,128)(2,1)} %select_bitcast_fusion), channel_id=1, source_target_pairs={{0,4},{4,0},{1,5},{5,1},{2,6},{6,2},{3,7},{7,3},{8,12},{12,8},{9,1... | collective-permute-start | bytes 8650760 | tf_op jit(solution)/shard_map/ppermute | solution.py:29
  630.4 9.0 %collective-permute-start.30 = (bf16[64,2048]{1,0:T(8,128)(2,1)}, bf16[64,2048]{1,0:T(8,128)(2,1)S(1)}, u32[]{:S(2)}, u32[]{:S(2)}) collective-permute-start(bf16[64,2048]{1,0:T(8,128)(2,1)} %reduce-scatter.11.cloned.1.call-done), channel_id=1, source_target_pairs={{0,0},{4,1},{8,2},{12,3},{16,4},{20,5},{24,6},{28,7},{1,8},{5,9},{... | collective-permute-start | bytes 786440 | tf_op jit(solution)/shard_map/ppermute | solution.py:623
  678.1 17.8 %all-to-all-start.7 = ((bf16[4,64,1664]{2,1,0:T(8,128)(2,1)}), bf16[4,64,1664]{2,1,0:T(8,128)(2,1)S(1)}, u32[]{:S(2)}, u32[]{:S(2)}) async-start(bf16[4,64,1664]{2,1,0:T(8,128)(2,1)} %bitcast.292), calls=%async_computation.10 | async-start | bytes 1703936 | tf_op jit(solution)/shard_map/all_to_all | solution.py:42
  699.5 42.8 %all-to-all-start.8 = ((bf16[4,4,64,1408]{3,2,1,0:T(8,128)(2,1)}), bf16[4,4,64,1408]{3,2,1,0:T(8,128)(2,1)}, u32[]{:S(2)}, u32[]{:S(2)}) async-start(bf16[4,4,64,1408]{3,2,1,0:T(8,128)(2,1)} %copy.201), calls=%async_computation.12 | async-start | bytes 5767168 | tf_op jit(solution)/shard_map/all_to_all | solution.py:42
  709.1 45.1 %collective-permute-start.34 = (bf16[2,512,1408]{2,1,0:T(8,128)(2,1)}, bf16[2,512,1408]{2,1,0:T(8,128)(2,1)}, u32[]{:S(2)}, u32[]{:S(2)}) collective-permute-start(bf16[2,512,1408]{2,1,0:T(8,128)(2,1)} %broadcast_select_fusion.3), channel_id=1, source_target_pairs={{0,4},{4,0},{1,5},{5,1},{2,6},{6,2},{3,7},{7,3},{8,12},{12,8},{9,1... | collective-permute-start | bytes 8650760 | tf_op jit(solution)/shard_map/ppermute | solution.py:29
  742.3 37.1 %all-to-all-start.10 = ((bf16[4,352,1024]{2,1,0:T(8,128)(2,1)}), bf16[4,352,1024]{2,1,0:T(8,128)(2,1)S(1)}, u32[]{:S(2)}, u32[]{:S(2)}) async-start(bf16[4,352,1024]{2,1,0:T(8,128)(2,1)} %bitcast.252), calls=%async_computation.14 | async-start | bytes 5767168 | tf_op jit(solution)/shard_map/all_to_all | solution.py:42
  748.1 14.8 %collective-permute-start.31 = (bf16[64,1408]{1,0:T(8,128)(2,1)S(1)}, bf16[64,1408]{1,0:T(8,128)(2,1)S(1)}, u32[]{:S(2)}, u32[]{:S(2)}) collective-permute-start(bf16[64,1408]{1,0:T(8,128)(2,1)S(1)} %get-tuple-element.237), channel_id=1, source_target_pairs={{0,8},{8,0},{16,24},{24,16},{1,9},{9,1},{17,25},{25,17},{2,10},{10... | collective-permute-start | bytes 540680 | tf_op jit(solution)/shard_map/ppermute | solution.py:29
  748.2 16.1 %collective-permute-start.32 = (bf16[64,1408]{1,0:T(8,128)(2,1)S(1)}, bf16[64,1408]{1,0:T(8,128)(2,1)S(1)}, u32[]{:S(2)}, u32[]{:S(2)}) collective-permute-start(bf16[64,1408]{1,0:T(8,128)(2,1)S(1)} %get-tuple-element.236), channel_id=1, source_target_pairs={{0,16},{8,24},{16,0},{24,8},{1,17},{9,25},{17,1},{25,9},{2,18},{10... | collective-permute-start | bytes 540680 | tf_op jit(solution)/shard_map/ppermute | solution.py:29
  750.4 34.5 %collective-permute-start.33 = (bf16[64,1408]{1,0:T(8,128)(2,1)S(1)}, bf16[64,1408]{1,0:T(8,128)(2,1)S(1)}, u32[]{:S(2)}, u32[]{:S(2)}) collective-permute-start(bf16[64,1408]{1,0:T(8,128)(2,1)S(1)} %get-tuple-element.235), channel_id=1, source_target_pairs={{0,24},{8,16},{16,8},{24,0},{1,25},{9,17},{17,9},{25,1},{2,26},{10... | collective-permute-start | bytes 540680 | tf_op jit(solution)/shard_map/ppermute | solution.py:29
  779.3 22.4 %all-to-all-start.9 = ((bf16[4,1,88,2048]{3,2,1,0:T(8,128)(2,1)}), bf16[4,1,88,2048]{3,2,1,0:T(8,128)(2,1)}, u32[]{:S(2)}, u32[]{:S(2)}) async-start(bf16[4,1,88,2048]{3,2,1,0:T(8,128)(2,1)} %bitcast.262), calls=%async_computation.13 | async-start | bytes 2883584 | tf_op jit(solution)/shard_map/all_to_all | solution.py:42
  784.9 19.2 %collective-permute-start.35 = (bf16[2,352,1024]{2,1,0:T(8,128)(2,1)}, bf16[2,352,1024]{2,1,0:T(8,128)(2,1)}, u32[]{:S(2)}, u32[]{:S(2)}) collective-permute-start(bf16[2,352,1024]{2,1,0:T(8,128)(2,1)} %broadcast_select_fusion.11), channel_id=1, source_target_pairs={{0,4},{4,0},{1,5},{5,1},{2,6},{6,2},{3,7},{7,3},{8,12},{12,8},{9,1... | collective-permute-start | bytes 4325384 | tf_op jit(solution)/shard_map/ppermute | solution.py:29
  (56 other events, 406.6 us)
Sparse Core Ops, SparseCore 0:
  34.1 87.9 all-gather.5
  123.7 44.3 all-gather.9
  206.0 45.9 all-gather.7
  324.4 60.7 all-gather.11
  454.7 48.2 reduce-scatter.4
  552.6 35.6 reduce-scatter.10
  590.6 86.2 reduce-scatter.8
  679.2 47.7 reduce-scatter.6
